TPU v7x, 1024 devices: a whole 4x4x32 slice. The times are simulated.
1024 devices in a mesh: replica: 16 (over z_lo, core), shard: 64 (over x, z_hi, y).
Axes of the slice: x: 4, y: 4, z: 32 (z_hi: 4, z_lo: 8; z = z_hi * 8 + z_lo), core: 2. Of those that a mesh axis runs over, the one named last changes fastest.
Arguments:
- emb_table: float32 [262144, 128], P('shard'), may hold values from -2 to 2
- active_blocks: int32 [16, 64, 16], P(None, 'shard'), may hold values from 0 to 255, as said below
- hit_shards: int32 [16, 4, 16384, 2], P('replica', None, 'shard'), may hold values from 0 to 63, all different within a row; in each aligned block of 256 rows (0 to 255, 256 to 511, ..., all dimensions but the last counted through in order) at most 12 rows name the same one
- lookup_slot: int32 [16, 4, 16384, 2, 4], P('replica', None, 'shard'), may hold values from 0 to 15
- lookup_offset: int32 [16, 4, 16384, 2, 4], P('replica', None, 'shard'), may hold values from 0 to 15
- block_weight: float32 [16, 4, 64, 16], P('replica', None, 'shard'), may hold values from 0.25 to 2
- dense_feat: bfloat16 [16, 4, 16384, 128], P('replica', None, 'shard'), may hold values from -6 to 6
- labels: int32 [16, 4, 16384], P('replica', None, 'shard'), may hold values from 0 to 1
Outputs:
- new_table: float32 [262144, 128], P('shard')
- step_logits: float32 [16, 4, 16384], P('replica', None, 'shard')
Inputs may be any that keep to these rules, and one draw needn't show every extreme that they name: `hit_shards`: in each aligned block of 256 rows (the samples of one device in one step) no shard is named by more than 12 hits, and a sample's 2 shards differ. `active_blocks`: the 16 blocks of one group and shard differ and stand in ascending order.
All inputs are finite; a program needn't handle non-finite values.
Results may differ from a plain program's by a relative error of at most 0.0016.
Values may be sent and summed in bfloat16 or wider, within the bound.
No kernel may reach another device: no remote copies, remote signals or barrier semaphores. Data moves between devices by JAX's collectives and lax.ppermute only.
A program may use at most 32 MiB of HBM per device.

v0:
```python
import jax
import jax.numpy as jnp
from jax import lax
from jax.sharding import PartitionSpec as P

BLK = 16


step_rate = 1.0


def body(
    emb_table,
    active_blocks,
    hit_shards,
    lookup_slot,
    lookup_offset,
    block_weight,
    dense_feat,
    labels,
):
    shards = lax.axis_size("shard")
    groups = lax.axis_size("replica")
    num_steps = hit_shards.shape[1]
    samples = hit_shards.shape[2]
    fanout = hit_shards.shape[3]
    per_hit = lookup_slot.shape[4]
    emb_width = emb_table.shape[1]
    active = active_blocks.shape[2]
    act_rows = active * BLK
    capacity = max(2, 3 * samples * fanout // (2 * shards))
    inv_root = emb_width ** (-0.5)
    within = jnp.arange(BLK, dtype=jnp.int32)
    my_blocks = active_blocks[lax.axis_index("replica"), 0]
    local_index = (my_blocks[:, None] * BLK + within[None, :]).reshape(-1)
    initial = emb_table[local_index]
    targets = hit_shards[0].reshape(num_steps, samples * fanout)
    onehot = (targets[:, :, None] == jnp.arange(shards, dtype=jnp.int32)).astype(jnp.int32)
    ranking = jnp.sum((jnp.cumsum(onehot, axis=1) - onehot) * onehot, axis=2)
    slot_of = targets * capacity + ranking
    combined = (lookup_slot[0] * BLK + lookup_offset[0]).reshape(
        num_steps, samples * fanout, per_hit
    )
    step_grid = jnp.broadcast_to(jnp.arange(num_steps, dtype=jnp.int32)[:, None], targets.shape)
    outgoing = (
        jnp.full((num_steps, shards * capacity, per_hit), -1, jnp.int32)
        .at[step_grid, slot_of]
        .set(combined)
    )
    outgoing = outgoing.reshape(num_steps, shards, capacity, per_hit)
    columns = jnp.arange(act_rows, dtype=jnp.int32)
    current = initial
    logit_list = []
    for step_no in range(num_steps):
        received = lax.all_to_all(
            outgoing[step_no], "shard", split_axis=0, concat_axis=0, tiled=True
        )
        received = received.reshape(shards * capacity, per_hit)
        counts = jnp.sum((received[:, :, None] == columns).astype(jnp.float32), axis=1)
        weight_rows = jnp.repeat(block_weight[0, step_no, 0], BLK)
        lookup_matrix = counts * weight_rows[None, :]
        partial_value = jnp.dot(
            lookup_matrix,
            current,
            precision=lax.Precision.HIGHEST,
            preferred_element_type=jnp.float32,
        )
        features = dense_feat[0, step_no].astype(jnp.float32)
        returned = lax.all_to_all(
            partial_value.reshape(shards, capacity, emb_width),
            "shard",
            split_axis=0,
            concat_axis=0,
            tiled=True,
        )
        picked = returned.reshape(shards * capacity, emb_width)[slot_of[step_no]]
        pooled = jnp.sum(picked.reshape(samples, fanout, emb_width), axis=1)
        logits = jnp.sum(pooled * features, axis=1) * inv_root
        loss_grad = (
            (jax.nn.sigmoid(logits) - labels[0, step_no].astype(jnp.float32))[:, None]
            * features
            * inv_root
        ).astype(jnp.bfloat16)
        spread = (
            jnp.zeros((shards * capacity, emb_width), jnp.bfloat16)
            .at[slot_of[step_no]]
            .set(jnp.repeat(loss_grad, fanout, axis=0))
        )
        arrived_grads = lax.all_to_all(
            spread.reshape(shards, capacity, emb_width),
            "shard",
            split_axis=0,
            concat_axis=0,
            tiled=True,
        )
        slot_grad = arrived_grads.reshape(shards * capacity, emb_width)
        row_grad = lax.dot_general(
            lookup_matrix,
            slot_grad.astype(jnp.float32),
            (((0,), (0,)), ((), ())),
            precision=lax.Precision.HIGHEST,
            preferred_element_type=jnp.float32,
        )
        current = current - step_rate * row_grad
        logit_list.append(logits)
    row_delta = current - initial
    scattered = jnp.zeros(emb_table.shape, jnp.float32).at[local_index].set(row_delta)
    summed = lax.psum(scattered.astype(jnp.bfloat16), "replica").astype(jnp.float32)
    new_table = emb_table + summed / groups
    return (new_table, jnp.stack(logit_list)[None])


def solution(mesh):
    placed = (
        P("shard", None),
        P(None, "shard", None),
        P("replica", None, "shard", None),
        P("replica", None, "shard", None, None),
        P("replica", None, "shard", None, None),
        P("replica", None, "shard", None),
        P("replica", None, "shard", None),
        P("replica", None, "shard"),
    )
    return jax.shard_map(
        body,
        mesh=mesh,
        in_specs=placed,
        out_specs=(P("shard", None), P("replica", None, "shard")),
        check_vma=False,
    )
```

profile of v0, /device:TPU:1, one launch (start us, length us, event | category | flops | bytes accessed | tf_op | source)
XLA Modules:
  0.0 800.4 jit_solution(8378476218079731237)
XLA Ops:
  7.2 0.9 copy.98
  8.0 0.7 broadcast_multiply_fusion
  8.9 4.8 reduce-window.6
  16.5 6.0 scatter_custom_fusion.5
  22.9 0.7 copy.110
  23.7 35.0 %all-to-all-start = ((s32[64,12,4]{1,2,0:T(4,128)}), s32[64,12,4]{1,2,0:T(4,128)S(1)}, u32[]{:S(2)}, u32[]{:S(2)}) async-start(s32[64,12,4]{1,2,0:T(4,128)} %copy.110), calls=%async_computation | async-start | bytes 262144 | tf_op jit(solution)/shard_map/all_to_all | solution.py:55
  58.7 0.7 multiply_bitcast_fusion
  59.7 2.3 gather_fusion
  62.0 23.7 %all-to-all-done = s32[64,12,4]{1,2,0:T(4,128)S(1)} async-done(((s32[64,12,4]{1,2,0:T(4,128)}), s32[64,12,4]{1,2,0:T(4,128)S(1)}, u32[]{:S(2)}, u32[]{:S(2)}) %all-to-all-start) | async-done | bytes 12320 | tf_op jit(solution)/shard_map/all_to_all | solution.py:55
  85.9 0.6 convert_reduce_fusion.3
  86.5 0.8 fusion.15
  87.3 0.8 reshape.403
  88.1 6.5 all-to-all-start.1
  94.9 0.7 copy.114
  95.7 34.3 %all-to-all-done.1 = f32[64,12,128]{2,1,0:T(8,128)S(1)} async-done(((f32[64,12,128]{2,1,0:T(8,128)}), f32[64,12,128]{2,1,0:T(8,128)S(1)}, u32[]{:S(2)}, u32[]{:S(2)}) %all-to-all-start.1) | async-done | bytes 393248 | tf_op jit(solution)/shard_map/all_to_all | solution.py:69
  130.0 6.5 all-to-all-start.3
  136.5 1.0 gather_fusion.1
  138.2 1.8 scatter_custom_fusion
  140.0 0.7 reshape.407
  140.7 23.2 %all-to-all-done.3 = s32[64,12,4]{1,2,0:T(4,128)S(1)} async-done(((s32[64,12,4]{1,2,0:T(4,128)}), s32[64,12,4]{1,2,0:T(4,128)S(1)}, u32[]{:S(2)}, u32[]{:S(2)}) %all-to-all-start.3) | async-done | bytes 12320 | tf_op jit(solution)/shard_map/all_to_all | solution.py:55
  164.0 13.5 %all-to-all-start.2 = ((bf16[64,12,128]{2,1,0:T(8,128)(2,1)}), bf16[64,12,128]{2,1,0:T(8,128)(2,1)S(1)}, u32[]{:S(2)}, u32[]{:S(2)}) async-start(bf16[64,12,128]{2,1,0:T(8,128)(2,1)} %reshape.407), calls=%async_computation.2 | async-start | bytes 524288 | tf_op jit(solution)/shard_map/all_to_all | solution.py:89
  177.8 0.6 convert_reduce_fusion.2
  178.4 25.8 %all-to-all-done.2 = bf16[64,12,128]{2,1,0:T(8,128)(2,1)S(1)} async-done(((bf16[64,12,128]{2,1,0:T(8,128)(2,1)}), bf16[64,12,128]{2,1,0:T(8,128)(2,1)S(1)}, u32[]{:S(2)}, u32[]{:S(2)}) %all-to-all-start.2) | async-done | bytes 196640 | tf_op jit(solution)/shard_map/all_to_all | solution.py:89
  204.3 0.8 convolution_subtract_fusion.3
  205.1 0.8 fusion.12
  205.9 0.8 reshape.409
  206.7 7.0 all-to-all-start.4
  214.1 0.7 copy.117
  214.8 28.8 %all-to-all-done.4 = f32[64,12,128]{2,1,0:T(8,128)S(1)} async-done(((f32[64,12,128]{2,1,0:T(8,128)}), f32[64,12,128]{2,1,0:T(8,128)S(1)}, u32[]{:S(2)}, u32[]{:S(2)}) %all-to-all-start.4) | async-done | bytes 393248 | tf_op jit(solution)/shard_map/all_to_all | solution.py:69
  243.6 8.7 %all-to-all-start.6 = ((s32[64,12,4]{1,2,0:T(4,128)}), s32[64,12,4]{1,2,0:T(4,128)S(1)}, u32[]{:S(2)}, u32[]{:S(2)}) async-start(s32[64,12,4]{1,2,0:T(4,128)} %copy.117), calls=%async_computation.6 | async-start | bytes 262144 | tf_op jit(solution)/shard_map/all_to_all | solution.py:55
  252.3 1.0 gather_fusion.2
  254.0 1.8 scatter_custom_fusion.1
  255.8 0.7 reshape.413
  256.6 31.6 %all-to-all-done.6 = s32[64,12,4]{1,2,0:T(4,128)S(1)} async-done(((s32[64,12,4]{1,2,0:T(4,128)}), s32[64,12,4]{1,2,0:T(4,128)S(1)}, u32[]{:S(2)}, u32[]{:S(2)}) %all-to-all-start.6) | async-done | bytes 12320 | tf_op jit(solution)/shard_map/all_to_all | solution.py:55
  288.2 15.3 %all-to-all-start.5 = ((bf16[64,12,128]{2,1,0:T(8,128)(2,1)}), bf16[64,12,128]{2,1,0:T(8,128)(2,1)S(1)}, u32[]{:S(2)}, u32[]{:S(2)}) async-start(bf16[64,12,128]{2,1,0:T(8,128)(2,1)} %reshape.413), calls=%async_computation.5 | async-start | bytes 524288 | tf_op jit(solution)/shard_map/all_to_all | solution.py:89
  303.8 0.6 convert_reduce_fusion.1
  304.4 26.0 %all-to-all-done.5 = bf16[64,12,128]{2,1,0:T(8,128)(2,1)S(1)} async-done(((bf16[64,12,128]{2,1,0:T(8,128)(2,1)}), bf16[64,12,128]{2,1,0:T(8,128)(2,1)S(1)}, u32[]{:S(2)}, u32[]{:S(2)}) %all-to-all-start.5) | async-done | bytes 196640 | tf_op jit(solution)/shard_map/all_to_all | solution.py:89
  330.5 0.8 convolution_subtract_fusion.2
  331.3 0.8 fusion.9
  332.1 0.8 reshape.415
  332.9 12.8 %all-to-all-start.7 = ((f32[64,12,128]{2,1,0:T(8,128)}), f32[64,12,128]{2,1,0:T(8,128)S(1)}, u32[]{:S(2)}, u32[]{:S(2)}) async-start(f32[64,12,128]{2,1,0:T(8,128)} %reshape.415), calls=%async_computation.7 | async-start | bytes 1048576 | tf_op jit(solution)/shard_map/all_to_all | solution.py:69
  346.0 0.7 copy.120
  346.8 31.5 %all-to-all-done.7 = f32[64,12,128]{2,1,0:T(8,128)S(1)} async-done(((f32[64,12,128]{2,1,0:T(8,128)}), f32[64,12,128]{2,1,0:T(8,128)S(1)}, u32[]{:S(2)}, u32[]{:S(2)}) %all-to-all-start.7) | async-done | bytes 393248 | tf_op jit(solution)/shard_map/all_to_all | solution.py:69
  378.2 13.1 %all-to-all-start.9 = ((s32[64,12,4]{1,2,0:T(4,128)}), s32[64,12,4]{1,2,0:T(4,128)S(1)}, u32[]{:S(2)}, u32[]{:S(2)}) async-start(s32[64,12,4]{1,2,0:T(4,128)} %copy.120), calls=%async_computation.9 | async-start | bytes 262144 | tf_op jit(solution)/shard_map/all_to_all | solution.py:55
  391.4 1.0 gather_fusion.3
  393.1 1.8 scatter_custom_fusion.2
  394.9 0.7 reshape.419
  395.6 21.2 %all-to-all-done.9 = s32[64,12,4]{1,2,0:T(4,128)S(1)} async-done(((s32[64,12,4]{1,2,0:T(4,128)}), s32[64,12,4]{1,2,0:T(4,128)S(1)}, u32[]{:S(2)}, u32[]{:S(2)}) %all-to-all-start.9) | async-done | bytes 12320 | tf_op jit(solution)/shard_map/all_to_all | solution.py:55
  416.9 10.3 %all-to-all-start.8 = ((bf16[64,12,128]{2,1,0:T(8,128)(2,1)}), bf16[64,12,128]{2,1,0:T(8,128)(2,1)S(1)}, u32[]{:S(2)}, u32[]{:S(2)}) async-start(bf16[64,12,128]{2,1,0:T(8,128)(2,1)} %reshape.419), calls=%async_computation.8 | async-start | bytes 524288 | tf_op jit(solution)/shard_map/all_to_all | solution.py:89
  427.5 0.6 convert_reduce_fusion
  428.1 26.5 %all-to-all-done.8 = bf16[64,12,128]{2,1,0:T(8,128)(2,1)S(1)} async-done(((bf16[64,12,128]{2,1,0:T(8,128)(2,1)}), bf16[64,12,128]{2,1,0:T(8,128)(2,1)S(1)}, u32[]{:S(2)}, u32[]{:S(2)}) %all-to-all-start.8) | async-done | bytes 196640 | tf_op jit(solution)/shard_map/all_to_all | solution.py:89
  454.7 0.8 convolution_subtract_fusion.1
  455.5 0.8 fusion.6
  456.3 0.8 reshape.421
  457.1 5.2 all-to-all-start.10
  462.4 30.8 %all-to-all-done.10 = f32[64,12,128]{2,1,0:T(8,128)S(1)} async-done(((f32[64,12,128]{2,1,0:T(8,128)}), f32[64,12,128]{2,1,0:T(8,128)S(1)}, u32[]{:S(2)}, u32[]{:S(2)}) %all-to-all-start.10) | async-done | bytes 393248 | tf_op jit(solution)/shard_map/all_to_all | solution.py:69
  493.2 1.0 gather_fusion.4
  494.9 1.8 scatter_custom_fusion.3
  496.8 36.7 %all_to_all.60 = bf16[64,12,128]{2,1,0:T(8,128)(2,1)S(1)} all-to-all(bf16[64,12,128]{2,1,0:T(8,128)(2,1)S(1)} %reshape.425), channel_id=1, replica_groups=mesh['replica'=16,'shard'=64] {'shard'}, dimensions={0} | all-to-all | bytes 393216 | tf_op jit(solution)/shard_map/all_to_all | solution.py:89
  533.6 0.8 fusion
  534.4 1.7 scatter_custom_fusion.4
  536.0 1.1 convert_element_type.131
  537.7 252.4 %all-reduce.2.cloned.1.call-done = bf16[4096,128]{1,0:T(8,128)(2,1)} async-done(((bf16[4096,128]{1,0:T(8,128)(2,1)}), bf16[4096,128]{1,0:T(8,128)(2,1)}) %all-reduce.2.cloned.1.call-update) | async-done | bytes 1048592 | tf_op jit(solution)/shard_map/psum | solution.py:108
  790.1 3.4 multiply_add_fusion
  (104 shorter events, 9.1 us)
Async XLA Ops:
  8.9 6.3 copy-start.6
  8.9 6.5 copy-start.5
  13.7 2.1 copy-start.1
  13.7 2.1 copy-start.2
  22.5 37.0 %copy-start.4 = (f32[1,4,1,16]{3,2,1,0:T(1,128)S(1)}, f32[1,4,1,16]{3,2,1,0:T(1,128)}, u32[]{:S(2)}) copy-start(f32[1,4,1,16]{3,2,1,0:T(1,128)} %param.13) | copy-start | bytes 772
  23.7 62.1 %all-to-all-start = ((s32[64,12,4]{1,2,0:T(4,128)}), s32[64,12,4]{1,2,0:T(4,128)S(1)}, u32[]{:S(2)}, u32[]{:S(2)}) async-start(s32[64,12,4]{1,2,0:T(4,128)} %copy.110), calls=%async_computation | async-start | bytes 262144 | tf_op jit(solution)/shard_map/all_to_all | solution.py:55
  86.5 9.2 %copy-start.3 = (s32[1,4,256]{2,1,0:T(4,128)S(1)}, s32[1,4,256]{2,1,0:T(4,128)}, u32[]{:S(2)}) copy-start(s32[1,4,256]{2,1,0:T(4,128)} %param.15) | copy-start | bytes 12292
  88.1 41.8 %all-to-all-start.1 = ((f32[64,12,128]{2,1,0:T(8,128)}), f32[64,12,128]{2,1,0:T(8,128)S(1)}, u32[]{:S(2)}, u32[]{:S(2)}) async-start(f32[64,12,128]{2,1,0:T(8,128)} %reshape.403), calls=%async_computation.1 | async-start | bytes 1048576 | tf_op jit(solution)/shard_map/all_to_all | solution.py:69
  94.9 42.9 %copy-start = (bf16[1,4,256,128]{3,2,1,0:T(8,128)(2,1)S(1)}, bf16[1,4,256,128]{3,2,1,0:T(8,128)(2,1)}, u32[]{:S(2)}) copy-start(bf16[1,4,256,128]{3,2,1,0:T(8,128)(2,1)} %param.14) | copy-start | bytes 786436
  130.0 34.0 %all-to-all-start.3 = ((s32[64,12,4]{1,2,0:T(4,128)}), s32[64,12,4]{1,2,0:T(4,128)S(1)}, u32[]{:S(2)}, u32[]{:S(2)}) async-start(s32[64,12,4]{1,2,0:T(4,128)} %copy.114), calls=%async_computation.3 | async-start | bytes 262144 | tf_op jit(solution)/shard_map/all_to_all | solution.py:55
  164.0 40.2 %all-to-all-start.2 = ((bf16[64,12,128]{2,1,0:T(8,128)(2,1)}), bf16[64,12,128]{2,1,0:T(8,128)(2,1)S(1)}, u32[]{:S(2)}, u32[]{:S(2)}) async-start(bf16[64,12,128]{2,1,0:T(8,128)(2,1)} %reshape.407), calls=%async_computation.2 | async-start | bytes 524288 | tf_op jit(solution)/shard_map/all_to_all | solution.py:89
  206.7 36.9 %all-to-all-start.4 = ((f32[64,12,128]{2,1,0:T(8,128)}), f32[64,12,128]{2,1,0:T(8,128)S(1)}, u32[]{:S(2)}, u32[]{:S(2)}) async-start(f32[64,12,128]{2,1,0:T(8,128)} %reshape.409), calls=%async_computation.4 | async-start | bytes 1048576 | tf_op jit(solution)/shard_map/all_to_all | solution.py:69
  243.6 44.6 %all-to-all-start.6 = ((s32[64,12,4]{1,2,0:T(4,128)}), s32[64,12,4]{1,2,0:T(4,128)S(1)}, u32[]{:S(2)}, u32[]{:S(2)}) async-start(s32[64,12,4]{1,2,0:T(4,128)} %copy.117), calls=%async_computation.6 | async-start | bytes 262144 | tf_op jit(solution)/shard_map/all_to_all | solution.py:55
  288.2 42.2 %all-to-all-start.5 = ((bf16[64,12,128]{2,1,0:T(8,128)(2,1)}), bf16[64,12,128]{2,1,0:T(8,128)(2,1)S(1)}, u32[]{:S(2)}, u32[]{:S(2)}) async-start(bf16[64,12,128]{2,1,0:T(8,128)(2,1)} %reshape.413), calls=%async_computation.5 | async-start | bytes 524288 | tf_op jit(solution)/shard_map/all_to_all | solution.py:89
  332.9 45.3 %all-to-all-start.7 = ((f32[64,12,128]{2,1,0:T(8,128)}), f32[64,12,128]{2,1,0:T(8,128)S(1)}, u32[]{:S(2)}, u32[]{:S(2)}) async-start(f32[64,12,128]{2,1,0:T(8,128)} %reshape.415), calls=%async_computation.7 | async-start | bytes 1048576 | tf_op jit(solution)/shard_map/all_to_all | solution.py:69
  378.2 38.6 %all-to-all-start.9 = ((s32[64,12,4]{1,2,0:T(4,128)}), s32[64,12,4]{1,2,0:T(4,128)S(1)}, u32[]{:S(2)}, u32[]{:S(2)}) async-start(s32[64,12,4]{1,2,0:T(4,128)} %copy.120), calls=%async_computation.9 | async-start | bytes 262144 | tf_op jit(solution)/shard_map/all_to_all | solution.py:55
  416.9 37.8 %all-to-all-start.8 = ((bf16[64,12,128]{2,1,0:T(8,128)(2,1)}), bf16[64,12,128]{2,1,0:T(8,128)(2,1)S(1)}, u32[]{:S(2)}, u32[]{:S(2)}) async-start(bf16[64,12,128]{2,1,0:T(8,128)(2,1)} %reshape.419), calls=%async_computation.8 | async-start | bytes 524288 | tf_op jit(solution)/shard_map/all_to_all | solution.py:89
  457.1 36.1 %all-to-all-start.10 = ((f32[64,12,128]{2,1,0:T(8,128)}), f32[64,12,128]{2,1,0:T(8,128)S(1)}, u32[]{:S(2)}, u32[]{:S(2)}) async-start(f32[64,12,128]{2,1,0:T(8,128)} %reshape.421), calls=%async_computation.10 | async-start | bytes 1048576 | tf_op jit(solution)/shard_map/all_to_all | solution.py:69
  462.3 327.8 %all-reduce.2.cloned.1.call-start = ((), (), s32[]{:S(2)}) async-start(), calls=%async_computation.12 | async-start | bytes 2097152 | tf_op jit(solution)/shard_map/psum | solution.py:108
Sparse Core Ops, SparseCore 0:
  537.3 252.8 all-reduce.1
where the time goes:
time: 801 us; the launch traced here: 800 us
  waiting for transfers between devices  556 us (69%)
  starting transfers between devices  134 us (17%)
  blocking collectives  36.7 us (5%)
  local copies, waits for them, and re-layouts  36.2 us (5%)
  other arithmetic  16.6 us (2%)
  between operations  14.7 us (2%)
    psum x1, waiting for transfers between devices, body(): lax.psum(scattered.astype(jnp.bfloat16), 'replica').astype(jnp.float32)  252 us
    all_to_all x4, waiting for transfers between devices, body(): lax.all_to_all(partial_value.reshape(shards, capacity, emb_width), 'shard...  125 us
    all_to_all x4, waiting for transfers between devices, body(): lax.all_to_all(outgoing[step_no], 'shard', split_axis=0, concat_axis=0, t...  99.9 us
    all_to_all x3, waiting for transfers between devices, body(): lax.all_to_all(spread.reshape(shards, capacity, emb_width), 'shard', spli...  78.4 us
    all_to_all x4, starting transfers between devices, body(): lax.all_to_all(outgoing[step_no], 'shard', split_axis=0, concat_axis=0, t...  63.2 us
    all_to_all x3, starting transfers between devices, body(): lax.all_to_all(spread.reshape(shards, capacity, emb_width), 'shard', spli...  39.1 us
    all_to_all x1, blocking collectives, body(): lax.all_to_all(spread.reshape(shards, capacity, emb_width), 'shard', spli...  36.7 us
    all_to_all x4, starting transfers between devices, body(): lax.all_to_all(partial_value.reshape(shards, capacity, emb_width), 'shard...  31.5 us
  transfers between devices with their start and end apart: 12, of which 12 were waited for; matrix products, arithmetic and copies ran while one was open for 3% of the time, Pallas kernels for 0%

commit v1 on v0

v1 whole, which is shorter than its diff:
```python
import functools

import jax
import jax.numpy as jnp
from jax import lax
from jax.experimental import pallas as pl
from jax.experimental.pallas import tpu as pltpu
from jax.sharding import Mesh
from jax.sharding import PartitionSpec as P

BLK = 16
STRIDE = 16
META = 12
step_rate = 1.0

GROUP = ("x", "b", "c", "y")
HOME = ("a", "b", "c", "h")


def split3(v):
    hi = v.astype(jnp.bfloat16)
    rest = v - hi.astype(jnp.float32)
    mid = rest.astype(jnp.bfloat16)
    return hi, mid, (rest - mid.astype(jnp.float32)).astype(jnp.bfloat16)


def dot(lhs, rhs, contract=((1,), (0,))):
    return lax.dot_general(lhs, rhs, (contract, ((), ())), preferred_element_type=jnp.float32)


def iota(shape, axis):
    return lax.broadcasted_iota(jnp.int32, shape, axis)


def pack_kernel(shards, meta_ref, feat_ref, out_ref, slot_ref):
    meta = meta_ref[0].astype(jnp.float32)
    samples = meta.shape[1]
    hits = 2 * samples

    def pair(first, second):
        return jnp.concatenate([meta[first : first + 1], meta[second : second + 1]], axis=1)

    target = pair(0, 1).astype(jnp.int32)
    chosen = iota((shards, hits), 0) == target
    onehot = chosen.astype(jnp.float32).astype(jnp.bfloat16)
    before = (iota((hits, hits), 0) < iota((hits, hits), 1)).astype(jnp.float32).astype(jnp.bfloat16)
    rank = jnp.sum(jnp.where(chosen, dot(onehot, before), 0.0), axis=0, keepdims=True)
    rank_i = rank.astype(jnp.int32)
    slot = target * STRIDE + rank_i
    place = (iota((shards * STRIDE, hits), 0) == slot).astype(jnp.float32).astype(jnp.bfloat16)
    feats = feat_ref[0]
    packed = dot(place, jnp.concatenate([feats, feats], axis=0))
    other = jnp.concatenate([rank[:, samples:], rank[:, :samples]], axis=1)
    values = [pair(2 + n, 6 + n) for n in range(4)] + [pair(1, 0), other, pair(10, 10), jnp.ones_like(rank)]
    lane_of = iota((STRIDE, hits), 0) == rank_i
    spread = jnp.concatenate([jnp.where(lane_of, value, 0.0) for value in values], axis=0)
    rows = dot(onehot, spread.astype(jnp.bfloat16), ((1,), (1,)))
    at_row = iota((shards * STRIDE, shards), 0) == iota((shards * STRIDE, shards), 1) * STRIDE + META
    packed = packed + dot(at_row.astype(jnp.float32).astype(jnp.bfloat16), rows.astype(jnp.bfloat16))
    out_ref[...] = packed.astype(jnp.bfloat16).reshape(out_ref.shape)
    slot_ref[0] = slot


def pack(meta, feats, shards):
    steps, samples, width = feats.shape
    return pl.pallas_call(
        functools.partial(pack_kernel, shards),
        grid=(steps,),
        in_specs=[
            pl.BlockSpec((1, 16, samples), lambda t: (t, 0, 0)),
            pl.BlockSpec((1, samples, width), lambda t: (t, 0, 0)),
        ],
        out_specs=[
            pl.BlockSpec((shards, 1, STRIDE, width), lambda t: (0, t, 0, 0)),
            pl.BlockSpec((1, 1, 2 * samples), lambda t: (t, 0, 0)),
        ],
        out_shape=[
            jax.ShapeDtypeStruct((shards, steps, STRIDE, width), jnp.bfloat16),
            jax.ShapeDtypeStruct((steps, 1, 2 * samples), jnp.int32),
        ],
        compiler_params=pltpu.CompilerParams(vmem_limit_bytes=40 << 20),
    )(meta, feats)


def prep_kernel(act_rows, got_ref, counts_ref, cols_ref):
    shards, _, _, width = got_ref.shape
    slots = shards * STRIDE
    tiles = got_ref[...].reshape(shards, STRIDE, width).astype(jnp.float32)
    meta = jnp.broadcast_to(tiles[:, META : META + 1, :], tiles.shape).reshape(slots, width)
    own = iota((slots, width), 1) % STRIDE == iota((slots, width), 0) % STRIDE
    fold = iota((width, width), 0) // STRIDE == iota((width, width), 1)
    cols = dot(
        jnp.where(own, meta, 0.0).astype(jnp.bfloat16),
        fold.astype(jnp.float32).astype(jnp.bfloat16),
    )
    cols_ref[...] = cols.astype(jnp.bfloat16)
    row_no = (iota((slots, act_rows), 1) + 1).astype(jnp.float32)
    counts = jnp.zeros((slots, act_rows), jnp.float32)
    for n in range(4):
        counts = counts + jnp.where(row_no == cols[:, n : n + 1], 1.0, 0.0)
    counts_ref[...] = counts.astype(jnp.bfloat16)


def prep(got, step_no, act_rows):
    shards, _, _, width = got.shape
    slots = shards * STRIDE
    return pl.pallas_call(
        functools.partial(prep_kernel, act_rows),
        grid=(1,),
        in_specs=[pl.BlockSpec((shards, 1, STRIDE, width), lambda i: (0, step_no, 0, 0))],
        out_specs=[
            pl.BlockSpec((slots, act_rows), lambda i: (0, 0)),
            pl.BlockSpec((slots, width), lambda i: (0, 0)),
        ],
        out_shape=[
            jax.ShapeDtypeStruct((slots, act_rows), jnp.bfloat16),
            jax.ShapeDtypeStruct((slots, width), jnp.bfloat16),
        ],
        compiler_params=pltpu.CompilerParams(vmem_limit_bytes=40 << 20),
    )(got)


def weight_column(weights_ref, step_no, act_rows):
    row = weights_ref[step_no : step_no + 1, :]
    shape = (act_rows, row.shape[1])
    here = iota(shape, 1) == iota(shape, 0) // BLK
    return jnp.sum(jnp.where(here, row, 0.0), axis=1, keepdims=True)


def forward(weighted, counts, feats, mine_ref):
    width = weighted.shape[1]
    products = sum(dot(counts, part) for part in split3(weighted)) * feats.astype(jnp.float32)
    same = iota((128, 128), 0) == iota((128, 128), 1)
    for k in range(mine_ref.shape[0]):
        column = jnp.sum(products[k * 128 : (k + 1) * 128], axis=1, keepdims=True) * width**-0.5
        mine_ref[k : k + 1, :] = jnp.sum(jnp.where(same, column, 0.0), axis=0, keepdims=True)


def first_kernel(weights_ref, rows_ref, counts_ref, got_ref, mine_ref):
    act_rows, width = rows_ref.shape
    weighted = weight_column(weights_ref, 0, act_rows) * rows_ref[...]
    forward(weighted, counts_ref[...], got_ref[...].reshape(-1, width), mine_ref)


def gradient(table_ref, mine_ref, cols_ref, got_ref, counts_ref, grad_ref):
    shards, blocks, _ = table_ref.shape
    width = got_ref.shape[3]
    feats = got_ref[...].reshape(-1, width)
    row, lane = iota((128, 128), 0), iota((128, 128), 1)
    for k in range(blocks):
        cols = cols_ref[k * 128 : (k + 1) * 128, :].astype(jnp.float32)
        wanted = iota((128, shards), 1).astype(jnp.float32) == cols[:, 4:5]
        wanted = wanted.astype(jnp.float32).astype(jnp.bfloat16)
        found = sum(dot(wanted, part) for part in split3(table_ref[:, k, :]))
        at = (row // STRIDE) * STRIDE + cols[:, 5:6].astype(jnp.int32)
        partner = jnp.sum(jnp.where(lane == at, found, 0.0), axis=1, keepdims=True)
        own = jnp.sum(jnp.where(lane == row, mine_ref[k : k + 1, :], 0.0), axis=1, keepdims=True)
        error = jax.nn.sigmoid(own + partner) - cols[:, 6:7]
        part = error * feats[k * 128 : (k + 1) * 128].astype(jnp.float32) * width**-0.5
        grad_ref[k * 128 : (k + 1) * 128, :] = part.astype(jnp.bfloat16)
    return dot(counts_ref[...], grad_ref[...], ((0,), (0,)))


def step_kernel(
    step_no, weights_ref, rows_ref, table_ref, mine_ref, cols_ref, got_ref, counts_ref,
    next_got_ref, next_counts_ref, new_rows_ref, new_mine_ref, grad_ref,
):
    act_rows, width = rows_ref.shape
    row_grad = gradient(table_ref, mine_ref, cols_ref, got_ref, counts_ref, grad_ref)
    rows = rows_ref[...] - step_rate * (weight_column(weights_ref, step_no, act_rows) * row_grad)
    new_rows_ref[...] = rows
    weighted = weight_column(weights_ref, step_no + 1, act_rows) * rows
    forward(weighted, next_counts_ref[...], next_got_ref[...].reshape(-1, width), new_mine_ref)


def last_kernel(
    step_no, weights_ref, rows_ref, initial_ref, table_ref, mine_ref, cols_ref, got_ref, counts_ref,
    delta_ref, grad_ref,
):
    act_rows = rows_ref.shape[0]
    row_grad = gradient(table_ref, mine_ref, cols_ref, got_ref, counts_ref, grad_ref)
    rows = rows_ref[...] - step_rate * (weight_column(weights_ref, step_no, act_rows) * row_grad)
    delta_ref[...] = (rows - initial_ref[...]).astype(jnp.bfloat16)


def call(kernel, args, outs, scratch=()):
    specs, arrays = [], []
    for arg in args:
        if isinstance(arg, tuple):
            array, step_no = arg
            block = (array.shape[0], 1) + array.shape[2:]
            specs.append(pl.BlockSpec(block, functools.partial(lambda s, i: (0, s, 0, 0), step_no)))
            arrays.append(array)
        else:
            specs.append(pl.BlockSpec(arg.shape, functools.partial(lambda n, i: (0,) * n, arg.ndim)))
            arrays.append(arg)
    out_specs = [
        pl.BlockSpec(out.shape, functools.partial(lambda n, i: (0,) * n, len(out.shape))) for out in outs
    ]
    result = pl.pallas_call(
        kernel,
        grid=(1,),
        in_specs=specs,
        out_specs=out_specs,
        out_shape=list(outs),
        scratch_shapes=list(scratch),
        compiler_params=pltpu.CompilerParams(vmem_limit_bytes=40 << 20),
    )(*arrays)
    return result


def merge_kernel(blocks_ref, core_ref, table_ref, mine_ref, other_ref, out_ref):
    places, act_rows, _ = mine_ref.shape
    active = act_rows // BLK
    groups = 2 * places
    low = core_ref[0] == 0
    out_ref[...] = table_ref[...]

    def one(n, carry):
        place, slot = n // active, n % active
        at = pl.ds(pl.multiple_of(slot * BLK, BLK), BLK)
        mine = mine_ref[place, at, :].astype(jnp.float32)
        other = other_ref[place, at, :].astype(jnp.float32)
        for c, value in enumerate((jnp.where(low, mine, other), jnp.where(low, other, mine))):
            where = pl.ds(pl.multiple_of(blocks_ref[2 * place + c, slot] * BLK, BLK), BLK)
            out_ref[where, :] = out_ref[where, :] + value * (1.0 / groups)
        return carry

    lax.fori_loop(0, places * active, one, 0, unroll=4)


def merge(blocks, core, table, mine, other):
    smem = pl.BlockSpec(memory_space=pltpu.SMEM)
    vmem = pl.BlockSpec(memory_space=pltpu.VMEM)
    return pl.pallas_call(
        merge_kernel,
        in_specs=[smem, smem, vmem, vmem, vmem],
        out_specs=vmem,
        out_shape=jax.ShapeDtypeStruct(table.shape, jnp.float32),
        compiler_params=pltpu.CompilerParams(vmem_limit_bytes=40 << 20),
    )(blocks, core, table, mine, other)


def body(turn, sizes, emb_table, active_blocks, hit_shards, lookup_slot, lookup_offset, block_weight, dense_feat, labels):
    shards = sizes["x"] * sizes["h"] * sizes["y"]
    _, steps, samples, _ = hit_shards.shape
    width = emb_table.shape[1]
    active = active_blocks.shape[2]
    act_rows = active * BLK
    slots = shards * STRIDE
    within = jnp.arange(BLK, dtype=jnp.int32)

    there = functools.partial(lax.ppermute, axis_name=HOME, perm=turn)
    looked = (lookup_slot[0] * BLK + lookup_offset[0] + 1).transpose(0, 2, 3, 1).reshape(steps, 8, samples)
    meta = jnp.concatenate(
        [
            hit_shards[0].transpose(0, 2, 1),
            looked,
            labels[0][:, None, :],
            jnp.zeros((steps, 5, samples), jnp.int32),
        ],
        axis=1,
    ).astype(jnp.bfloat16)
    meta = there(meta)
    feats = there(dense_feat[0])
    my_blocks = active_blocks[lax.axis_index(("a", "b", "c")), 0]
    local_index = (my_blocks[:, None] * BLK + within[None, :]).reshape(-1)
    weights = jnp.pad(block_weight[0, :, 0], ((0, 8 - steps), (0, width - active)))
    carried = there(jnp.concatenate([emb_table[local_index], weights], axis=0))
    initial, weights = carried[:act_rows], carried[act_rows:]

    packed, slot_of = pack(meta, feats, shards)
    got = lax.all_to_all(packed, GROUP, 0, 0, tiled=True)

    rows_like = jax.ShapeDtypeStruct((act_rows, width), jnp.float32)
    mine_like = jax.ShapeDtypeStruct((slots // 128, 128), jnp.float32)
    delta_like = jax.ShapeDtypeStruct((act_rows, width), jnp.bfloat16)
    scratch = [pltpu.VMEM((slots, width), jnp.bfloat16)]
    prepared = [prep(got, t, act_rows) for t in range(steps)]
    rows = initial
    (mine,) = call(first_kernel, [weights, rows, prepared[0][0], (got, 0)], [mine_like])
    tables = []
    for t in range(steps):
        table = lax.all_to_all(jnp.broadcast_to(mine[None], (shards,) + mine.shape), GROUP, 0, 0, tiled=True)
        tables.append(table)
        counts, cols = prepared[t]
        if t + 1 < steps:
            rows, mine = call(
                functools.partial(step_kernel, t),
                [weights, rows, table, mine, cols, (got, t), counts, (got, t + 1), prepared[t + 1][0]],
                [rows_like, mine_like],
                scratch,
            )
        else:
            (delta,) = call(
                functools.partial(last_kernel, t),
                [weights, rows, initial, table, mine, cols, (got, t), counts],
                [delta_like],
                scratch,
            )

    delta = there(delta)
    mine = lax.all_to_all(jnp.broadcast_to(delta[None], (sizes["a"] * 2,) + delta.shape), ("a", "b"), 0, 0, tiled=True)
    other = lax.ppermute(mine, "c", [(0, 1), (1, 0)])
    new_table = merge(active_blocks[:, 0], lax.axis_index("c")[None], emb_table, mine, other)

    me = lax.axis_index(GROUP)
    held = jnp.stack([lax.dynamic_slice(table.reshape(shards, slots), (0, me * STRIDE), (shards, STRIDE)) for table in tables])
    slot_of = slot_of.reshape(steps, 1, 2 * samples)
    onehot = (jnp.arange(shards)[None, :, None] == slot_of // STRIDE).astype(jnp.float32)
    picked = jnp.einsum("tsj,tsi->tji", held, onehot, precision=lax.Precision.HIGHEST)
    picked = jnp.sum(jnp.where(jnp.arange(STRIDE)[None, :, None] == slot_of % STRIDE, picked, 0.0), axis=1)
    logits = there(picked[:, :samples] + picked[:, samples:])
    return new_table, logits[None]


def solution(mesh):
    shards = mesh.shape["shard"]
    y = min(4, shards // 4)
    sizes = {"a": mesh.shape["replica"] // 4, "b": 2, "c": 2, "x": shards // 4 // y, "h": 4, "y": y}
    finer = Mesh(mesh.devices.reshape(tuple(sizes.values())), tuple(sizes))
    index = lambda a, b, c, h: ((a * 2 + b) * 2 + c) * 4 + h
    turn = [
        (index(a, b, c, h), index((a + sizes["a"] // 2) % sizes["a"], h // 2, h % 2, b * 2 + c))
        for a in range(sizes["a"])
        for b in range(2)
        for c in range(2)
        for h in range(4)
    ]
    group, shard = ("a", "b", "c"), ("x", "h", "y")
    placed = (
        P(shard, None),
        P(None, shard, None),
        P(group, None, shard, None),
        P(group, None, shard, None, None),
        P(group, None, shard, None, None),
        P(group, None, shard, None),
        P(group, None, shard, None),
        P(group, None, shard),
    )
    return jax.shard_map(
        functools.partial(body, turn, sizes),
        mesh=finer,
        in_specs=placed,
        out_specs=(P(shard, None), P(group, None, shard)),
        check_vma=False,
    )
```

time: 801 us -> 279 us (0.35)
  waiting for transfers between devices: 556 us -> 106 us
  starting transfers between devices: 134 us -> 99.5 us
  Pallas kernels: 0 us -> 24.4 us
  blocking collectives: 36.7 us -> 13.9 us
  between operations: 14.7 us -> 1.05 us
  other arithmetic: 16.6 us -> 3.09 us
    all_to_all x11 -> x5, waiting for transfers between devices: 304 us -> 39.6 us  [the longest x3 21.5 us: body(): lax.all_to_all(jnp.broadcast_to(mine[None], (shards,) + mine.shape), GROU...]
    psum x1 -> x0, waiting for transfers between devices: 252 us -> none  [body(): lax.psum(scattered.astype(jnp.bfloat16), 'replica').astype(jnp.float32)]
    all_to_all x11 -> x5, starting transfers between devices: 134 us -> 53.3 us  [the longest x3 31.1 us: body(): lax.all_to_all(jnp.broadcast_to(mine[None], (shards,) + mine.shape), GROU...]
    ppermute x0 -> x6, waiting for transfers between devices: none -> 66.8 us  [the longest x1 19.2 us: body(): carried = there(jnp.concatenate([emb_table[local_index], weights], axis=0))]
    ppermute x0 -> x6, starting transfers between devices: none -> 46.2 us  [the longest x1 23.6 us: body(): feats = there(dense_feat[0])]
    pallas_call x0 -> x11, Pallas kernels: none -> 24.4 us  [the longest x5 13.3 us: call(): pl.pallas_call(kernel, grid=(1,), in_specs=specs, out_specs=out_specs, ou...]
    all_to_all x1, blocking collectives: 36.7 us -> 13.9 us  [body(): lax.all_to_all(jnp.broadcast_to(mine[None], (shards,) + mine.shape), GROU...]
    unnamed x20 -> x70, local copies, waits for them, and re-layouts: 7.36 us -> 24 us
  transfers between devices with their start and end apart: 12 -> 11, of which waited for: 12 -> 8; matrix products, arithmetic and copies ran while one was open for 3% -> 3% of each run, Pallas kernels for 0% -> 1%
where the time goes in v1:
time: 279 us; the launch traced here: 278 us
  waiting for transfers between devices  106 us (38%)
  starting transfers between devices  99.5 us (36%)
  local copies, waits for them, and re-layouts  29.2 us (10%)
  Pallas kernels  24.4 us (9%)
  blocking collectives  13.9 us (5%)
  other arithmetic  3.09 us (1%)
    all_to_all x3, starting transfers between devices, body(): lax.all_to_all(jnp.broadcast_to(mine[None], (shards,) + mine.shape), GROU...  31.1 us
    unnamed x70, local copies, waits for them, and re-layouts  24 us
    ppermute x1, starting transfers between devices, body(): feats = there(dense_feat[0])  23.6 us
    all_to_all x3, waiting for transfers between devices, body(): lax.all_to_all(jnp.broadcast_to(mine[None], (shards,) + mine.shape), GROU...  21.5 us
    ppermute x1, waiting for transfers between devices, body(): carried = there(jnp.concatenate([emb_table[local_index], weights], axis=0))  19.2 us
    all_to_all x1, starting transfers between devices, body(): got = lax.all_to_all(packed, GROUP, 0, 0, tiled=True)  18.6 us
    ppermute x1, waiting for transfers between devices, body(): meta = there(meta)  18.1 us
    all_to_all x1, waiting for transfers between devices, body(): lax.all_to_all(jnp.broadcast_to(delta[None], (sizes['a'] * 2,) + delta.sh...  18.1 us
  transfers between devices with their start and end apart: 11, of which 8 were waited for; matrix products, arithmetic and copies ran while one was open for 3% of the time, Pallas kernels for 1%

profile of v1, /device:TPU:1, one launch (start us, length us, event | category | flops | bytes accessed | tf_op | source)
XLA Modules:
  0.0 277.9 jit_solution(4979352658533654984)
XLA Ops:
  0.7 23.6 %collective-permute-start.2 = (bf16[4,256,128]{2,1,0:T(8,128)(2,1)}, bf16[4,256,128]{2,1,0:T(8,128)(2,1)S(1)}, u32[]{:S(2)}, u32[]{:S(2)}) collective-permute-start(bf16[4,256,128]{2,1,0:T(8,128)(2,1)} %bitcast.57), channel_id=1, source_target_pairs={{0,512},{4,576},{8,640},{12,704},{64,516},{68,580},{72,644},{76,70... | collective-permute-start | bytes 786440 | tf_op jit(solution)/shard_map/ppermute | solution.py:265
  24.2 0.7 convert_bitcast_fusion
  25.0 0.8 fusion.9
  25.7 0.7 convert_bitcast_fusion.1
  26.6 1.9 collective-permute-start.1
  28.5 18.1 %collective-permute-done.1.meta_ref = bf16[4,16,256]{2,1,0:T(8,128)(2,1)S(1)} collective-permute-done((bf16[4,16,256]{2,1,0:T(8,128)(2,1)S(1)}, bf16[4,16,256]{2,1,0:T(8,128)(2,1)S(1)}, u32[]{:S(2)}, u32[]{:S(2)}) %collective-permute-start.1) | collective-permute-done | bytes 32800 | tf_op jit(solution)/shard_map/ppermute | solution.py:264
  46.7 3.7 %shard_map.95 = (bf16[64,4,16,128]{3,2,1,0:T(8,128)(2,1)S(1)}, s32[4,1,512]{2,1,0:T(1,128)S(1)}) custom-call(bf16[4,16,256]{2,1,0:T(8,128)(2,1)S(1)} %collective-permute-done.1.meta_ref, bf16[4,256,128]{2,1,0:T(8,128)(2,1)S(1)} %collective-permute-done.2.feat_ref), custom_call_target="tpu_custom_call" | custom-call | tf_op jit(solution)/shard_map/pallas_call | solution.py:66
  50.4 1.0 copy-done.15
  51.3 18.6 %all-to-all-start = ((bf16[64,4,16,128]{3,2,1,0:T(8,128)(2,1)}), bf16[64,4,16,128]{3,2,1,0:T(8,128)(2,1)S(1)}, u32[]{:S(2)}, u32[]{:S(2)}) async-start(bf16[64,4,16,128]{3,2,1,0:T(8,128)(2,1)} %copy-done.15), calls=%async_computation | async-start | bytes 2097152 | tf_op jit(solution)/shard_map/all_to_all | solution.py:273
  70.0 0.7 fusion.11
  70.8 0.7 gather_fusion
  71.6 1.9 collective-permute-start
  73.5 19.2 %collective-permute-done = f32[264,128]{1,0:T(8,128)S(1)} collective-permute-done((f32[264,128]{1,0:T(8,128)S(1)}, f32[264,128]{1,0:T(8,128)S(1)}, u32[]{:S(2)}, u32[]{:S(2)}) %collective-permute-start) | collective-permute-done | bytes 135200 | tf_op jit(solution)/shard_map/ppermute | solution.py:269
  92.7 0.8 shard_map.96
  93.5 0.7 copy-done.22
  94.2 0.7 shard_map.97.mine_ref
  95.0 0.8 copy-done.7
  95.8 0.7 broadcast_in_dim.21
  96.5 20.2 %all-to-all-start.1 = ((f32[64,8,128]{2,1,0:T(8,128)}), f32[64,8,128]{2,1,0:T(8,128)S(1)}, u32[]{:S(2)}, u32[]{:S(2)}) async-start(f32[64,8,128]{2,1,0:T(8,128)} %broadcast_in_dim.21), calls=%async_computation.1 | async-start | bytes 524288 | tf_op jit(solution)/shard_map/all_to_all | solution.py:284
  116.7 0.8 shard_map.98
  117.5 0.8 copy-done.12
  118.3 0.7 copy-done.20
  119.0 7.1 %all-to-all-done.1.table_ref = f32[64,8,128]{2,1,0:T(8,128)S(1)} async-done(((f32[64,8,128]{2,1,0:T(8,128)}), f32[64,8,128]{2,1,0:T(8,128)S(1)}, u32[]{:S(2)}, u32[]{:S(2)}) %all-to-all-start.1) | async-done | bytes 262176 | tf_op jit(solution)/shard_map/all_to_all | solution.py:284
  126.2 1.1 copy-done.8
  127.3 1.0 copy-done.13
  128.3 0.9 copy-done.23
  129.3 2.9 %shard_map.99 = (f32[256,128]{1,0:T(8,128)S(1)}, f32[8,128]{1,0:T(8,128)S(1)}) custom-call(f32[8,128]{1,0:T(8,128)S(1)} %slice.18.weights_ref, f32[256,128]{1,0:T(8,128)S(1)} %slice.19.rows_ref.initial_ref, f32[64,8,128]{2,1,0:T(8,128)S(1)} %all-to-all-done.1.table_ref, f32[8,128]{1,0:T(8,128)S(1)} %shard_map.97.mine_ref, bf16[1024,128]{1,0:T(8,128)(2,1)S(1)} %copy-done.23, ...), custom_call_target="tpu_custom_call" | custom-call | tf_op jit(solution)/shard_map/pallas_call | solution.py:200
  132.9 0.7 broadcast_in_dim.22
  134.2 5.8 %all-to-all-start.2 = ((f32[64,8,128]{2,1,0:T(8,128)}), f32[64,8,128]{2,1,0:T(8,128)}, u32[]{:S(2)}, u32[]{:S(2)}) async-start(f32[64,8,128]{2,1,0:T(8,128)} %broadcast_in_dim.22), calls=%async_computation.2 | async-start | bytes 524288 | tf_op jit(solution)/shard_map/all_to_all | solution.py:284
  140.0 0.8 shard_map.100
  140.8 0.8 copy-done.9
  141.6 0.7 copy-done.18
  142.3 7.1 %all-to-all-done.2.table_ref = f32[64,8,128]{2,1,0:T(8,128)} async-done(((f32[64,8,128]{2,1,0:T(8,128)}), f32[64,8,128]{2,1,0:T(8,128)}, u32[]{:S(2)}, u32[]{:S(2)}) %all-to-all-start.2) | async-done | bytes 262176 | tf_op jit(solution)/shard_map/all_to_all | solution.py:284
  149.4 1.0 copy-done.10
  150.5 1.0 copy-done.14
  151.5 0.9 copy-done.21
  152.5 0.9 copy-done.27
  153.4 0.7 copy-done.29
  154.1 4.0 %shard_map.101 = (f32[256,128]{1,0:T(8,128)S(1)}, f32[8,128]{1,0:T(8,128)S(1)}) custom-call(f32[8,128]{1,0:T(8,128)S(1)} %slice.18.weights_ref, f32[256,128]{1,0:T(8,128)S(1)} %copy-done.27, f32[64,8,128]{2,1,0:T(8,128)} %all-to-all-done.2.table_ref, f32[8,128]{1,0:T(8,128)S(1)} %copy-done.29, bf16[1024,128]{1,0:T(8,128)(2,1)S(1)} %copy-done.21, ...), custom_call_target="tpu_custom_call" | custom-call | tf_op jit(solution)/shard_map/pallas_call | solution.py:200
  158.7 0.7 broadcast_in_dim.23
  159.4 5.0 %all-to-all-start.3 = ((f32[64,8,128]{2,1,0:T(8,128)}), f32[64,8,128]{2,1,0:T(8,128)S(1)}, u32[]{:S(2)}, u32[]{:S(2)}) async-start(f32[64,8,128]{2,1,0:T(8,128)} %broadcast_in_dim.23), calls=%async_computation.3 | async-start | bytes 524288 | tf_op jit(solution)/shard_map/all_to_all | solution.py:284
  164.4 0.8 shard_map.102
  165.3 0.8 copy-done.4
  166.0 0.7 copy-done.16
  166.7 7.2 %all-to-all-done.3.table_ref = f32[64,8,128]{2,1,0:T(8,128)S(1)} async-done(((f32[64,8,128]{2,1,0:T(8,128)}), f32[64,8,128]{2,1,0:T(8,128)S(1)}, u32[]{:S(2)}, u32[]{:S(2)}) %all-to-all-start.3) | async-done | bytes 262176 | tf_op jit(solution)/shard_map/all_to_all | solution.py:284
  174.0 1.1 copy-done.5
  175.1 1.0 copy-done.11
  176.2 0.9 copy-done.19
  177.1 0.9 copy-done.25
  178.0 2.9 %shard_map.103 = (f32[256,128]{1,0:T(8,128)S(1)}, f32[8,128]{1,0:T(8,128)S(1)}) custom-call(f32[8,128]{1,0:T(8,128)S(1)} %slice.18.weights_ref, f32[256,128]{1,0:T(8,128)S(1)} %copy-done.25, f32[64,8,128]{2,1,0:T(8,128)S(1)} %all-to-all-done.3.table_ref, f32[8,128]{1,0:T(8,128)S(1)} %get-tuple-element.27.mine_ref, bf16[1024,128]{1,0:T(8,128)(2,1)S(1)} %copy-done.19, ...), custom_call_target="tpu_custom_call" | custom-call | tf_op jit(solution)/shard_map/pallas_call | solution.py:200
  181.0 13.9 %all_to_all.30.table_ref = f32[64,8,128]{2,1,0:T(8,128)S(1)} all-to-all(f32[64,8,128]{2,1,0:T(8,128)S(1)} %broadcast_in_dim.24), channel_id=1, replica_groups=mesh['a'=4,'b'=2,'c'=2,'x'=4,'h'=4,'y'=4] {'x','b','c','y'}, dimensions={0} | all-to-all | bytes 524288 | tf_op jit(solution)/shard_map/all_to_all | solution.py:284
  194.9 2.8 %shard_map.104 = bf16[256,128]{1,0:T(8,128)(2,1)S(1)} custom-call(f32[8,128]{1,0:T(8,128)S(1)} %slice.18.weights_ref, f32[256,128]{1,0:T(8,128)S(1)} %get-tuple-element.30.rows_ref, f32[256,128]{1,0:T(8,128)S(1)} %slice.19.rows_ref.initial_ref, f32[64,8,128]{2,1,0:T(8,128)S(1)} %all_to_all.30.table_ref, f32[8,128]{1,0:T(8,128)S(1)} %get-tuple-element.31.mine_ref, ...), custom_call_target="tpu_custom_call" | custom-call | tf_op jit(solution)/shard_map/pallas_call | solution.py:200
  197.7 6.2 %collective-permute-start.3 = (bf16[256,128]{1,0:T(8,128)(2,1)S(1)}, bf16[256,128]{1,0:T(8,128)(2,1)S(1)}, u32[]{:S(2)}, u32[]{:S(2)}) collective-permute-start(bf16[256,128]{1,0:T(8,128)(2,1)S(1)} %shard_map.104), channel_id=1, source_target_pairs={{0,512},{4,576},{8,640},{12,704},{64,516},{68,580},{72,644},{76,70... | collective-permute-start | bytes 196616 | tf_op jit(solution)/shard_map/ppermute | solution.py:302
  204.0 13.0 %collective-permute-done.3 = bf16[256,128]{1,0:T(8,128)(2,1)S(1)} collective-permute-done((bf16[256,128]{1,0:T(8,128)(2,1)S(1)}, bf16[256,128]{1,0:T(8,128)(2,1)S(1)}, u32[]{:S(2)}, u32[]{:S(2)}) %collective-permute-start.3) | collective-permute-done | bytes 65568 | tf_op jit(solution)/shard_map/ppermute | solution.py:302
  216.9 0.9 broadcast_in_dim.25
  217.8 3.6 %all-to-all-start.5 = ((bf16[8,256,128]{2,1,0:T(8,128)(2,1)}), bf16[8,256,128]{2,1,0:T(8,128)(2,1)S(1)}, u32[]{:S(2)}, u32[]{:S(2)}) async-start(bf16[8,256,128]{2,1,0:T(8,128)(2,1)} %broadcast_in_dim.25), calls=%async_computation.5 | async-start | bytes 1048576 | tf_op jit(solution)/shard_map/all_to_all | solution.py:303
  221.5 1.0 copy.34
  222.5 1.7 copy.33
  224.2 18.1 %all-to-all-done.5.mine_ref = bf16[8,256,128]{2,1,0:T(8,128)(2,1)S(1)} async-done(((bf16[8,256,128]{2,1,0:T(8,128)(2,1)}), bf16[8,256,128]{2,1,0:T(8,128)(2,1)S(1)}, u32[]{:S(2)}, u32[]{:S(2)}) %all-to-all-start.5) | async-done | bytes 524320 | tf_op jit(solution)/shard_map/all_to_all | solution.py:303
  242.3 10.6 %collective-permute-start.4 = (bf16[8,256,128]{2,1,0:T(8,128)(2,1)S(1)}, bf16[8,256,128]{2,1,0:T(8,128)(2,1)}, u32[]{:S(2)}, u32[]{:S(2)}) collective-permute-start(bf16[8,256,128]{2,1,0:T(8,128)(2,1)S(1)} %all-to-all-done.5.mine_ref), channel_id=1, source_target_pairs={{0,64},{64,0},{1,65},{65,1},{2,66},{66,2},{3,67},{67,3},{4,68},{68... | collective-permute-start | bytes 1572872 | tf_op jit(solution)/shard_map/ppermute | solution.py:304
  252.9 0.8 constant_dynamic-slice_fusion.2
  254.6 1.9 collective-permute-start.5
  256.5 16.5 %collective-permute-done.5 = f32[4,256]{1,0:T(4,128)S(1)} collective-permute-done((f32[4,256]{1,0:T(4,128)S(1)}, f32[4,256]{1,0:T(4,128)S(1)}, u32[]{:S(2)}, u32[]{:S(2)}) %collective-permute-start.5) | collective-permute-done | bytes 4128 | tf_op jit(solution)/shard_map/ppermute | solution.py:313
  273.1 4.2 %shard_map.105 = f32[4096,128]{1,0:T(8,128)} custom-call(s32[16,16]{1,0:T(8,128)S(1)} %bitcast.45, s32[1]{0:T(128)} %bitcast.1.core_ref, f32[4096,128]{1,0:T(8,128)S(1)} %copy-done, bf16[8,256,128]{2,1,0:T(8,128)(2,1)S(1)} %all-to-all-done.5.mine_ref, bf16[8,256,128]{2,1,0:T(8,128)(2,1)} %collective-permute-done.4.other_ref), custom_call_target="tpu_custom_call" | custom-call | tf_op jit(solution)/shard_map/pallas_call | solution.py:235
  (72 shorter events, 3.8 us)
Async XLA Ops:
  0.6 70.2 %copy-start = (f32[4096,128]{1,0:T(8,128)S(1)}, f32[4096,128]{1,0:T(8,128)}, u32[]{:S(2)}) copy-start(f32[4096,128]{1,0:T(8,128)} %table_ref.1) | copy-start | bytes 6291460
  0.6 70.9 %copy-start.31 = (f32[1,4,1,16]{3,2,1,0:T(1,128)S(1)}, f32[1,4,1,16]{3,2,1,0:T(1,128)}, u32[]{:S(2)}) copy-start(f32[1,4,1,16]{3,2,1,0:T(1,128)} %param.13) | copy-start | bytes 772
  0.7 46.0 %collective-permute-start.2 = (bf16[4,256,128]{2,1,0:T(8,128)(2,1)}, bf16[4,256,128]{2,1,0:T(8,128)(2,1)S(1)}, u32[]{:S(2)}, u32[]{:S(2)}) collective-permute-start(bf16[4,256,128]{2,1,0:T(8,128)(2,1)} %bitcast.57), channel_id=1, source_target_pairs={{0,512},{4,576},{8,640},{12,704},{64,516},{68,580},{72,644},{76,70... | collective-permute-start | bytes 786440 | tf_op jit(solution)/shard_map/ppermute | solution.py:265
  26.6 20.0 %collective-permute-start.1 = (bf16[4,16,256]{2,1,0:T(8,128)(2,1)S(1)}, bf16[4,16,256]{2,1,0:T(8,128)(2,1)S(1)}, u32[]{:S(2)}, u32[]{:S(2)}) collective-permute-start(bf16[4,16,256]{2,1,0:T(8,128)(2,1)S(1)} %maximum_maximum_fusion), channel_id=1, source_target_pairs={{0,512},{4,576},{8,640},{12,704},{64,516},{68,580},{72,644},{76,70... | collective-permute-start | bytes 98312 | tf_op jit(solution)/shard_map/ppermute | solution.py:264
  50.4 1.0 copy-start.15
  51.3 41.4 %all-to-all-start = ((bf16[64,4,16,128]{3,2,1,0:T(8,128)(2,1)}), bf16[64,4,16,128]{3,2,1,0:T(8,128)(2,1)S(1)}, u32[]{:S(2)}, u32[]{:S(2)}) async-start(bf16[64,4,16,128]{3,2,1,0:T(8,128)(2,1)} %copy-done.15), calls=%async_computation | async-start | bytes 2097152 | tf_op jit(solution)/shard_map/all_to_all | solution.py:273
  71.6 21.1 %collective-permute-start = (f32[264,128]{1,0:T(8,128)S(1)}, f32[264,128]{1,0:T(8,128)S(1)}, u32[]{:S(2)}, u32[]{:S(2)}) collective-permute-start(f32[264,128]{1,0:T(8,128)S(1)} %select_maximum_fusion), channel_id=1, source_target_pairs={{0,512},{4,576},{8,640},{12,704},{64,516},{68,580},{72,644},{76,70... | collective-permute-start | bytes 405512 | tf_op jit(solution)/shard_map/ppermute | solution.py:269
  93.5 0.7 copy-start.22
  95.0 0.8 copy-start.7
  96.5 29.7 %all-to-all-start.1 = ((f32[64,8,128]{2,1,0:T(8,128)}), f32[64,8,128]{2,1,0:T(8,128)S(1)}, u32[]{:S(2)}, u32[]{:S(2)}) async-start(f32[64,8,128]{2,1,0:T(8,128)} %broadcast_in_dim.21), calls=%async_computation.1 | async-start | bytes 524288 | tf_op jit(solution)/shard_map/all_to_all | solution.py:284
  117.5 0.8 copy-start.12
  118.3 0.7 copy-start.20
  126.2 8.0 %copy-start.1 = (f32[64,8,128]{2,1,0:T(8,128)}, f32[64,8,128]{2,1,0:T(8,128)S(1)}, u32[]{:S(2)}) copy-start(f32[64,8,128]{2,1,0:T(8,128)S(1)} %all-to-all-done.1.table_ref) | copy-start | bytes 786436
  126.2 1.1 copy-start.8
  127.3 1.0 copy-start.13
  128.3 0.9 copy-start.23
  132.2 0.7 copy-start.26
  133.6 0.6 copy-start.28
  134.2 15.3 %all-to-all-start.2 = ((f32[64,8,128]{2,1,0:T(8,128)}), f32[64,8,128]{2,1,0:T(8,128)}, u32[]{:S(2)}, u32[]{:S(2)}) async-start(f32[64,8,128]{2,1,0:T(8,128)} %broadcast_in_dim.22), calls=%async_computation.2 | async-start | bytes 524288 | tf_op jit(solution)/shard_map/all_to_all | solution.py:284
  140.8 0.8 copy-start.9
  141.6 0.7 copy-start.18
  149.4 1.0 copy-start.10
  150.5 1.0 copy-start.14
  151.5 0.9 copy-start.21
  152.5 0.9 copy-start.27
  153.4 0.7 copy-start.29
  158.0 0.7 copy-start.24
  159.4 14.6 %all-to-all-start.3 = ((f32[64,8,128]{2,1,0:T(8,128)}), f32[64,8,128]{2,1,0:T(8,128)S(1)}, u32[]{:S(2)}, u32[]{:S(2)}) async-start(f32[64,8,128]{2,1,0:T(8,128)} %broadcast_in_dim.23), calls=%async_computation.3 | async-start | bytes 524288 | tf_op jit(solution)/shard_map/all_to_all | solution.py:284
  165.2 0.8 copy-start.4
  166.0 0.7 copy-start.16
  174.0 7.0 %copy-start.2 = (f32[64,8,128]{2,1,0:T(8,128)}, f32[64,8,128]{2,1,0:T(8,128)S(1)}, u32[]{:S(2)}) copy-start(f32[64,8,128]{2,1,0:T(8,128)S(1)} %all-to-all-done.3.table_ref) | copy-start | bytes 786436
  174.0 1.1 copy-start.5
  175.1 1.0 copy-start.11
  176.2 0.9 copy-start.19
  177.1 0.9 copy-start.25
  178.0 16.9 %copy-start.6 = (bf16[1024,256]{1,0:T(8,128)(2,1)S(1)}, bf16[1024,256]{1,0:T(8,128)(2,1)}, u32[]{:S(2)}) copy-start(bf16[1024,256]{1,0:T(8,128)(2,1)} %copy-done.4) | copy-start | bytes 1572868
  178.0 16.9 %copy-start.17 = (bf16[1024,128]{1,0:T(8,128)(2,1)S(1)}, bf16[1024,128]{1,0:T(8,128)(2,1)}, u32[]{:S(2)}) copy-start(bf16[1024,128]{1,0:T(8,128)(2,1)} %copy-done.16) | copy-start | bytes 786436
  197.7 56.2 %copy-start.3 = (f32[64,8,128]{2,1,0:T(8,128)S(1)}, f32[64,8,128]{2,1,0:T(8,128)}, u32[]{:S(2)}) copy-start(f32[64,8,128]{2,1,0:T(8,128)} %copy-done.2) | copy-start | bytes 786436
  197.7 19.2 %collective-permute-start.3 = (bf16[256,128]{1,0:T(8,128)(2,1)S(1)}, bf16[256,128]{1,0:T(8,128)(2,1)S(1)}, u32[]{:S(2)}, u32[]{:S(2)}) collective-permute-start(bf16[256,128]{1,0:T(8,128)(2,1)S(1)} %shard_map.104), channel_id=1, source_target_pairs={{0,512},{4,576},{8,640},{12,704},{64,516},{68,580},{72,644},{76,70... | collective-permute-start | bytes 196616 | tf_op jit(solution)/shard_map/ppermute | solution.py:302
  217.8 55.3 %copy-start.30 = (s32[16,1,16]{2,1,0:T(1,128)S(1)}, s32[16,1,16]{2,1,0:T(1,128)}, u32[]{:S(2)}) copy-start(s32[16,1,16]{2,1,0:T(1,128)} %param.9) | copy-start | bytes 3076
  217.8 24.5 %all-to-all-start.5 = ((bf16[8,256,128]{2,1,0:T(8,128)(2,1)}), bf16[8,256,128]{2,1,0:T(8,128)(2,1)S(1)}, u32[]{:S(2)}, u32[]{:S(2)}) async-start(bf16[8,256,128]{2,1,0:T(8,128)(2,1)} %broadcast_in_dim.25), calls=%async_computation.5 | async-start | bytes 1048576 | tf_op jit(solution)/shard_map/all_to_all | solution.py:303
  242.3 30.7 %collective-permute-start.4 = (bf16[8,256,128]{2,1,0:T(8,128)(2,1)S(1)}, bf16[8,256,128]{2,1,0:T(8,128)(2,1)}, u32[]{:S(2)}, u32[]{:S(2)}) collective-permute-start(bf16[8,256,128]{2,1,0:T(8,128)(2,1)S(1)} %all-to-all-done.5.mine_ref), channel_id=1, source_target_pairs={{0,64},{64,0},{1,65},{65,1},{2,66},{66,2},{3,67},{67,3},{4,68},{68... | collective-permute-start | bytes 1572872 | tf_op jit(solution)/shard_map/ppermute | solution.py:304
  254.6 18.4 %collective-permute-start.5 = (f32[4,256]{1,0:T(4,128)S(1)}, f32[4,256]{1,0:T(4,128)S(1)}, u32[]{:S(2)}, u32[]{:S(2)}) collective-permute-start(f32[4,256]{1,0:T(4,128)S(1)} %slice_add_fusion), channel_id=1, source_target_pairs={{0,512},{4,576},{8,640},{12,704},{64,516},{68,580},{72,644},{76,70... | collective-permute-start | bytes 12296 | tf_op jit(solution)/shard_map/ppermute | solution.py:313

commit v2 on v1

--- a/solution.py
+++ b/solution.py
@@ -11,6 +11,7 @@
 BLK = 16
 STRIDE = 16
 META = 12
+VMEM_LIMIT = 16 << 20
 step_rate = 1.0
 
 GROUP = ("x", "b", "c", "y")
@@ -78,7 +79,7 @@
             jax.ShapeDtypeStruct((shards, steps, STRIDE, width), jnp.bfloat16),
             jax.ShapeDtypeStruct((steps, 1, 2 * samples), jnp.int32),
         ],
-        compiler_params=pltpu.CompilerParams(vmem_limit_bytes=40 << 20),
+        compiler_params=pltpu.CompilerParams(vmem_limit_bytes=VMEM_LIMIT),
     )(meta, feats)
 
 
@@ -116,7 +117,7 @@
             jax.ShapeDtypeStruct((slots, act_rows), jnp.bfloat16),
             jax.ShapeDtypeStruct((slots, width), jnp.bfloat16),
         ],
-        compiler_params=pltpu.CompilerParams(vmem_limit_bytes=40 << 20),
+        compiler_params=pltpu.CompilerParams(vmem_limit_bytes=VMEM_LIMIT),
     )(got)
 
 
@@ -131,9 +132,12 @@
     width = weighted.shape[1]
     products = sum(dot(counts, part) for part in split3(weighted)) * feats.astype(jnp.float32)
     same = iota((128, 128), 0) == iota((128, 128), 1)
-    for k in range(mine_ref.shape[0]):
+    mine = []
+    for k in range(mine_ref.shape[1]):
         column = jnp.sum(products[k * 128 : (k + 1) * 128], axis=1, keepdims=True) * width**-0.5
-        mine_ref[k : k + 1, :] = jnp.sum(jnp.where(same, column, 0.0), axis=0, keepdims=True)
+        mine.append(jnp.sum(jnp.where(same, column, 0.0), axis=0, keepdims=True))
+    mine = jnp.concatenate(mine, axis=0)
+    mine_ref[...] = jnp.broadcast_to(mine[None], mine_ref.shape)
 
 
 def first_kernel(weights_ref, rows_ref, counts_ref, got_ref, mine_ref):
@@ -154,7 +158,7 @@
         found = sum(dot(wanted, part) for part in split3(table_ref[:, k, :]))
         at = (row // STRIDE) * STRIDE + cols[:, 5:6].astype(jnp.int32)
         partner = jnp.sum(jnp.where(lane == at, found, 0.0), axis=1, keepdims=True)
-        own = jnp.sum(jnp.where(lane == row, mine_ref[k : k + 1, :], 0.0), axis=1, keepdims=True)
+        own = jnp.sum(jnp.where(lane == row, mine_ref[0, k : k + 1, :], 0.0), axis=1, keepdims=True)
         error = jax.nn.sigmoid(own + partner) - cols[:, 6:7]
         part = error * feats[k * 128 : (k + 1) * 128].astype(jnp.float32) * width**-0.5
         grad_ref[k * 128 : (k + 1) * 128, :] = part.astype(jnp.bfloat16)
@@ -173,14 +177,39 @@
     forward(weighted, next_counts_ref[...], next_got_ref[...].reshape(-1, width), new_mine_ref)
 
 
+def own_logits(me, table_ref, slot):
+    shards, blocks, _ = table_ref.shape
+    hits = slot.shape[1]
+    part = sum(jnp.where(me // (128 // STRIDE) == k, table_ref[:, k, :], 0.0) for k in range(blocks))
+    onehot = iota((shards, hits), 0) == slot // STRIDE
+    onehot = onehot.astype(jnp.float32).astype(jnp.bfloat16)
+    found = sum(dot(term, onehot, ((0,), (0,))) for term in split3(part))
+    at = (me % (128 // STRIDE)) * STRIDE + slot % STRIDE
+    picked = jnp.sum(jnp.where(iota((128, hits), 0) == at, found, 0.0), axis=0, keepdims=True)
+    logits = picked[:, : hits // 2] + picked[:, hits // 2 :]
+    return jnp.concatenate([logits[:, n : n + 128] for n in range(0, hits // 2, 128)], axis=0)
+
+
+def early_kernel(me_ref, slot_ref, *refs):
+    tables, out_ref = refs[:-1], refs[-1]
+    done = [own_logits(me_ref[0], table_ref, slot_ref[t]) for t, table_ref in enumerate(tables)]
+    missing = out_ref.shape[0] - sum(part.shape[0] for part in done)
+    out_ref[...] = jnp.concatenate(done + [jnp.zeros((missing, 128), jnp.float32)], axis=0)
+
+
 def last_kernel(
-    step_no, weights_ref, rows_ref, initial_ref, table_ref, mine_ref, cols_ref, got_ref, counts_ref,
-    delta_ref, grad_ref,
+    step_no, me_ref, slot_ref, early_ref, weights_ref, rows_ref, initial_ref, table_ref, mine_ref, cols_ref, got_ref,
+    counts_ref, back_ref, grad_ref,
 ):
     act_rows = rows_ref.shape[0]
     row_grad = gradient(table_ref, mine_ref, cols_ref, got_ref, counts_ref, grad_ref)
     rows = rows_ref[...] - step_rate * (weight_column(weights_ref, step_no, act_rows) * row_grad)
-    delta_ref[...] = (rows - initial_ref[...]).astype(jnp.bfloat16)
+    back_ref[:act_rows, :] = (rows - initial_ref[...]).astype(jnp.bfloat16)
+    logits = own_logits(me_ref[0], table_ref, slot_ref[step_no])
+    known = early_ref.shape[0] - logits.shape[0]
+    logits = jnp.concatenate([early_ref[:known, :], logits], axis=0)
+    terms = [term.astype(jnp.float32) for term in split3(logits)]
+    back_ref[act_rows:, :] = jnp.concatenate(terms + [jnp.zeros_like(logits)], axis=0).astype(jnp.bfloat16)
 
 
 def call(kernel, args, outs, scratch=()):
@@ -191,6 +220,9 @@
             block = (array.shape[0], 1) + array.shape[2:]
             specs.append(pl.BlockSpec(block, functools.partial(lambda s, i: (0, s, 0, 0), step_no)))
             arrays.append(array)
+        elif arg.size == 1:
+            specs.append(pl.BlockSpec(memory_space=pltpu.SMEM))
+            arrays.append(arg)
         else:
             specs.append(pl.BlockSpec(arg.shape, functools.partial(lambda n, i: (0,) * n, arg.ndim)))
             arrays.append(arg)
@@ -204,7 +236,7 @@
         out_specs=out_specs,
         out_shape=list(outs),
         scratch_shapes=list(scratch),
-        compiler_params=pltpu.CompilerParams(vmem_limit_bytes=40 << 20),
+        compiler_params=pltpu.CompilerParams(vmem_limit_bytes=VMEM_LIMIT),
     )(*arrays)
     return result
 
@@ -237,7 +269,7 @@
         in_specs=[smem, smem, vmem, vmem, vmem],
         out_specs=vmem,
         out_shape=jax.ShapeDtypeStruct(table.shape, jnp.float32),
-        compiler_params=pltpu.CompilerParams(vmem_limit_bytes=40 << 20),
+        compiler_params=pltpu.CompilerParams(vmem_limit_bytes=VMEM_LIMIT),
     )(blocks, core, table, mine, other)
 
 
@@ -267,22 +299,25 @@
     local_index = (my_blocks[:, None] * BLK + within[None, :]).reshape(-1)
     weights = jnp.pad(block_weight[0, :, 0], ((0, 8 - steps), (0, width - active)))
     carried = there(jnp.concatenate([emb_table[local_index], weights], axis=0))
+    meta, feats, carried = lax.optimization_barrier((meta, feats, carried))
     initial, weights = carried[:act_rows], carried[act_rows:]
 
     packed, slot_of = pack(meta, feats, shards)
     got = lax.all_to_all(packed, GROUP, 0, 0, tiled=True)
 
+    logit_rows = steps * samples // 128
     rows_like = jax.ShapeDtypeStruct((act_rows, width), jnp.float32)
-    mine_like = jax.ShapeDtypeStruct((slots // 128, 128), jnp.float32)
-    delta_like = jax.ShapeDtypeStruct((act_rows, width), jnp.bfloat16)
+    mine_like = jax.ShapeDtypeStruct((shards, slots // 128, 128), jnp.float32)
+    early_like = jax.ShapeDtypeStruct((logit_rows, 128), jnp.float32)
+    back_like = jax.ShapeDtypeStruct((act_rows + 4 * logit_rows, width), jnp.bfloat16)
     scratch = [pltpu.VMEM((slots, width), jnp.bfloat16)]
+    me = lax.axis_index(GROUP)[None]
     prepared = [prep(got, t, act_rows) for t in range(steps)]
     rows = initial
     (mine,) = call(first_kernel, [weights, rows, prepared[0][0], (got, 0)], [mine_like])
     tables = []
     for t in range(steps):
-        table = lax.all_to_all(jnp.broadcast_to(mine[None], (shards,) + mine.shape), GROUP, 0, 0, tiled=True)
-        tables.append(table)
+        table = lax.all_to_all(mine, GROUP, 0, 0, tiled=True)
         counts, cols = prepared[t]
         if t + 1 < steps:
             rows, mine = call(
@@ -291,26 +326,22 @@
                 [rows_like, mine_like],
                 scratch,
             )
+            tables.append(table)
         else:
-            (delta,) = call(
+            (early,) = call(early_kernel, [me, slot_of, *tables], [early_like])
+            (back,) = call(
                 functools.partial(last_kernel, t),
-                [weights, rows, initial, table, mine, cols, (got, t), counts],
-                [delta_like],
+                [me, slot_of, early, weights, rows, initial, table, mine, cols, (got, t), counts],
+                [back_like],
                 scratch,
             )
 
-    delta = there(delta)
+    back = there(back)
+    delta, terms = back[:act_rows], back[act_rows:].astype(jnp.float32).reshape(4, logit_rows, 128)
     mine = lax.all_to_all(jnp.broadcast_to(delta[None], (sizes["a"] * 2,) + delta.shape), ("a", "b"), 0, 0, tiled=True)
     other = lax.ppermute(mine, "c", [(0, 1), (1, 0)])
     new_table = merge(active_blocks[:, 0], lax.axis_index("c")[None], emb_table, mine, other)
-
-    me = lax.axis_index(GROUP)
-    held = jnp.stack([lax.dynamic_slice(table.reshape(shards, slots), (0, me * STRIDE), (shards, STRIDE)) for table in tables])
-    slot_of = slot_of.reshape(steps, 1, 2 * samples)
-    onehot = (jnp.arange(shards)[None, :, None] == slot_of // STRIDE).astype(jnp.float32)
-    picked = jnp.einsum("tsj,tsi->tji", held, onehot, precision=lax.Precision.HIGHEST)
-    picked = jnp.sum(jnp.where(jnp.arange(STRIDE)[None, :, None] == slot_of % STRIDE, picked, 0.0), axis=1)
-    logits = there(picked[:, :samples] + picked[:, samples:])
+    logits = (terms[0] + terms[1] + terms[2]).reshape(steps, samples)
     return new_table, logits[None]
 
 

time: 279 us -> 247 us (0.89)
  waiting for transfers between devices: 106 us -> 76.2 us
  local copies, waits for them, and re-layouts: 29.2 us -> 10.5 us
  blocking collectives: 13.9 us -> 25.9 us
  Pallas kernels: 24.4 us -> 32.3 us
  starting transfers between devices: 99.5 us -> 96.6 us
    ppermute x1, waiting for transfers between devices: 19.2 us -> 0.01 us  [body(): carried = there(jnp.concatenate([emb_table[local_index], weights], axis=0))]
    all_to_all x1, waiting for transfers between devices: 0.01 us -> 17 us  [body(): got = lax.all_to_all(packed, GROUP, 0, 0, tiled=True)]
    unnamed x70 -> x24, local copies, waits for them, and re-layouts: 24 us -> 7.36 us
    ppermute x1, starting transfers between devices: 1.91 us -> 17.2 us  [body(): meta = there(meta)]
    all_to_all x4, starting transfers between devices: 34.7 us -> 20.6 us  [body(): table = lax.all_to_all(mine, GROUP, 0, 0, tiled=True)]
    ppermute x1, waiting for transfers between devices: 18.1 us -> 4.26 us  [body(): meta = there(meta)]
    all_to_all x1, blocking collectives: 13.9 us -> 25.9 us  [body(): lax.all_to_all(jnp.broadcast_to(delta[None], (sizes['a'] * 2,) + delta.sh...]
    ppermute x2 -> x1, waiting for transfers between devices: 29.5 us -> 19.6 us  [body(): back = there(back)]
  transfers between devices with their start and end apart: 11 -> 10, of which waited for: 8 -> 8; matrix products, arithmetic and copies ran while one was open for 3% -> 3% of each run, Pallas kernels for 1% -> 1%
where the time goes in v2:
time: 247 us; the launch traced here: 246 us
  starting transfers between devices  96.6 us (39%)
  waiting for transfers between devices  76.2 us (31%)
  Pallas kernels  32.3 us (13%)
  blocking collectives  25.9 us (10%)
  local copies, waits for them, and re-layouts  10.5 us (4%)
  other arithmetic  3.72 us (2%)
    all_to_all x4, waiting for transfers between devices, body(): table = lax.all_to_all(mine, GROUP, 0, 0, tiled=True)  34.4 us
    all_to_all x1, blocking collectives, body(): lax.all_to_all(jnp.broadcast_to(delta[None], (sizes['a'] * 2,) + delta.sh...  25.9 us
    ppermute x1, starting transfers between devices, body(): feats = there(dense_feat[0])  23.5 us
    all_to_all x1, starting transfers between devices, body(): got = lax.all_to_all(packed, GROUP, 0, 0, tiled=True)  22.4 us
    pallas_call x6, Pallas kernels, call(): pl.pallas_call(kernel, grid=(1,), in_specs=specs, out_specs=out_specs, ou...  20.9 us
    all_to_all x4, starting transfers between devices, body(): table = lax.all_to_all(mine, GROUP, 0, 0, tiled=True)  20.6 us
    ppermute x1, waiting for transfers between devices, body(): back = there(back)  19.6 us
    ppermute x1, starting transfers between devices, body(): meta = there(meta)  17.2 us
  transfers between devices with their start and end apart: 10, of which 8 were waited for; matrix products, arithmetic and copies ran while one was open for 3% of the time, Pallas kernels for 1%

profile of v2, /device:TPU:1, one launch (start us, length us, event | category | flops | bytes accessed | tf_op | source)
XLA Modules:
  0.0 246.1 jit_solution(4889589992179250199)
XLA Ops:
  0.6 23.5 %collective-permute-start.1 = (bf16[4,256,128]{2,1,0:T(8,128)(2,1)}, bf16[4,256,128]{2,1,0:T(8,128)(2,1)S(1)}, u32[]{:S(2)}, u32[]{:S(2)}) collective-permute-start(bf16[4,256,128]{2,1,0:T(8,128)(2,1)} %bitcast.21), channel_id=1, source_target_pairs={{0,512},{4,576},{8,640},{12,704},{64,516},{68,580},{72,644},{76,70... | collective-permute-start | bytes 786440 | tf_op jit(solution)/shard_map/ppermute | solution.py:297
  24.1 0.7 multiply_bitcast_fusion
  24.8 0.1 iota_add_fusion
  24.8 0.1 add.107
  24.9 2.3 gather_fusion
  27.3 0.7 select_maximum_fusion
  27.9 1.9 collective-permute-start.2
  29.9 0.7 convert_bitcast_fusion
  30.6 0.8 fusion
  31.4 0.7 convert_bitcast_fusion.1
  32.1 0.1 pad.10.clone
  32.2 0.1 maximum_maximum_fusion
  32.3 17.2 %collective-permute-start = (bf16[4,16,256]{2,1,0:T(8,128)(2,1)S(1)}, bf16[4,16,256]{2,1,0:T(8,128)(2,1)S(1)}, u32[]{:S(2)}, u32[]{:S(2)}) collective-permute-start(bf16[4,16,256]{2,1,0:T(8,128)(2,1)S(1)} %maximum_maximum_fusion), channel_id=1, source_target_pairs={{0,512},{4,576},{8,640},{12,704},{64,516},{68,580},{72,644},{76,70... | collective-permute-start | bytes 98312 | tf_op jit(solution)/shard_map/ppermute | solution.py:296
  49.4 4.3 %collective-permute-done.meta_ref = bf16[4,16,256]{2,1,0:T(8,128)(2,1)S(1)} collective-permute-done((bf16[4,16,256]{2,1,0:T(8,128)(2,1)S(1)}, bf16[4,16,256]{2,1,0:T(8,128)(2,1)S(1)}, u32[]{:S(2)}, u32[]{:S(2)}) %collective-permute-start) | collective-permute-done | bytes 32800 | tf_op jit(solution)/shard_map/ppermute | solution.py:296
  53.7 0.0 collective-permute-done.2
  53.7 0.0 collective-permute-done.1.feat_ref
  53.7 4.4 %shard_map.95 = (bf16[64,4,16,128]{3,2,1,0:T(8,128)(2,1)}, s32[4,1,512]{2,1,0:T(1,128)S(1)}) custom-call(bf16[4,16,256]{2,1,0:T(8,128)(2,1)S(1)} %collective-permute-done.meta_ref, bf16[4,256,128]{2,1,0:T(8,128)(2,1)S(1)} %collective-permute-done.1.feat_ref), custom_call_target="tpu_custom_call" | custom-call | tf_op jit(solution)/shard_map/pallas_call | solution.py:67
  58.1 22.4 %all-to-all-start = ((bf16[64,4,16,128]{3,2,1,0:T(8,128)(2,1)}), bf16[64,4,16,128]{3,2,1,0:T(8,128)(2,1)S(1)}, u32[]{:S(2)}, u32[]{:S(2)}) async-start(bf16[64,4,16,128]{3,2,1,0:T(8,128)(2,1)} %get-tuple-element.25), calls=%async_computation | async-start | bytes 2097152 | tf_op jit(solution)/shard_map/all_to_all | solution.py:306
  80.5 17.0 %all-to-all-done.got_ref.next_got_ref = bf16[64,4,16,128]{3,2,1,0:T(8,128)(2,1)S(1)} async-done(((bf16[64,4,16,128]{3,2,1,0:T(8,128)(2,1)}), bf16[64,4,16,128]{3,2,1,0:T(8,128)(2,1)S(1)}, u32[]{:S(2)}, u32[]{:S(2)}) %all-to-all-start) | async-done | bytes 1048608 | tf_op jit(solution)/shard_map/all_to_all | solution.py:306
  97.6 0.8 shard_map.96
  98.4 1.5 shard_map.97.mine_ref
  99.8 5.6 %all-to-all-start.1 = ((f32[64,8,128]{2,1,0:T(8,128)}), f32[64,8,128]{2,1,0:T(8,128)S(1)}, u32[]{:S(2)}, u32[]{:S(2)}) async-start(f32[64,8,128]{2,1,0:T(8,128)} %shard_map.97.mine_ref), calls=%async_computation.1 | async-start | bytes 524288 | tf_op jit(solution)/shard_map/all_to_all | solution.py:320
  105.4 0.8 shard_map.98
  106.2 8.7 %all-to-all-done.1.table_ref.refs_0_ = f32[64,8,128]{2,1,0:T(8,128)S(1)} async-done(((f32[64,8,128]{2,1,0:T(8,128)}), f32[64,8,128]{2,1,0:T(8,128)S(1)}, u32[]{:S(2)}, u32[]{:S(2)}) %all-to-all-start.1) | async-done | bytes 262176 | tf_op jit(solution)/shard_map/all_to_all | solution.py:320
  114.9 4.7 %shard_map.99 = (f32[256,128]{1,0:T(8,128)S(1)}, f32[64,8,128]{2,1,0:T(8,128)}) custom-call(f32[8,128]{1,0:T(8,128)S(1)} %slice.24.weights_ref, f32[256,128]{1,0:T(8,128)S(1)} %slice.25.rows_ref.initial_ref, f32[64,8,128]{2,1,0:T(8,128)S(1)} %all-to-all-done.1.table_ref.refs_0_, f32[64,8,128]{2,1,0:T(8,128)} %shard_map.97.mine_ref, ...), custom_call_target="tpu_custom_call" | custom-call | tf_op jit(solution)/shard_map/pallas_call | solution.py:232
  119.6 0.0 copy-start.9
  119.6 0.7 copy-done.9
  120.3 5.0 %all-to-all-start.2 = ((f32[64,8,128]{2,1,0:T(8,128)}), f32[64,8,128]{2,1,0:T(8,128)S(1)}, u32[]{:S(2)}, u32[]{:S(2)}) async-start(f32[64,8,128]{2,1,0:T(8,128)} %get-tuple-element.29.mine_ref), calls=%async_computation.2 | async-start | bytes 524288 | tf_op jit(solution)/shard_map/all_to_all | solution.py:320
  125.3 0.8 shard_map.100
  126.1 8.7 %all-to-all-done.2.table_ref.refs_1_ = f32[64,8,128]{2,1,0:T(8,128)S(1)} async-done(((f32[64,8,128]{2,1,0:T(8,128)}), f32[64,8,128]{2,1,0:T(8,128)S(1)}, u32[]{:S(2)}, u32[]{:S(2)}) %all-to-all-start.2) | async-done | bytes 262176 | tf_op jit(solution)/shard_map/all_to_all | solution.py:320
  134.8 0.0 copy-start.10
  134.8 0.9 copy-done.10
  135.7 4.7 %shard_map.101 = (f32[256,128]{1,0:T(8,128)S(1)}, f32[64,8,128]{2,1,0:T(8,128)}) custom-call(f32[8,128]{1,0:T(8,128)S(1)} %slice.24.weights_ref, f32[256,128]{1,0:T(8,128)S(1)} %copy-done.10, f32[64,8,128]{2,1,0:T(8,128)S(1)} %all-to-all-done.2.table_ref.refs_1_, f32[64,8,128]{2,1,0:T(8,128)} %get-tuple-element.29.mine_ref, ...), custom_call_target="tpu_custom_call" | custom-call | tf_op jit(solution)/shard_map/pallas_call | solution.py:232
  140.4 0.0 copy-start.7
  140.4 0.6 copy-done.7
  141.1 5.0 %all-to-all-start.3 = ((f32[64,8,128]{2,1,0:T(8,128)}), f32[64,8,128]{2,1,0:T(8,128)S(1)}, u32[]{:S(2)}, u32[]{:S(2)}) async-start(f32[64,8,128]{2,1,0:T(8,128)} %get-tuple-element.33.mine_ref), calls=%async_computation.3 | async-start | bytes 524288 | tf_op jit(solution)/shard_map/all_to_all | solution.py:320
  146.1 0.8 shard_map.103
  146.9 0.0 copy-start.1
  146.9 0.0 copy-start.3
  146.9 8.7 %all-to-all-done.3.refs_2_.table_ref = f32[64,8,128]{2,1,0:T(8,128)S(1)} async-done(((f32[64,8,128]{2,1,0:T(8,128)}), f32[64,8,128]{2,1,0:T(8,128)S(1)}, u32[]{:S(2)}, u32[]{:S(2)}) %all-to-all-start.3) | async-done | bytes 262176 | tf_op jit(solution)/shard_map/all_to_all | solution.py:320
  155.6 0.0 copy-start.8
  155.6 0.9 copy-done.8
  156.5 4.7 %shard_map.104 = (f32[256,128]{1,0:T(8,128)S(1)}, f32[64,8,128]{2,1,0:T(8,128)}) custom-call(f32[8,128]{1,0:T(8,128)S(1)} %slice.24.weights_ref, f32[256,128]{1,0:T(8,128)S(1)} %copy-done.8, f32[64,8,128]{2,1,0:T(8,128)S(1)} %all-to-all-done.3.refs_2_.table_ref, f32[64,8,128]{2,1,0:T(8,128)} %get-tuple-element.33.mine_ref, ...), custom_call_target="tpu_custom_call" | custom-call | tf_op jit(solution)/shard_map/pallas_call | solution.py:232
  161.2 0.0 copy-start.5
  161.2 0.6 copy-done.5
  161.9 0.0 copy-done.1
  161.9 0.0 copy-done.3
  161.9 5.0 %all-to-all-start.4 = ((f32[64,8,128]{2,1,0:T(8,128)}), f32[64,8,128]{2,1,0:T(8,128)S(1)}, u32[]{:S(2)}, u32[]{:S(2)}) async-start(f32[64,8,128]{2,1,0:T(8,128)} %get-tuple-element.38.mine_ref), calls=%async_computation.4 | async-start | bytes 524288 | tf_op jit(solution)/shard_map/all_to_all | solution.py:320
  166.9 1.3 shard_map.102.early_ref
  168.2 8.2 %all-to-all-done.4.table_ref = f32[64,8,128]{2,1,0:T(8,128)S(1)} async-done(((f32[64,8,128]{2,1,0:T(8,128)}), f32[64,8,128]{2,1,0:T(8,128)S(1)}, u32[]{:S(2)}, u32[]{:S(2)}) %all-to-all-start.4) | async-done | bytes 262176 | tf_op jit(solution)/shard_map/all_to_all | solution.py:320
  176.4 1.0 copy-done.2
  177.5 0.9 copy-done.4
  178.4 0.9 copy-done.6
  179.3 4.1 %shard_map.105 = bf16[288,128]{1,0:T(8,128)(2,1)S(1)} custom-call(s32[1]{0:T(128)} %bitcast.2.me_ref, s32[4,1,512]{2,1,0:T(1,128)S(1)} %get-tuple-element.23.slot_ref, f32[8,128]{1,0:T(8,128)S(1)} %shard_map.102.early_ref, f32[8,128]{1,0:T(8,128)S(1)} %slice.24.weights_ref, f32[256,128]{1,0:T(8,128)S(1)} %copy-done.6, ...), custom_call_target="tpu_custom_call" | custom-call | tf_op jit(solution)/shard_map/pallas_call | solution.py:232
  183.5 1.9 collective-permute-start.3
  185.4 19.6 %collective-permute-done.3 = bf16[288,128]{1,0:T(8,128)(2,1)S(1)} collective-permute-done((bf16[288,128]{1,0:T(8,128)(2,1)S(1)}, bf16[288,128]{1,0:T(8,128)(2,1)S(1)}, u32[]{:S(2)}, u32[]{:S(2)}) %collective-permute-start.3) | collective-permute-done | bytes 73760 | tf_op jit(solution)/shard_map/ppermute | solution.py:339
  205.0 0.1 broadcast_in_dim.20
  205.1 25.9 %all_to_all.30.mine_ref = bf16[8,256,128]{2,1,0:T(8,128)(2,1)S(1)} all-to-all(bf16[8,256,128]{2,1,0:T(8,128)(2,1)S(1)} %broadcast_in_dim.20), channel_id=1, replica_groups=mesh['a'=4,'b'=2,'c'=2,'x'=4,'h'=4,'y'=4] {'a','b'}, dimensions={0} | all-to-all | bytes 1048576 | tf_op jit(solution)/shard_map/all_to_all | solution.py:341
  230.9 9.1 %collective-permute-start.4 = (bf16[8,256,128]{2,1,0:T(8,128)(2,1)S(1)}, bf16[8,256,128]{2,1,0:T(8,128)(2,1)S(1)}, u32[]{:S(2)}, u32[]{:S(2)}) collective-permute-start(bf16[8,256,128]{2,1,0:T(8,128)(2,1)S(1)} %all_to_all.30.mine_ref), channel_id=1, source_target_pairs={{0,64},{64,0},{1,65},{65,1},{2,66},{66,2},{3,67},{67,3},{4,68},{68... | collective-permute-start | bytes 1572872 | tf_op jit(solution)/shard_map/ppermute | solution.py:342
  240.1 0.6 add.112
  240.7 0.9 collective-permute-done.4.other_ref
  241.6 0.0 copy-done
  241.6 0.7 copy-done.11
  242.3 3.8 %shard_map.106 = f32[4096,128]{1,0:T(8,128)} custom-call(s32[16,16]{1,0:T(8,128)S(1)} %bitcast.18, s32[1]{0:T(128)} %bitcast.1.core_ref, f32[4096,128]{1,0:T(8,128)S(1)} %copy-done, bf16[8,256,128]{2,1,0:T(8,128)(2,1)S(1)} %all_to_all.30.mine_ref, bf16[8,256,128]{2,1,0:T(8,128)(2,1)S(1)} %collective-permute-done.4.other_ref), custom_call_target="tpu_custom_call" | custom-call | tf_op jit(solution)/shard_map/pallas_call | solution.py:267
  (15 shorter events, 0.1 us)
Async XLA Ops:
  0.6 53.0 %collective-permute-start.1 = (bf16[4,256,128]{2,1,0:T(8,128)(2,1)}, bf16[4,256,128]{2,1,0:T(8,128)(2,1)S(1)}, u32[]{:S(2)}, u32[]{:S(2)}) collective-permute-start(bf16[4,256,128]{2,1,0:T(8,128)(2,1)} %bitcast.21), channel_id=1, source_target_pairs={{0,512},{4,576},{8,640},{12,704},{64,516},{68,580},{72,644},{76,70... | collective-permute-start | bytes 786440 | tf_op jit(solution)/shard_map/ppermute | solution.py:297
  27.9 25.7 %collective-permute-start.2 = (f32[264,128]{1,0:T(8,128)S(1)}, f32[264,128]{1,0:T(8,128)S(1)}, u32[]{:S(2)}, u32[]{:S(2)}) collective-permute-start(f32[264,128]{1,0:T(8,128)S(1)} %select_maximum_fusion), channel_id=1, source_target_pairs={{0,512},{4,576},{8,640},{12,704},{64,516},{68,580},{72,644},{76,70... | collective-permute-start | bytes 405512 | tf_op jit(solution)/shard_map/ppermute | solution.py:301
  32.3 21.4 %collective-permute-start = (bf16[4,16,256]{2,1,0:T(8,128)(2,1)S(1)}, bf16[4,16,256]{2,1,0:T(8,128)(2,1)S(1)}, u32[]{:S(2)}, u32[]{:S(2)}) collective-permute-start(bf16[4,16,256]{2,1,0:T(8,128)(2,1)S(1)} %maximum_maximum_fusion), channel_id=1, source_target_pairs={{0,512},{4,576},{8,640},{12,704},{64,516},{68,580},{72,644},{76,70... | collective-permute-start | bytes 98312 | tf_op jit(solution)/shard_map/ppermute | solution.py:296
  58.1 39.5 %all-to-all-start = ((bf16[64,4,16,128]{3,2,1,0:T(8,128)(2,1)}), bf16[64,4,16,128]{3,2,1,0:T(8,128)(2,1)S(1)}, u32[]{:S(2)}, u32[]{:S(2)}) async-start(bf16[64,4,16,128]{3,2,1,0:T(8,128)(2,1)} %get-tuple-element.25), calls=%async_computation | async-start | bytes 2097152 | tf_op jit(solution)/shard_map/all_to_all | solution.py:306
  99.8 15.1 %all-to-all-start.1 = ((f32[64,8,128]{2,1,0:T(8,128)}), f32[64,8,128]{2,1,0:T(8,128)S(1)}, u32[]{:S(2)}, u32[]{:S(2)}) async-start(f32[64,8,128]{2,1,0:T(8,128)} %shard_map.97.mine_ref), calls=%async_computation.1 | async-start | bytes 524288 | tf_op jit(solution)/shard_map/all_to_all | solution.py:320
  119.6 0.7 copy-start.9
  120.3 14.6 %all-to-all-start.2 = ((f32[64,8,128]{2,1,0:T(8,128)}), f32[64,8,128]{2,1,0:T(8,128)S(1)}, u32[]{:S(2)}, u32[]{:S(2)}) async-start(f32[64,8,128]{2,1,0:T(8,128)} %get-tuple-element.29.mine_ref), calls=%async_computation.2 | async-start | bytes 524288 | tf_op jit(solution)/shard_map/all_to_all | solution.py:320
  134.8 0.9 copy-start.10
  140.4 0.6 copy-start.7
  141.1 14.6 %all-to-all-start.3 = ((f32[64,8,128]{2,1,0:T(8,128)}), f32[64,8,128]{2,1,0:T(8,128)S(1)}, u32[]{:S(2)}, u32[]{:S(2)}) async-start(f32[64,8,128]{2,1,0:T(8,128)} %get-tuple-element.33.mine_ref), calls=%async_computation.3 | async-start | bytes 524288 | tf_op jit(solution)/shard_map/all_to_all | solution.py:320
  146.9 15.0 %copy-start.1 = (bf16[1024,256]{1,0:T(8,128)(2,1)}, bf16[1024,256]{1,0:T(8,128)(2,1)S(1)}, u32[]{:S(2)}) copy-start(bf16[1024,256]{1,0:T(8,128)(2,1)S(1)} %get-tuple-element.36.next_counts_ref.counts_ref) | copy-start | bytes 1572868
  146.9 15.0 %copy-start.3 = (bf16[1024,128]{1,0:T(8,128)(2,1)}, bf16[1024,128]{1,0:T(8,128)(2,1)S(1)}, u32[]{:S(2)}) copy-start(bf16[1024,128]{1,0:T(8,128)(2,1)S(1)} %get-tuple-element.39.cols_ref) | copy-start | bytes 786436
  155.6 0.9 copy-start.8
  161.2 0.6 copy-start.5
  161.9 14.6 %all-to-all-start.4 = ((f32[64,8,128]{2,1,0:T(8,128)}), f32[64,8,128]{2,1,0:T(8,128)S(1)}, u32[]{:S(2)}, u32[]{:S(2)}) async-start(f32[64,8,128]{2,1,0:T(8,128)} %get-tuple-element.38.mine_ref), calls=%async_computation.4 | async-start | bytes 524288 | tf_op jit(solution)/shard_map/all_to_all | solution.py:320
  176.4 1.0 copy-start.2
  177.5 0.9 copy-start.4
  178.4 0.9 copy-start.6
  179.3 62.2 %copy-start = (f32[4096,128]{1,0:T(8,128)S(1)}, f32[4096,128]{1,0:T(8,128)}, u32[]{:S(2)}) copy-start(f32[4096,128]{1,0:T(8,128)} %table_ref.1) | copy-start | bytes 6291460
  183.5 21.5 %collective-permute-start.3 = (bf16[288,128]{1,0:T(8,128)(2,1)S(1)}, bf16[288,128]{1,0:T(8,128)(2,1)S(1)}, u32[]{:S(2)}, u32[]{:S(2)}) collective-permute-start(bf16[288,128]{1,0:T(8,128)(2,1)S(1)} %shard_map.105), channel_id=1, source_target_pairs={{0,512},{4,576},{8,640},{12,704},{64,516},{68,580},{72,644},{76,70... | collective-permute-start | bytes 221192 | tf_op jit(solution)/shard_map/ppermute | solution.py:339
  230.9 10.6 %collective-permute-start.4 = (bf16[8,256,128]{2,1,0:T(8,128)(2,1)S(1)}, bf16[8,256,128]{2,1,0:T(8,128)(2,1)S(1)}, u32[]{:S(2)}, u32[]{:S(2)}) collective-permute-start(bf16[8,256,128]{2,1,0:T(8,128)(2,1)S(1)} %all_to_all.30.mine_ref), channel_id=1, source_target_pairs={{0,64},{64,0},{1,65},{65,1},{2,66},{66,2},{3,67},{67,3},{4,68},{68... | collective-permute-start | bytes 1572872 | tf_op jit(solution)/shard_map/ppermute | solution.py:342
  241.6 0.7 copy-start.11

commit v3 on v2

v3 whole, which is shorter than its diff:
```python
import functools

import jax
import jax.numpy as jnp
from jax import lax
from jax.experimental import pallas as pl
from jax.experimental.pallas import tpu as pltpu
from jax.sharding import Mesh
from jax.sharding import PartitionSpec as P

BLK = 16
STRIDE = 16
META = 12
VMEM_LIMIT = 16 << 20
MERGE_LIMIT = 60 << 20
step_rate = 1.0

GROUP = ("x", "b", "c", "y")
HOME = ("a", "b", "c", "h")


def split3(v):
    hi = v.astype(jnp.bfloat16)
    rest = v - hi.astype(jnp.float32)
    mid = rest.astype(jnp.bfloat16)
    return hi, mid, (rest - mid.astype(jnp.float32)).astype(jnp.bfloat16)


def wide(v):
    hi = v.astype(jnp.bfloat16)
    return jnp.concatenate([hi, (v - hi.astype(jnp.float32)).astype(jnp.bfloat16)], axis=1)


def halves(v):
    return v[:, : v.shape[1] // 2] + v[:, v.shape[1] // 2 :]


def dot(lhs, rhs, contract=((1,), (0,))):
    return lax.dot_general(lhs, rhs, (contract, ((), ())), preferred_element_type=jnp.float32)


def iota(shape, axis):
    return lax.broadcasted_iota(jnp.int32, shape, axis)


def pack_kernel(shards, meta_ref, feat_ref, out_ref, slot_ref):
    meta = meta_ref[0].astype(jnp.float32)
    samples = meta.shape[1]
    hits = 2 * samples

    def pair(first, second):
        return jnp.concatenate([meta[first : first + 1], meta[second : second + 1]], axis=1)

    target = pair(0, 1).astype(jnp.int32)
    chosen = iota((shards, hits), 0) == target
    onehot = chosen.astype(jnp.float32).astype(jnp.bfloat16)
    before = (iota((hits, hits), 0) < iota((hits, hits), 1)).astype(jnp.float32).astype(jnp.bfloat16)
    rank = jnp.sum(jnp.where(chosen, dot(onehot, before), 0.0), axis=0, keepdims=True)
    rank_i = rank.astype(jnp.int32)
    slot = target * STRIDE + rank_i
    at = iota((shards * STRIDE, samples), 0)
    place = jnp.where((at == slot[:, :samples]) | (at == slot[:, samples:]), 1.0, 0.0).astype(jnp.bfloat16)
    packed = dot(place, feat_ref[0])
    other = jnp.concatenate([rank[:, samples:], rank[:, :samples]], axis=1)
    values = [pair(2 + n, 6 + n) for n in range(4)] + [pair(1, 0), other, pair(10, 10), jnp.ones_like(rank)]
    lane_of = iota((STRIDE, hits), 0) == rank_i
    spread = jnp.concatenate([jnp.where(lane_of, value, 0.0) for value in values], axis=0)
    rows = dot(onehot, spread.astype(jnp.bfloat16), ((1,), (1,)))
    at_row = iota((shards * STRIDE, shards), 0) == iota((shards * STRIDE, shards), 1) * STRIDE + META
    packed = packed + dot(at_row.astype(jnp.float32).astype(jnp.bfloat16), rows.astype(jnp.bfloat16))
    out_ref[...] = packed.astype(jnp.bfloat16).reshape(out_ref.shape)
    slot_ref[0] = slot


def pack(meta, feats, shards):
    steps, samples, width = feats.shape
    return pl.pallas_call(
        functools.partial(pack_kernel, shards),
        grid=(steps,),
        in_specs=[
            pl.BlockSpec((1, 16, samples), lambda t: (t, 0, 0)),
            pl.BlockSpec((1, samples, width), lambda t: (t, 0, 0)),
        ],
        out_specs=[
            pl.BlockSpec((shards, 1, STRIDE, width), lambda t: (0, t, 0, 0)),
            pl.BlockSpec((1, 1, 2 * samples), lambda t: (t, 0, 0)),
        ],
        out_shape=[
            jax.ShapeDtypeStruct((shards, steps, STRIDE, width), jnp.bfloat16),
            jax.ShapeDtypeStruct((steps, 1, 2 * samples), jnp.int32),
        ],
        compiler_params=pltpu.CompilerParams(vmem_limit_bytes=VMEM_LIMIT),
    )(meta, feats)


def columns(got_ref, step_no):
    tiles = got_ref[:, step_no].astype(jnp.float32)
    width = tiles.shape[2]
    meta = jnp.broadcast_to(tiles[:, META : META + 1, :], tiles.shape).reshape(-1, width)
    own = iota(meta.shape, 1) % STRIDE == iota(meta.shape, 0) % STRIDE
    fold = iota((width, width), 0) // STRIDE == iota((width, width), 1)
    return dot(
        jnp.where(own, meta, 0.0).astype(jnp.bfloat16),
        fold.astype(jnp.float32).astype(jnp.bfloat16),
    )


def lookups(cols, act_rows):
    row_no = (iota((cols.shape[0], act_rows), 1) + 1).astype(jnp.float32)
    return sum(jnp.where(row_no == cols[:, n : n + 1], 1.0, 0.0) for n in range(4))


def own_logits(me, table_ref, slot):
    shards, blocks, _ = table_ref.shape
    hits = slot.shape[1]
    part = sum(jnp.where(me // (128 // STRIDE) == k, table_ref[:, k, :], 0.0) for k in range(blocks))
    onehot = iota((shards, hits), 0) == slot // STRIDE
    onehot = onehot.astype(jnp.float32).astype(jnp.bfloat16)
    found = dot(wide(part), onehot, ((0,), (0,)))
    found = found[:128] + found[128:]
    at = (me % (128 // STRIDE)) * STRIDE + slot % STRIDE
    picked = jnp.sum(jnp.where(iota((128, hits), 0) == at, found, 0.0), axis=0, keepdims=True)
    logits = picked[:, : hits // 2] + picked[:, hits // 2 :]
    return jnp.concatenate([logits[:, n : n + 128] for n in range(0, hits // 2, 128)], axis=0)


def prep_kernel(step_no, steps, me_ref, slot_ref, got_ref, *refs):
    if step_no:
        old_table_ref, *refs = refs
        *refs, logits_ref = refs
        logits_ref[...] = own_logits(me_ref[0], old_table_ref, slot_ref[step_no - 1])
    turned_ref, cols_ref, *next_counts_ref = refs
    act_rows = turned_ref.shape[0]
    cols = columns(got_ref, step_no)
    cols_ref[...] = cols.astype(jnp.bfloat16)
    turned_ref[...] = lookups(cols, act_rows).T.astype(jnp.bfloat16)
    if next_counts_ref:
        next_cols = columns(got_ref, step_no + 1)
        next_counts_ref[0][...] = lookups(next_cols, act_rows).astype(jnp.bfloat16)


def prep(me, slot_of, got, old_table, step_no, act_rows):
    shards, steps, _, width = got.shape
    slots = shards * STRIDE
    outs = [
        jax.ShapeDtypeStruct((act_rows, slots), jnp.bfloat16),
        jax.ShapeDtypeStruct((slots, width), jnp.bfloat16),
    ]
    if step_no + 1 < steps:
        outs.append(jax.ShapeDtypeStruct((slots, act_rows), jnp.bfloat16))
    if step_no:
        outs.append(jax.ShapeDtypeStruct((slot_of.shape[2] // 256, 128), jnp.float32))
    args = [me, slot_of, got] + ([old_table] if step_no else [])
    return call(functools.partial(prep_kernel, step_no, steps), args, outs)


def weight_column(weights_ref, step_no, act_rows):
    row = weights_ref[step_no : step_no + 1, :]
    shape = (act_rows, row.shape[1])
    here = iota(shape, 1) == iota(shape, 0) // BLK
    return jnp.sum(jnp.where(here, row, 0.0), axis=1, keepdims=True)


def forward(weighted, counts, feats, mine_ref):
    width = weighted.shape[1]
    products = halves(dot(counts, wide(weighted))) * feats.astype(jnp.float32)
    same = iota((128, 128), 0) == iota((128, 128), 1)
    mine = []
    for k in range(mine_ref.shape[1]):
        column = jnp.sum(products[k * 128 : (k + 1) * 128], axis=1, keepdims=True) * width**-0.5
        mine.append(jnp.sum(jnp.where(same, column, 0.0), axis=0, keepdims=True))
    mine = jnp.concatenate(mine, axis=0)
    mine_ref[...] = jnp.broadcast_to(mine[None], mine_ref.shape)


def first_kernel(weights_ref, rows_ref, got_ref, mine_ref):
    act_rows, width = rows_ref.shape
    counts = lookups(columns(got_ref, 0), act_rows).astype(jnp.bfloat16)
    weighted = weight_column(weights_ref, 0, act_rows) * rows_ref[...]
    forward(weighted, counts, got_ref[:, 0].reshape(-1, width), mine_ref)


def gradient(step_no, table_ref, mine_ref, cols_ref, got_ref, turned_ref, grad_ref):
    shards, blocks, _ = table_ref.shape
    width = got_ref.shape[3]
    feats = got_ref[:, step_no].reshape(-1, width)
    row, lane = iota((128, 128), 0), iota((128, 128), 1)
    base = (row // STRIDE) * STRIDE
    shard = iota((128, shards), 1).astype(jnp.float32)
    for k in range(blocks):
        cols = cols_ref[k * 128 : (k + 1) * 128, :].astype(jnp.float32)
        wanted = (shard == cols[:, 4:5]).astype(jnp.float32).astype(jnp.bfloat16)
        found = halves(dot(wanted, wide(table_ref[:, k, :])))
        partner = jnp.where(lane == base + cols[:, 5:6].astype(jnp.int32), found, 0.0)
        own = jnp.where(lane == row, mine_ref[0, k : k + 1, :], 0.0)
        error = jax.nn.sigmoid(jnp.sum(partner + own, axis=1, keepdims=True)) - cols[:, 6:7]
        part = error * feats[k * 128 : (k + 1) * 128].astype(jnp.float32) * width**-0.5
        grad_ref[k * 128 : (k + 1) * 128, :] = part.astype(jnp.bfloat16)
    return dot(turned_ref[...], grad_ref[...])


def step_kernel(
    step_no, weights_ref, rows_ref, table_ref, mine_ref, cols_ref, got_ref, turned_ref, next_counts_ref,
    new_rows_ref, new_mine_ref, grad_ref,
):
    act_rows, width = rows_ref.shape
    row_grad = gradient(step_no, table_ref, mine_ref, cols_ref, got_ref, turned_ref, grad_ref)
    rows = rows_ref[...] - step_rate * (weight_column(weights_ref, step_no, act_rows) * row_grad)
    new_rows_ref[...] = rows
    weighted = weight_column(weights_ref, step_no + 1, act_rows) * rows
    forward(weighted, next_counts_ref[...], got_ref[:, step_no + 1].reshape(-1, width), new_mine_ref)


def last_kernel(
    step_no, me_ref, slot_ref, weights_ref, rows_ref, initial_ref, table_ref, mine_ref, cols_ref, got_ref, turned_ref,
    *refs,
):
    *known_refs, back_ref, grad_ref = refs
    act_rows = rows_ref.shape[0]
    row_grad = gradient(step_no, table_ref, mine_ref, cols_ref, got_ref, turned_ref, grad_ref)
    rows = rows_ref[...] - step_rate * (weight_column(weights_ref, step_no, act_rows) * row_grad)
    back_ref[:act_rows, :] = (rows - initial_ref[...]).astype(jnp.bfloat16)
    logits = own_logits(me_ref[0], table_ref, slot_ref[step_no])
    logits = jnp.concatenate([ref[...] for ref in known_refs] + [logits], axis=0)
    terms = [term.astype(jnp.float32) for term in split3(logits)]
    back_ref[act_rows:, :] = jnp.concatenate(terms + [jnp.zeros_like(logits)], axis=0).astype(jnp.bfloat16)


def call(kernel, args, outs, scratch=()):
    smem, vmem = (pl.BlockSpec(memory_space=space) for space in (pltpu.SMEM, pltpu.VMEM))
    return pl.pallas_call(
        kernel,
        in_specs=[smem if arg.size == 1 else vmem for arg in args],
        out_specs=[vmem] * len(outs),
        out_shape=list(outs),
        scratch_shapes=list(scratch),
        compiler_params=pltpu.CompilerParams(vmem_limit_bytes=VMEM_LIMIT),
    )(*args)


def merge_kernel(blocks_ref, core_ref, table_ref, mine_ref, other_ref, out_ref, sem):
    places, act_rows, _ = mine_ref.shape
    active = act_rows // BLK
    groups = 2 * places
    low = core_ref[0] == 0
    copy = pltpu.make_async_copy(table_ref, out_ref, sem)
    copy.start()
    copy.wait()

    def one(place, carry):
        for c in range(2):
            spots, values = [], []
            for slot in range(active):
                at = pl.ds(slot * BLK, BLK)
                mine, other = mine_ref[place, at, :], other_ref[place, at, :]
                value = jnp.where(low, mine, other) if c == 0 else jnp.where(low, other, mine)
                spot = pl.ds(pl.multiple_of(blocks_ref[2 * place + c, slot] * BLK, BLK), BLK)
                spots.append(spot)
                values.append(out_ref[spot, :] + value.astype(jnp.float32) * (1.0 / groups))
            for spot, value in zip(spots, values):
                out_ref[spot, :] = value
        return carry

    lax.fori_loop(0, places, one, 0)


def merge(blocks, core, table, mine, other):
    smem, hbm = (pl.BlockSpec(memory_space=space) for space in (pltpu.SMEM, pltpu.HBM))
    whole = pl.BlockSpec(mine.shape, lambda i: (0, 0, 0))
    return pl.pallas_call(
        merge_kernel,
        grid=(1,),
        in_specs=[smem, smem, hbm, whole, whole],
        out_specs=pl.BlockSpec(table.shape, lambda i: (0, 0)),
        out_shape=jax.ShapeDtypeStruct(table.shape, jnp.float32),
        scratch_shapes=[pltpu.SemaphoreType.DMA],
        compiler_params=pltpu.CompilerParams(vmem_limit_bytes=MERGE_LIMIT),
    )(blocks, core, table, mine, other)


def body(turn, sizes, emb_table, active_blocks, hit_shards, lookup_slot, lookup_offset, block_weight, dense_feat, labels):
    shards = sizes["x"] * sizes["h"] * sizes["y"]
    _, steps, samples, _ = hit_shards.shape
    width = emb_table.shape[1]
    active = active_blocks.shape[2]
    act_rows = active * BLK
    slots = shards * STRIDE
    within = jnp.arange(BLK, dtype=jnp.int32)

    there = functools.partial(lax.ppermute, axis_name=HOME, perm=turn)
    looked = (lookup_slot[0] * BLK + lookup_offset[0] + 1).transpose(0, 2, 3, 1).reshape(steps, 8, samples)
    meta = jnp.concatenate(
        [
            hit_shards[0].transpose(0, 2, 1),
            looked,
            labels[0][:, None, :],
            jnp.zeros((steps, 5, samples), jnp.int32),
        ],
        axis=1,
    ).astype(jnp.bfloat16)
    meta = there(meta)
    feats = there(dense_feat[0])
    my_blocks = active_blocks[lax.axis_index(("a", "b", "c")), 0]
    local_index = (my_blocks[:, None] * BLK + within[None, :]).reshape(-1)
    weights = jnp.pad(block_weight[0, :, 0], ((0, 8 - steps), (0, width - active)))
    carried = there(jnp.concatenate([emb_table[local_index], weights], axis=0))
    meta, feats, carried = lax.optimization_barrier((meta, feats, carried))
    initial, weights = carried[:act_rows], carried[act_rows:]

    packed, slot_of = pack(meta, feats, shards)
    got = lax.all_to_all(packed, GROUP, 0, 0, tiled=True)

    logit_rows = steps * samples // 128
    rows_like = jax.ShapeDtypeStruct((act_rows, width), jnp.float32)
    mine_like = jax.ShapeDtypeStruct((shards, slots // 128, 128), jnp.float32)
    back_like = jax.ShapeDtypeStruct((act_rows + 4 * logit_rows, width), jnp.bfloat16)
    scratch = [pltpu.VMEM((slots, width), jnp.bfloat16)]
    me = lax.axis_index(GROUP)[None]
    rows = initial
    (mine,) = call(first_kernel, [weights, rows, got], [mine_like])
    table, known = None, []
    for t in range(steps):
        turned, cols, *more = prep(me, slot_of, got, table, t, act_rows)
        known += more[1:] if t + 1 < steps else more
        table = lax.all_to_all(mine, GROUP, 0, 0, tiled=True)
        if t + 1 < steps:
            rows, mine = call(
                functools.partial(step_kernel, t),
                [weights, rows, table, mine, cols, got, turned, more[0]],
                [rows_like, mine_like],
                scratch,
            )
        else:
            (back,) = call(
                functools.partial(last_kernel, t),
                [me, slot_of, weights, rows, initial, table, mine, cols, got, turned, *known],
                [back_like],
                scratch,
            )

    back = there(back)
    delta, terms = back[:act_rows], back[act_rows:].astype(jnp.float32).reshape(4, logit_rows, 128)
    mine = lax.all_to_all(jnp.broadcast_to(delta[None], (sizes["a"] * 2,) + delta.shape), ("a", "b"), 0, 0, tiled=True)
    other = lax.ppermute(mine, "c", [(0, 1), (1, 0)])
    new_table = merge(active_blocks[:, 0], lax.axis_index("c")[None], emb_table, mine, other)
    logits = (terms[0] + terms[1] + terms[2]).reshape(steps, samples)
    return new_table, logits[None]


def solution(mesh):
    shards = mesh.shape["shard"]
    y = min(4, shards // 4)
    sizes = {"a": mesh.shape["replica"] // 4, "b": 2, "c": 2, "x": shards // 4 // y, "h": 4, "y": y}
    finer = Mesh(mesh.devices.reshape(tuple(sizes.values())), tuple(sizes))
    index = lambda a, b, c, h: ((a * 2 + b) * 2 + c) * 4 + h
    turn = [
        (index(a, b, c, h), index((a + sizes["a"] // 2) % sizes["a"], h // 2, h % 2, b * 2 + c))
        for a in range(sizes["a"])
        for b in range(2)
        for c in range(2)
        for h in range(4)
    ]
    group, shard = ("a", "b", "c"), ("x", "h", "y")
    placed = (
        P(shard, None),
        P(None, shard, None),
        P(group, None, shard, None),
        P(group, None, shard, None, None),
        P(group, None, shard, None, None),
        P(group, None, shard, None),
        P(group, None, shard, None),
        P(group, None, shard),
    )
    return jax.shard_map(
        functools.partial(body, turn, sizes),
        mesh=finer,
        in_specs=placed,
        out_specs=(P(shard, None), P(group, None, shard)),
        check_vma=False,
    )
```

time: 247 us -> 236 us (0.955)
  local copies, waits for them, and re-layouts: 10.5 us -> 3.99 us
  waiting for transfers between devices: 76.2 us -> 73.1 us
    unnamed x24 -> x4, local copies, waits for them, and re-layouts: 7.36 us -> 0.81 us
    all_to_all x4, waiting for transfers between devices: 34.4 us -> 31.3 us  [body(): table = lax.all_to_all(mine, GROUP, 0, 0, tiled=True)]
    pallas_call x11 -> x10, Pallas kernels: 27.9 us -> 27.3 us  [the longest x9 22.7 us: call(): pl.pallas_call(kernel, in_specs=[smem if arg.size == 1 else vmem for arg...]
  transfers between devices with their start and end apart: 10 -> 10, of which waited for: 8 -> 8; matrix products, arithmetic and copies ran while one was open for 3% -> 3% of each run, Pallas kernels for 1% -> 3%
where the time goes in v3:
time: 236 us; the launch traced here: 235 us
  starting transfers between devices  96.9 us (41%)
  waiting for transfers between devices  73.1 us (31%)
  Pallas kernels  31.1 us (13%)
  blocking collectives  25.6 us (11%)
  local copies, waits for them, and re-layouts  3.99 us (2%)
  other arithmetic  3.72 us (2%)
    all_to_all x4, waiting for transfers between devices, body(): table = lax.all_to_all(mine, GROUP, 0, 0, tiled=True)  31.3 us
    all_to_all x1, blocking collectives, body(): lax.all_to_all(jnp.broadcast_to(delta[None], (sizes['a'] * 2,) + delta.sh...  25.6 us
    ppermute x1, starting transfers between devices, body(): feats = there(dense_feat[0])  23.5 us
    pallas_call x9, Pallas kernels, call(): pl.pallas_call(kernel, in_specs=[smem if arg.size == 1 else vmem for arg...  22.7 us
    all_to_all x1, starting transfers between devices, body(): got = lax.all_to_all(packed, GROUP, 0, 0, tiled=True)  22.4 us
    all_to_all x4, starting transfers between devices, body(): table = lax.all_to_all(mine, GROUP, 0, 0, tiled=True)  20.6 us
    ppermute x1, waiting for transfers between devices, body(): back = there(back)  19.6 us
    ppermute x1, starting transfers between devices, body(): meta = there(meta)  17.2 us
  transfers between devices with their start and end apart: 10, of which 8 were waited for; matrix products, arithmetic and copies ran while one was open for 3% of the time, Pallas kernels for 3%

profile of v3, /device:TPU:1, one launch (start us, length us, event | category | flops | bytes accessed | tf_op | source)
XLA Modules:
  0.0 235.4 jit_solution(15918011918602347897)
XLA Ops:
  0.6 23.5 %collective-permute-start.1 = (bf16[4,256,128]{2,1,0:T(8,128)(2,1)}, bf16[4,256,128]{2,1,0:T(8,128)(2,1)S(1)}, u32[]{:S(2)}, u32[]{:S(2)}) collective-permute-start(bf16[4,256,128]{2,1,0:T(8,128)(2,1)} %bitcast.21), channel_id=1, source_target_pairs={{0,512},{4,576},{8,640},{12,704},{64,516},{68,580},{72,644},{76,70... | collective-permute-start | bytes 786440 | tf_op jit(solution)/shard_map/ppermute | solution.py:302
  24.1 0.7 multiply_bitcast_fusion
  24.8 0.1 iota_add_fusion
  24.8 0.1 add.107
  24.9 2.3 gather_fusion
  27.3 0.7 select_maximum_fusion
  27.9 1.9 collective-permute-start.2
  29.9 0.7 convert_bitcast_fusion
  30.6 0.8 fusion
  31.4 0.7 convert_bitcast_fusion.1
  32.1 0.1 pad.10.clone
  32.2 0.1 maximum_maximum_fusion
  32.3 17.2 %collective-permute-start = (bf16[4,16,256]{2,1,0:T(8,128)(2,1)S(1)}, bf16[4,16,256]{2,1,0:T(8,128)(2,1)S(1)}, u32[]{:S(2)}, u32[]{:S(2)}) collective-permute-start(bf16[4,16,256]{2,1,0:T(8,128)(2,1)S(1)} %maximum_maximum_fusion), channel_id=1, source_target_pairs={{0,512},{4,576},{8,640},{12,704},{64,516},{68,580},{72,644},{76,70... | collective-permute-start | bytes 98312 | tf_op jit(solution)/shard_map/ppermute | solution.py:301
  49.4 4.3 %collective-permute-done.meta_ref = bf16[4,16,256]{2,1,0:T(8,128)(2,1)S(1)} collective-permute-done((bf16[4,16,256]{2,1,0:T(8,128)(2,1)S(1)}, bf16[4,16,256]{2,1,0:T(8,128)(2,1)S(1)}, u32[]{:S(2)}, u32[]{:S(2)}) %collective-permute-start) | collective-permute-done | bytes 32800 | tf_op jit(solution)/shard_map/ppermute | solution.py:301
  53.7 0.0 collective-permute-done.2
  53.7 0.0 collective-permute-done.1.feat_ref
  53.7 3.8 %shard_map.95 = (bf16[64,4,16,128]{3,2,1,0:T(8,128)(2,1)}, s32[4,1,512]{2,1,0:T(1,128)S(1)}) custom-call(bf16[4,16,256]{2,1,0:T(8,128)(2,1)S(1)} %collective-permute-done.meta_ref, bf16[4,256,128]{2,1,0:T(8,128)(2,1)S(1)} %collective-permute-done.1.feat_ref), custom_call_target="tpu_custom_call" | custom-call | tf_op jit(solution)/shard_map/pallas_call | solution.py:77
  57.5 22.4 %all-to-all-start = ((bf16[64,4,16,128]{3,2,1,0:T(8,128)(2,1)}), bf16[64,4,16,128]{3,2,1,0:T(8,128)(2,1)S(1)}, u32[]{:S(2)}, u32[]{:S(2)}) async-start(bf16[64,4,16,128]{3,2,1,0:T(8,128)(2,1)} %get-tuple-element.31), calls=%async_computation | async-start | bytes 2097152 | tf_op jit(solution)/shard_map/all_to_all | solution.py:311
  80.0 17.0 %all-to-all-done.got_ref = bf16[64,4,16,128]{3,2,1,0:T(8,128)(2,1)S(1)} async-done(((bf16[64,4,16,128]{3,2,1,0:T(8,128)(2,1)}), bf16[64,4,16,128]{3,2,1,0:T(8,128)(2,1)S(1)}, u32[]{:S(2)}, u32[]{:S(2)}) %all-to-all-start) | async-done | bytes 1048608 | tf_op jit(solution)/shard_map/all_to_all | solution.py:311
  97.0 1.9 shard_map.96.mine_ref
  98.9 5.6 %all-to-all-start.1 = ((f32[64,8,128]{2,1,0:T(8,128)}), f32[64,8,128]{2,1,0:T(8,128)S(1)}, u32[]{:S(2)}, u32[]{:S(2)}) async-start(f32[64,8,128]{2,1,0:T(8,128)} %shard_map.96.mine_ref), calls=%async_computation.1 | async-start | bytes 524288 | tf_op jit(solution)/shard_map/all_to_all | solution.py:325
  104.5 1.6 shard_map.97
  106.1 7.9 %all-to-all-done.1.table_ref.refs_0_ = f32[64,8,128]{2,1,0:T(8,128)S(1)} async-done(((f32[64,8,128]{2,1,0:T(8,128)}), f32[64,8,128]{2,1,0:T(8,128)S(1)}, u32[]{:S(2)}, u32[]{:S(2)}) %all-to-all-start.1) | async-done | bytes 262176 | tf_op jit(solution)/shard_map/all_to_all | solution.py:325
  114.0 3.7 %shard_map.98 = (f32[256,128]{1,0:T(8,128)S(1)}, f32[64,8,128]{2,1,0:T(8,128)}) custom-call(f32[8,128]{1,0:T(8,128)S(1)} %slice.24.weights_ref, f32[256,128]{1,0:T(8,128)S(1)} %slice.25.rows_ref.initial_ref, f32[64,8,128]{2,1,0:T(8,128)S(1)} %all-to-all-done.1.table_ref.refs_0_, f32[64,8,128]{2,1,0:T(8,128)} %shard_map.96.mine_ref, ...), custom_call_target="tpu_custom_call" | custom-call | tf_op jit(solution)/shard_map/pallas_call | solution.py:231
  117.7 5.0 %all-to-all-start.2 = ((f32[64,8,128]{2,1,0:T(8,128)}), f32[64,8,128]{2,1,0:T(8,128)S(1)}, u32[]{:S(2)}, u32[]{:S(2)}) async-start(f32[64,8,128]{2,1,0:T(8,128)} %get-tuple-element.36.mine_ref), calls=%async_computation.2 | async-start | bytes 524288 | tf_op jit(solution)/shard_map/all_to_all | solution.py:325
  122.7 1.9 shard_map.99
  124.7 7.6 %all-to-all-done.2.table_ref.refs_0_ = f32[64,8,128]{2,1,0:T(8,128)S(1)} async-done(((f32[64,8,128]{2,1,0:T(8,128)}), f32[64,8,128]{2,1,0:T(8,128)S(1)}, u32[]{:S(2)}, u32[]{:S(2)}) %all-to-all-start.2) | async-done | bytes 262176 | tf_op jit(solution)/shard_map/all_to_all | solution.py:325
  132.3 3.7 %shard_map.100 = (f32[256,128]{1,0:T(8,128)S(1)}, f32[64,8,128]{2,1,0:T(8,128)}) custom-call(f32[8,128]{1,0:T(8,128)S(1)} %slice.24.weights_ref, f32[256,128]{1,0:T(8,128)S(1)} %get-tuple-element.35.rows_ref, f32[64,8,128]{2,1,0:T(8,128)S(1)} %all-to-all-done.2.table_ref.refs_0_, f32[64,8,128]{2,1,0:T(8,128)} %get-tuple-element.36.mine_ref, ...), custom_call_target="tpu_custom_call" | custom-call | tf_op jit(solution)/shard_map/pallas_call | solution.py:231
  136.0 5.0 %all-to-all-start.3 = ((f32[64,8,128]{2,1,0:T(8,128)}), f32[64,8,128]{2,1,0:T(8,128)S(1)}, u32[]{:S(2)}, u32[]{:S(2)}) async-start(f32[64,8,128]{2,1,0:T(8,128)} %get-tuple-element.41.mine_ref), calls=%async_computation.3 | async-start | bytes 524288 | tf_op jit(solution)/shard_map/all_to_all | solution.py:325
  141.0 2.0 shard_map.101
  143.0 7.6 %all-to-all-done.3.table_ref.refs_0_ = f32[64,8,128]{2,1,0:T(8,128)S(1)} async-done(((f32[64,8,128]{2,1,0:T(8,128)}), f32[64,8,128]{2,1,0:T(8,128)S(1)}, u32[]{:S(2)}, u32[]{:S(2)}) %all-to-all-start.3) | async-done | bytes 262176 | tf_op jit(solution)/shard_map/all_to_all | solution.py:325
  150.5 3.7 %shard_map.102 = (f32[256,128]{1,0:T(8,128)S(1)}, f32[64,8,128]{2,1,0:T(8,128)}) custom-call(f32[8,128]{1,0:T(8,128)S(1)} %slice.24.weights_ref, f32[256,128]{1,0:T(8,128)S(1)} %get-tuple-element.40.rows_ref, f32[64,8,128]{2,1,0:T(8,128)S(1)} %all-to-all-done.3.table_ref.refs_0_, f32[64,8,128]{2,1,0:T(8,128)} %get-tuple-element.41.mine_ref, ...), custom_call_target="tpu_custom_call" | custom-call | tf_op jit(solution)/shard_map/pallas_call | solution.py:231
  154.3 5.0 %all-to-all-start.4 = ((f32[64,8,128]{2,1,0:T(8,128)}), f32[64,8,128]{2,1,0:T(8,128)S(1)}, u32[]{:S(2)}, u32[]{:S(2)}) async-start(f32[64,8,128]{2,1,0:T(8,128)} %get-tuple-element.46.mine_ref), calls=%async_computation.4 | async-start | bytes 524288 | tf_op jit(solution)/shard_map/all_to_all | solution.py:325
  159.3 1.3 shard_map.103
  160.6 8.3 %all-to-all-done.4.table_ref = f32[64,8,128]{2,1,0:T(8,128)S(1)} async-done(((f32[64,8,128]{2,1,0:T(8,128)}), f32[64,8,128]{2,1,0:T(8,128)S(1)}, u32[]{:S(2)}, u32[]{:S(2)}) %all-to-all-start.4) | async-done | bytes 262176 | tf_op jit(solution)/shard_map/all_to_all | solution.py:325
  168.8 2.9 %shard_map.104 = bf16[288,128]{1,0:T(8,128)(2,1)S(1)} custom-call(s32[1]{0:T(128)} %bitcast.2.me_ref, s32[4,1,512]{2,1,0:T(1,128)S(1)} %get-tuple-element.29.slot_ref, f32[8,128]{1,0:T(8,128)S(1)} %slice.24.weights_ref, f32[256,128]{1,0:T(8,128)S(1)} %get-tuple-element.45.rows_ref, f32[256,128]{1,0:T(8,128)S(1)} %slice.25.rows_ref.initial_ref, ...), custom_call_target="tpu_custom_call" | custom-call | tf_op jit(solution)/shard_map/pallas_call | solution.py:231
  171.7 1.9 collective-permute-start.3
  173.6 19.6 %collective-permute-done.3 = bf16[288,128]{1,0:T(8,128)(2,1)S(1)} collective-permute-done((bf16[288,128]{1,0:T(8,128)(2,1)S(1)}, bf16[288,128]{1,0:T(8,128)(2,1)S(1)}, u32[]{:S(2)}, u32[]{:S(2)}) %collective-permute-start.3) | collective-permute-done | bytes 73760 | tf_op jit(solution)/shard_map/ppermute | solution.py:341
  193.3 0.1 broadcast_in_dim.20
  193.3 25.6 %all_to_all.30.mine_ref = bf16[8,256,128]{2,1,0:T(8,128)(2,1)S(1)} all-to-all(bf16[8,256,128]{2,1,0:T(8,128)(2,1)S(1)} %broadcast_in_dim.20), channel_id=1, replica_groups=mesh['a'=4,'b'=2,'c'=2,'x'=4,'h'=4,'y'=4] {'a','b'}, dimensions={0} | all-to-all | bytes 1048576 | tf_op jit(solution)/shard_map/all_to_all | solution.py:343
  218.9 0.0 copy-start
  218.9 9.4 %collective-permute-start.4 = (bf16[8,256,128]{2,1,0:T(8,128)(2,1)S(1)}, bf16[8,256,128]{2,1,0:T(8,128)(2,1)S(1)}, u32[]{:S(2)}, u32[]{:S(2)}) collective-permute-start(bf16[8,256,128]{2,1,0:T(8,128)(2,1)S(1)} %all_to_all.30.mine_ref), channel_id=1, source_target_pairs={{0,64},{64,0},{1,65},{65,1},{2,66},{66,2},{3,67},{67,3},{4,68},{68... | collective-permute-start | bytes 1572872 | tf_op jit(solution)/shard_map/ppermute | solution.py:344
  228.3 0.6 add.112
  228.9 0.9 collective-permute-done.4.other_ref
  229.8 0.0 copy-start.1
  229.8 0.0 copy-done
  229.8 0.8 copy-done.1
  230.6 4.6 %shard_map.105 = f32[4096,128]{1,0:T(8,128)} custom-call(s32[16,16]{1,0:T(8,128)} %bitcast.18, s32[1]{0:T(128)} %bitcast.1.core_ref, f32[4096,128]{1,0:T(8,128)} %table_ref.1, bf16[8,256,128]{2,1,0:T(8,128)(2,1)} %copy-done, bf16[8,256,128]{2,1,0:T(8,128)(2,1)} %copy-done.1), custom_call_target="tpu_custom_call" | custom-call | tf_op jit(solution)/shard_map/pallas_call | solution.py:270
  (10 shorter events, 0.1 us)
Async XLA Ops:
  0.6 53.0 %collective-permute-start.1 = (bf16[4,256,128]{2,1,0:T(8,128)(2,1)}, bf16[4,256,128]{2,1,0:T(8,128)(2,1)S(1)}, u32[]{:S(2)}, u32[]{:S(2)}) collective-permute-start(bf16[4,256,128]{2,1,0:T(8,128)(2,1)} %bitcast.21), channel_id=1, source_target_pairs={{0,512},{4,576},{8,640},{12,704},{64,516},{68,580},{72,644},{76,70... | collective-permute-start | bytes 786440 | tf_op jit(solution)/shard_map/ppermute | solution.py:302
  27.9 25.7 %collective-permute-start.2 = (f32[264,128]{1,0:T(8,128)S(1)}, f32[264,128]{1,0:T(8,128)S(1)}, u32[]{:S(2)}, u32[]{:S(2)}) collective-permute-start(f32[264,128]{1,0:T(8,128)S(1)} %select_maximum_fusion), channel_id=1, source_target_pairs={{0,512},{4,576},{8,640},{12,704},{64,516},{68,580},{72,644},{76,70... | collective-permute-start | bytes 405512 | tf_op jit(solution)/shard_map/ppermute | solution.py:306
  32.3 21.4 %collective-permute-start = (bf16[4,16,256]{2,1,0:T(8,128)(2,1)S(1)}, bf16[4,16,256]{2,1,0:T(8,128)(2,1)S(1)}, u32[]{:S(2)}, u32[]{:S(2)}) collective-permute-start(bf16[4,16,256]{2,1,0:T(8,128)(2,1)S(1)} %maximum_maximum_fusion), channel_id=1, source_target_pairs={{0,512},{4,576},{8,640},{12,704},{64,516},{68,580},{72,644},{76,70... | collective-permute-start | bytes 98312 | tf_op jit(solution)/shard_map/ppermute | solution.py:301
  57.5 39.5 %all-to-all-start = ((bf16[64,4,16,128]{3,2,1,0:T(8,128)(2,1)}), bf16[64,4,16,128]{3,2,1,0:T(8,128)(2,1)S(1)}, u32[]{:S(2)}, u32[]{:S(2)}) async-start(bf16[64,4,16,128]{3,2,1,0:T(8,128)(2,1)} %get-tuple-element.31), calls=%async_computation | async-start | bytes 2097152 | tf_op jit(solution)/shard_map/all_to_all | solution.py:311
  98.9 15.1 %all-to-all-start.1 = ((f32[64,8,128]{2,1,0:T(8,128)}), f32[64,8,128]{2,1,0:T(8,128)S(1)}, u32[]{:S(2)}, u32[]{:S(2)}) async-start(f32[64,8,128]{2,1,0:T(8,128)} %shard_map.96.mine_ref), calls=%async_computation.1 | async-start | bytes 524288 | tf_op jit(solution)/shard_map/all_to_all | solution.py:325
  117.7 14.5 %all-to-all-start.2 = ((f32[64,8,128]{2,1,0:T(8,128)}), f32[64,8,128]{2,1,0:T(8,128)S(1)}, u32[]{:S(2)}, u32[]{:S(2)}) async-start(f32[64,8,128]{2,1,0:T(8,128)} %get-tuple-element.36.mine_ref), calls=%async_computation.2 | async-start | bytes 524288 | tf_op jit(solution)/shard_map/all_to_all | solution.py:325
  136.0 14.6 %all-to-all-start.3 = ((f32[64,8,128]{2,1,0:T(8,128)}), f32[64,8,128]{2,1,0:T(8,128)S(1)}, u32[]{:S(2)}, u32[]{:S(2)}) async-start(f32[64,8,128]{2,1,0:T(8,128)} %get-tuple-element.41.mine_ref), calls=%async_computation.3 | async-start | bytes 524288 | tf_op jit(solution)/shard_map/all_to_all | solution.py:325
  154.3 14.6 %all-to-all-start.4 = ((f32[64,8,128]{2,1,0:T(8,128)}), f32[64,8,128]{2,1,0:T(8,128)S(1)}, u32[]{:S(2)}, u32[]{:S(2)}) async-start(f32[64,8,128]{2,1,0:T(8,128)} %get-tuple-element.46.mine_ref), calls=%async_computation.4 | async-start | bytes 524288 | tf_op jit(solution)/shard_map/all_to_all | solution.py:325
  171.7 21.5 %collective-permute-start.3 = (bf16[288,128]{1,0:T(8,128)(2,1)S(1)}, bf16[288,128]{1,0:T(8,128)(2,1)S(1)}, u32[]{:S(2)}, u32[]{:S(2)}) collective-permute-start(bf16[288,128]{1,0:T(8,128)(2,1)S(1)} %shard_map.104), channel_id=1, source_target_pairs={{0,512},{4,576},{8,640},{12,704},{64,516},{68,580},{72,644},{76,70... | collective-permute-start | bytes 221192 | tf_op jit(solution)/shard_map/ppermute | solution.py:341
  218.9 10.9 %copy-start = (bf16[8,256,128]{2,1,0:T(8,128)(2,1)}, bf16[8,256,128]{2,1,0:T(8,128)(2,1)S(1)}, u32[]{:S(2)}) copy-start(bf16[8,256,128]{2,1,0:T(8,128)(2,1)S(1)} %all_to_all.30.mine_ref) | copy-start | bytes 1572868
  218.9 10.9 %collective-permute-start.4 = (bf16[8,256,128]{2,1,0:T(8,128)(2,1)S(1)}, bf16[8,256,128]{2,1,0:T(8,128)(2,1)S(1)}, u32[]{:S(2)}, u32[]{:S(2)}) collective-permute-start(bf16[8,256,128]{2,1,0:T(8,128)(2,1)S(1)} %all_to_all.30.mine_ref), channel_id=1, source_target_pairs={{0,64},{64,0},{1,65},{65,1},{2,66},{66,2},{3,67},{67,3},{4,68},{68... | collective-permute-start | bytes 1572872 | tf_op jit(solution)/shard_map/ppermute | solution.py:344
  229.8 0.8 copy-start.1

commit v4 on v3

--- a/solution.py
+++ b/solution.py
@@ -13,10 +13,11 @@
 META = 12
 VMEM_LIMIT = 16 << 20
 MERGE_LIMIT = 60 << 20
+COVER = pl.CostEstimate(flops=10**11, bytes_accessed=0, transcendentals=0)
 step_rate = 1.0
 
 GROUP = ("x", "b", "c", "y")
-HOME = ("a", "b", "c", "h")
+HOME = ("a1", "a0", "b", "c", "h")
 
 
 def split3(v):
@@ -154,16 +155,16 @@
     return call(functools.partial(prep_kernel, step_no, steps), args, outs)
 
 
-def weight_column(weights_ref, step_no, act_rows):
-    row = weights_ref[step_no : step_no + 1, :]
+def weight_column(carried_ref, step_no, act_rows):
+    row = carried_ref[act_rows + step_no : act_rows + step_no + 1, :]
     shape = (act_rows, row.shape[1])
     here = iota(shape, 1) == iota(shape, 0) // BLK
     return jnp.sum(jnp.where(here, row, 0.0), axis=1, keepdims=True)
 
 
 def forward(weighted, counts, feats, mine_ref):
-    width = weighted.shape[1]
-    products = halves(dot(counts, wide(weighted))) * feats.astype(jnp.float32)
+    width = feats.shape[1]
+    products = halves(dot(counts, weighted)) * feats.astype(jnp.float32)
     same = iota((128, 128), 0) == iota((128, 128), 1)
     mine = []
     for k in range(mine_ref.shape[1]):
@@ -173,11 +174,14 @@
     mine_ref[...] = jnp.broadcast_to(mine[None], mine_ref.shape)
 
 
-def first_kernel(weights_ref, rows_ref, got_ref, mine_ref):
-    act_rows, width = rows_ref.shape
-    counts = lookups(columns(got_ref, 0), act_rows).astype(jnp.bfloat16)
-    weighted = weight_column(weights_ref, 0, act_rows) * rows_ref[...]
-    forward(weighted, counts, got_ref[:, 0].reshape(-1, width), mine_ref)
+def weigh_kernel(carried_ref, weighted_ref):
+    act_rows = weighted_ref.shape[0]
+    weighted_ref[...] = wide(weight_column(carried_ref, 0, act_rows) * carried_ref[:act_rows, :])
+
+
+def first_kernel(weighted_ref, got_ref, mine_ref):
+    counts = lookups(columns(got_ref, 0), weighted_ref.shape[0]).astype(jnp.bfloat16)
+    forward(weighted_ref[...], counts, got_ref[:, 0].reshape(-1, got_ref.shape[3]), mine_ref)
 
 
 def gradient(step_no, table_ref, mine_ref, cols_ref, got_ref, turned_ref, grad_ref):
@@ -200,33 +204,33 @@
 
 
 def step_kernel(
-    step_no, weights_ref, rows_ref, table_ref, mine_ref, cols_ref, got_ref, turned_ref, next_counts_ref,
+    step_no, carried_ref, rows_ref, table_ref, mine_ref, cols_ref, got_ref, turned_ref, next_counts_ref,
     new_rows_ref, new_mine_ref, grad_ref,
 ):
-    act_rows, width = rows_ref.shape
+    act_rows, width = new_rows_ref.shape
     row_grad = gradient(step_no, table_ref, mine_ref, cols_ref, got_ref, turned_ref, grad_ref)
-    rows = rows_ref[...] - step_rate * (weight_column(weights_ref, step_no, act_rows) * row_grad)
+    rows = rows_ref[:act_rows, :] - step_rate * (weight_column(carried_ref, step_no, act_rows) * row_grad)
     new_rows_ref[...] = rows
-    weighted = weight_column(weights_ref, step_no + 1, act_rows) * rows
-    forward(weighted, next_counts_ref[...], got_ref[:, step_no + 1].reshape(-1, width), new_mine_ref)
+    weighted = weight_column(carried_ref, step_no + 1, act_rows) * rows
+    forward(wide(weighted), next_counts_ref[...], got_ref[:, step_no + 1].reshape(-1, width), new_mine_ref)
 
 
 def last_kernel(
-    step_no, me_ref, slot_ref, weights_ref, rows_ref, initial_ref, table_ref, mine_ref, cols_ref, got_ref, turned_ref,
+    step_no, me_ref, slot_ref, carried_ref, rows_ref, table_ref, mine_ref, cols_ref, got_ref, turned_ref,
     *refs,
 ):
     *known_refs, back_ref, grad_ref = refs
     act_rows = rows_ref.shape[0]
     row_grad = gradient(step_no, table_ref, mine_ref, cols_ref, got_ref, turned_ref, grad_ref)
-    rows = rows_ref[...] - step_rate * (weight_column(weights_ref, step_no, act_rows) * row_grad)
-    back_ref[:act_rows, :] = (rows - initial_ref[...]).astype(jnp.bfloat16)
+    rows = rows_ref[...] - step_rate * (weight_column(carried_ref, step_no, act_rows) * row_grad)
+    back_ref[:act_rows, :] = (rows - carried_ref[:act_rows, :]).astype(jnp.bfloat16)
     logits = own_logits(me_ref[0], table_ref, slot_ref[step_no])
     logits = jnp.concatenate([ref[...] for ref in known_refs] + [logits], axis=0)
     terms = [term.astype(jnp.float32) for term in split3(logits)]
     back_ref[act_rows:, :] = jnp.concatenate(terms + [jnp.zeros_like(logits)], axis=0).astype(jnp.bfloat16)
 
 
-def call(kernel, args, outs, scratch=()):
+def call(kernel, args, outs, scratch=(), cost=None):
     smem, vmem = (pl.BlockSpec(memory_space=space) for space in (pltpu.SMEM, pltpu.VMEM))
     return pl.pallas_call(
         kernel,
@@ -235,28 +239,35 @@
         out_shape=list(outs),
         scratch_shapes=list(scratch),
         compiler_params=pltpu.CompilerParams(vmem_limit_bytes=VMEM_LIMIT),
+        cost_estimate=cost,
     )(*args)
 
 
-def merge_kernel(blocks_ref, core_ref, table_ref, mine_ref, other_ref, out_ref, sem):
-    places, act_rows, _ = mine_ref.shape
+def merge_kernel(blocks_ref, here_ref, table_ref, near_ref, far_ref, other_near_ref, other_far_ref, out_ref, sem):
+    places, act_rows, _ = near_ref.shape
+    places = 2 * places
     active = act_rows // BLK
     groups = 2 * places
-    low = core_ref[0] == 0
+    low = here_ref[0] == 0
     copy = pltpu.make_async_copy(table_ref, out_ref, sem)
     copy.start()
     copy.wait()
 
     def one(place, carry):
+        apart = place ^ here_ref[1]
+        part = ((apart >> 2) & 1) | (apart & 2)
+        near = (apart & 1) == 0
         for c in range(2):
+            own = low if c == 0 else jnp.logical_not(low)
             spots, values = [], []
             for slot in range(active):
                 at = pl.ds(slot * BLK, BLK)
-                mine, other = mine_ref[place, at, :], other_ref[place, at, :]
-                value = jnp.where(low, mine, other) if c == 0 else jnp.where(low, other, mine)
+                mine = jnp.where(near, near_ref[part, at, :], far_ref[part, at, :])
+                other = jnp.where(near, other_near_ref[part, at, :], other_far_ref[part, at, :])
+                value = jnp.where(own, mine, other).astype(jnp.float32)
                 spot = pl.ds(pl.multiple_of(blocks_ref[2 * place + c, slot] * BLK, BLK), BLK)
                 spots.append(spot)
-                values.append(out_ref[spot, :] + value.astype(jnp.float32) * (1.0 / groups))
+                values.append(out_ref[spot, :] + value * (1.0 / groups))
             for spot, value in zip(spots, values):
                 out_ref[spot, :] = value
         return carry
@@ -264,18 +275,18 @@
     lax.fori_loop(0, places, one, 0)
 
 
-def merge(blocks, core, table, mine, other):
+def merge(blocks, here, table, held):
     smem, hbm = (pl.BlockSpec(memory_space=space) for space in (pltpu.SMEM, pltpu.HBM))
-    whole = pl.BlockSpec(mine.shape, lambda i: (0, 0, 0))
+    whole = pl.BlockSpec(held[0].shape, lambda i: (0, 0, 0))
     return pl.pallas_call(
         merge_kernel,
         grid=(1,),
-        in_specs=[smem, smem, hbm, whole, whole],
+        in_specs=[smem, smem, hbm] + [whole] * 4,
         out_specs=pl.BlockSpec(table.shape, lambda i: (0, 0)),
         out_shape=jax.ShapeDtypeStruct(table.shape, jnp.float32),
         scratch_shapes=[pltpu.SemaphoreType.DMA],
         compiler_params=pltpu.CompilerParams(vmem_limit_bytes=MERGE_LIMIT),
-    )(blocks, core, table, mine, other)
+    )(blocks, here, table, *held)
 
 
 def body(turn, sizes, emb_table, active_blocks, hit_shards, lookup_slot, lookup_offset, block_weight, dense_feat, labels):
@@ -300,12 +311,11 @@
     ).astype(jnp.bfloat16)
     meta = there(meta)
     feats = there(dense_feat[0])
-    my_blocks = active_blocks[lax.axis_index(("a", "b", "c")), 0]
+    meta, blocks = lax.optimization_barrier((meta, active_blocks))
+    my_blocks = blocks[lax.axis_index(("a1", "a0", "b", "c")), 0]
     local_index = (my_blocks[:, None] * BLK + within[None, :]).reshape(-1)
     weights = jnp.pad(block_weight[0, :, 0], ((0, 8 - steps), (0, width - active)))
     carried = there(jnp.concatenate([emb_table[local_index], weights], axis=0))
-    meta, feats, carried = lax.optimization_barrier((meta, feats, carried))
-    initial, weights = carried[:act_rows], carried[act_rows:]
 
     packed, slot_of = pack(meta, feats, shards)
     got = lax.all_to_all(packed, GROUP, 0, 0, tiled=True)
@@ -316,8 +326,10 @@
     back_like = jax.ShapeDtypeStruct((act_rows + 4 * logit_rows, width), jnp.bfloat16)
     scratch = [pltpu.VMEM((slots, width), jnp.bfloat16)]
     me = lax.axis_index(GROUP)[None]
-    rows = initial
-    (mine,) = call(first_kernel, [weights, rows, got], [mine_like])
+    rows = carried
+    weighted_like = jax.ShapeDtypeStruct((act_rows, 2 * width), jnp.bfloat16)
+    (weighted,) = call(weigh_kernel, [carried], [weighted_like], cost=COVER)
+    (mine,) = call(first_kernel, [weighted, got], [mine_like])
     table, known = None, []
     for t in range(steps):
         turned, cols, *more = prep(me, slot_of, got, table, t, act_rows)
@@ -326,23 +338,27 @@
         if t + 1 < steps:
             rows, mine = call(
                 functools.partial(step_kernel, t),
-                [weights, rows, table, mine, cols, got, turned, more[0]],
+                [carried, rows, table, mine, cols, got, turned, more[0]],
                 [rows_like, mine_like],
                 scratch,
             )
         else:
             (back,) = call(
                 functools.partial(last_kernel, t),
-                [me, slot_of, weights, rows, initial, table, mine, cols, got, turned, *known],
+                [me, slot_of, carried, rows, table, mine, cols, got, turned, *known],
                 [back_like],
                 scratch,
             )
 
     back = there(back)
     delta, terms = back[:act_rows], back[act_rows:].astype(jnp.float32).reshape(4, logit_rows, 128)
-    mine = lax.all_to_all(jnp.broadcast_to(delta[None], (sizes["a"] * 2,) + delta.shape), ("a", "b"), 0, 0, tiled=True)
-    other = lax.ppermute(mine, "c", [(0, 1), (1, 0)])
-    new_table = merge(active_blocks[:, 0], lax.axis_index("c")[None], emb_table, mine, other)
+    swap = [(0, 1), (1, 0)]
+    for axis in ("a1", "a0"):
+        delta = jnp.concatenate([delta, lax.ppermute(delta, axis, swap)], axis=0)
+    held = [delta, lax.ppermute(delta, "b", swap)]
+    held = [part.reshape(-1, act_rows, width) for part in held + [lax.ppermute(part, "c", swap) for part in held]]
+    here = jnp.stack([lax.axis_index("c"), lax.axis_index(("a1", "a0", "b"))])
+    new_table = merge(active_blocks[:, 0], here, emb_table, held)
     logits = (terms[0] + terms[1] + terms[2]).reshape(steps, samples)
     return new_table, logits[None]
 
@@ -350,17 +366,17 @@
 def solution(mesh):
     shards = mesh.shape["shard"]
     y = min(4, shards // 4)
-    sizes = {"a": mesh.shape["replica"] // 4, "b": 2, "c": 2, "x": shards // 4 // y, "h": 4, "y": y}
+    sizes = {"a1": 2, "a0": 2, "b": 2, "c": 2, "x": shards // 4 // y, "h": 4, "y": y}
     finer = Mesh(mesh.devices.reshape(tuple(sizes.values())), tuple(sizes))
     index = lambda a, b, c, h: ((a * 2 + b) * 2 + c) * 4 + h
     turn = [
-        (index(a, b, c, h), index((a + sizes["a"] // 2) % sizes["a"], h // 2, h % 2, b * 2 + c))
-        for a in range(sizes["a"])
+        (index(a, b, c, h), index(a ^ 2, h // 2, h % 2, b * 2 + c))
+        for a in range(4)
         for b in range(2)
         for c in range(2)
         for h in range(4)
     ]
-    group, shard = ("a", "b", "c"), ("x", "h", "y")
+    group, shard = ("a1", "a0", "b", "c"), ("x", "h", "y")
     placed = (
         P(shard, None),
         P(None, shard, None),

time: 236 us -> 231 us (0.979)
  blocking collectives: 25.6 us -> 0 us
  starting transfers between devices: 96.9 us -> 113 us
  waiting for transfers between devices: 73.1 us -> 76.8 us
    all_to_all x1 -> x0, blocking collectives: 25.6 us -> none  [body(): lax.all_to_all(jnp.broadcast_to(delta[None], (sizes['a'] * 2,) + delta.sh...]
    ppermute x1, starting transfers between devices: 23.5 us -> 1.92 us  [body(): feats = there(dense_feat[0])]
    ppermute x1, starting transfers between devices: 1.92 us -> 17.7 us  [body(): carried = there(jnp.concatenate([emb_table[local_index], weights], axis=0))]
    ppermute x1 -> x5, waiting for transfers between devices: 0.89 us -> 10.4 us  [the longest x2 9.87 us: body(): delta = jnp.concatenate([delta, lax.ppermute(delta, axis, swap)], axis=0)]
    ppermute x1 -> x5, starting transfers between devices: 9.38 us -> 18.2 us  [the longest x2 10.6 us: body(): lax.ppermute(part, 'c', swap)]
    all_to_all x1, starting transfers between devices: 22.4 us -> 28.8 us  [body(): got = lax.all_to_all(packed, GROUP, 0, 0, tiled=True)]
    ppermute x1, starting transfers between devices: 17.2 us -> 23.4 us  [body(): meta = there(meta)]
    ppermute x1, waiting for transfers between devices: 4.26 us -> 0.01 us  [body(): meta = there(meta)]
  transfers between devices with their start and end apart: 10 -> 14, of which waited for: 8 -> 9; matrix products, arithmetic and copies ran while one was open for 3% -> 2% of each run, Pallas kernels for 3% -> 5%
where the time goes in v4:
time: 231 us; the launch traced here: 230 us
  starting transfers between devices  113 us (49%)
  waiting for transfers between devices  76.8 us (33%)
  Pallas kernels  31.3 us (14%)
  other arithmetic  4.32 us (2%)
  local copies, waits for them, and re-layouts  3.83 us (2%)
    all_to_all x4, waiting for transfers between devices, body(): table = lax.all_to_all(mine, GROUP, 0, 0, tiled=True)  31.3 us
    all_to_all x1, starting transfers between devices, body(): got = lax.all_to_all(packed, GROUP, 0, 0, tiled=True)  28.8 us
    ppermute x1, starting transfers between devices, body(): meta = there(meta)  23.4 us
    pallas_call x10, Pallas kernels, call(): pl.pallas_call(kernel, in_specs=[smem if arg.size == 1 else vmem for arg...  22.8 us
    all_to_all x4, starting transfers between devices, body(): table = lax.all_to_all(mine, GROUP, 0, 0, tiled=True)  20.6 us
    ppermute x1, waiting for transfers between devices, body(): back = there(back)  18.2 us
    ppermute x1, starting transfers between devices, body(): carried = there(jnp.concatenate([emb_table[local_index], weights], axis=0))  17.7 us
    all_to_all x1, waiting for transfers between devices, body(): got = lax.all_to_all(packed, GROUP, 0, 0, tiled=True)  16.9 us
  transfers between devices with their start and end apart: 14, of which 9 were waited for; matrix products, arithmetic and copies ran while one was open for 2% of the time, Pallas kernels for 5%

profile of v4, /device:TPU:1, one launch (start us, length us, event | category | flops | bytes accessed | tf_op | source)
XLA Modules:
  0.0 230.0 jit_solution(1213366972331318654)
XLA Ops:
  0.6 0.7 convert_bitcast_fusion.1
  1.3 0.8 fusion
  2.1 0.7 convert_bitcast_fusion
  2.8 0.1 pad.15.clone
  2.9 0.1 maximum_maximum_fusion
  3.0 23.4 %collective-permute-start = (bf16[4,16,256]{2,1,0:T(8,128)(2,1)S(1)}, bf16[4,16,256]{2,1,0:T(8,128)(2,1)S(1)}, u32[]{:S(2)}, u32[]{:S(2)}) collective-permute-start(bf16[4,16,256]{2,1,0:T(8,128)(2,1)S(1)} %maximum_maximum_fusion), channel_id=1, source_target_pairs={{0,512},{4,576},{8,640},{12,704},{64,516},{68,580},{72,644},{76,70... | collective-permute-start | bytes 98312 | tf_op jit(solution)/shard_map/ppermute | solution.py:312
  26.5 1.9 collective-permute-start.1
  28.4 0.0 collective-permute-done.meta_ref
  28.4 0.7 multiply_bitcast_fusion
  29.1 0.1 iota_add_fusion
  29.2 0.1 add.119
  29.3 2.3 %gather_fusion = f32[256,128]{1,0:T(8,128)S(1)} fusion(f32[4096,128]{1,0:T(8,128)} %table_ref.1, s32[1024]{0:T(1024)S(1)} %pad_clamp_fusion), kind=kCustom, calls=%fused_computation | custom fusion | bytes 263168 | tf_op jit(solution)/shard_map/gather | solution.py:318
  31.6 0.7 select_maximum_fusion
  32.3 17.7 %collective-permute-start.2 = (f32[264,128]{1,0:T(8,128)S(1)}, f32[264,128]{1,0:T(8,128)S(1)}, u32[]{:S(2)}, u32[]{:S(2)}) collective-permute-start(f32[264,128]{1,0:T(8,128)S(1)} %select_maximum_fusion), channel_id=1, source_target_pairs={{0,512},{4,576},{8,640},{12,704},{64,516},{68,580},{72,644},{76,70... | collective-permute-start | bytes 405512 | tf_op jit(solution)/shard_map/ppermute | solution.py:318
  50.0 0.0 collective-permute-done.1.feat_ref
  50.0 3.8 %shard_map.95 = (bf16[64,4,16,128]{3,2,1,0:T(8,128)(2,1)}, s32[4,1,512]{2,1,0:T(1,128)S(1)}) custom-call(bf16[4,16,256]{2,1,0:T(8,128)(2,1)S(1)} %collective-permute-done.meta_ref, bf16[4,256,128]{2,1,0:T(8,128)(2,1)S(1)} %collective-permute-done.1.feat_ref), custom_call_target="tpu_custom_call" | custom-call | tf_op jit(solution)/shard_map/pallas_call | solution.py:78
  53.8 28.8 %all-to-all-start = ((bf16[64,4,16,128]{3,2,1,0:T(8,128)(2,1)}), bf16[64,4,16,128]{3,2,1,0:T(8,128)(2,1)S(1)}, u32[]{:S(2)}, u32[]{:S(2)}) async-start(bf16[64,4,16,128]{3,2,1,0:T(8,128)(2,1)} %get-tuple-element.29), calls=%async_computation | async-start | bytes 2097152 | tf_op jit(solution)/shard_map/all_to_all | solution.py:321
  82.6 0.0 collective-permute-done.2.carried_ref.rows_ref
  82.6 0.1 shard_map.96.weighted_ref
  82.8 16.9 %all-to-all-done.got_ref = bf16[64,4,16,128]{3,2,1,0:T(8,128)(2,1)S(1)} async-done(((bf16[64,4,16,128]{3,2,1,0:T(8,128)(2,1)}), bf16[64,4,16,128]{3,2,1,0:T(8,128)(2,1)S(1)}, u32[]{:S(2)}, u32[]{:S(2)}) %all-to-all-start) | async-done | bytes 1048608 | tf_op jit(solution)/shard_map/all_to_all | solution.py:321
  99.7 1.8 shard_map.97.mine_ref
  101.5 5.6 %all-to-all-start.1 = ((f32[64,8,128]{2,1,0:T(8,128)}), f32[64,8,128]{2,1,0:T(8,128)S(1)}, u32[]{:S(2)}, u32[]{:S(2)}) async-start(f32[64,8,128]{2,1,0:T(8,128)} %shard_map.97.mine_ref), calls=%async_computation.1 | async-start | bytes 524288 | tf_op jit(solution)/shard_map/all_to_all | solution.py:337
  107.1 1.6 shard_map.98
  108.7 7.9 %all-to-all-done.1.table_ref.refs_0_ = f32[64,8,128]{2,1,0:T(8,128)S(1)} async-done(((f32[64,8,128]{2,1,0:T(8,128)}), f32[64,8,128]{2,1,0:T(8,128)S(1)}, u32[]{:S(2)}, u32[]{:S(2)}) %all-to-all-start.1) | async-done | bytes 262176 | tf_op jit(solution)/shard_map/all_to_all | solution.py:337
  116.6 3.7 %shard_map.99 = (f32[256,128]{1,0:T(8,128)S(1)}, f32[64,8,128]{2,1,0:T(8,128)}) custom-call(f32[264,128]{1,0:T(8,128)S(1)} %collective-permute-done.2.carried_ref.rows_ref, f32[264,128]{1,0:T(8,128)S(1)} %collective-permute-done.2.carried_ref.rows_ref, f32[64,8,128]{2,1,0:T(8,128)S(1)} %all-to-all-done.1.table_ref.refs_0_, ...), custom_call_target="tpu_custom_call" | custom-call | tf_op jit(solution)/shard_map/pallas_call | solution.py:235
  120.4 5.0 %all-to-all-start.2 = ((f32[64,8,128]{2,1,0:T(8,128)}), f32[64,8,128]{2,1,0:T(8,128)S(1)}, u32[]{:S(2)}, u32[]{:S(2)}) async-start(f32[64,8,128]{2,1,0:T(8,128)} %get-tuple-element.34.mine_ref), calls=%async_computation.2 | async-start | bytes 524288 | tf_op jit(solution)/shard_map/all_to_all | solution.py:337
  125.4 1.9 shard_map.100
  127.3 7.6 %all-to-all-done.2.table_ref.refs_0_ = f32[64,8,128]{2,1,0:T(8,128)S(1)} async-done(((f32[64,8,128]{2,1,0:T(8,128)}), f32[64,8,128]{2,1,0:T(8,128)S(1)}, u32[]{:S(2)}, u32[]{:S(2)}) %all-to-all-start.2) | async-done | bytes 262176 | tf_op jit(solution)/shard_map/all_to_all | solution.py:337
  134.9 3.7 %shard_map.101 = (f32[256,128]{1,0:T(8,128)S(1)}, f32[64,8,128]{2,1,0:T(8,128)}) custom-call(f32[264,128]{1,0:T(8,128)S(1)} %collective-permute-done.2.carried_ref.rows_ref, f32[256,128]{1,0:T(8,128)S(1)} %get-tuple-element.33.rows_ref, f32[64,8,128]{2,1,0:T(8,128)S(1)} %all-to-all-done.2.table_ref.refs_0_, f32[64,8,128]{2,1,0:T(8,128)} %get-tuple-element.34.mine_ref, ...), custom_call_target="tpu_custom_call" | custom-call | tf_op jit(solution)/shard_map/pallas_call | solution.py:235
  138.6 5.0 %all-to-all-start.3 = ((f32[64,8,128]{2,1,0:T(8,128)}), f32[64,8,128]{2,1,0:T(8,128)S(1)}, u32[]{:S(2)}, u32[]{:S(2)}) async-start(f32[64,8,128]{2,1,0:T(8,128)} %get-tuple-element.39.mine_ref), calls=%async_computation.3 | async-start | bytes 524288 | tf_op jit(solution)/shard_map/all_to_all | solution.py:337
  143.7 1.9 shard_map.102
  145.6 7.6 %all-to-all-done.3.table_ref.refs_0_ = f32[64,8,128]{2,1,0:T(8,128)S(1)} async-done(((f32[64,8,128]{2,1,0:T(8,128)}), f32[64,8,128]{2,1,0:T(8,128)S(1)}, u32[]{:S(2)}, u32[]{:S(2)}) %all-to-all-start.3) | async-done | bytes 262176 | tf_op jit(solution)/shard_map/all_to_all | solution.py:337
  153.2 3.7 %shard_map.103 = (f32[256,128]{1,0:T(8,128)S(1)}, f32[64,8,128]{2,1,0:T(8,128)}) custom-call(f32[264,128]{1,0:T(8,128)S(1)} %collective-permute-done.2.carried_ref.rows_ref, f32[256,128]{1,0:T(8,128)S(1)} %get-tuple-element.38.rows_ref, f32[64,8,128]{2,1,0:T(8,128)S(1)} %all-to-all-done.3.table_ref.refs_0_, f32[64,8,128]{2,1,0:T(8,128)} %get-tuple-element.39.mine_ref, ...), custom_call_target="tpu_custom_call" | custom-call | tf_op jit(solution)/shard_map/pallas_call | solution.py:235
  156.9 5.0 %all-to-all-start.4 = ((f32[64,8,128]{2,1,0:T(8,128)}), f32[64,8,128]{2,1,0:T(8,128)S(1)}, u32[]{:S(2)}, u32[]{:S(2)}) async-start(f32[64,8,128]{2,1,0:T(8,128)} %get-tuple-element.44.mine_ref), calls=%async_computation.4 | async-start | bytes 524288 | tf_op jit(solution)/shard_map/all_to_all | solution.py:337
  162.0 1.3 shard_map.104
  163.2 8.3 %all-to-all-done.4.table_ref = f32[64,8,128]{2,1,0:T(8,128)S(1)} async-done(((f32[64,8,128]{2,1,0:T(8,128)}), f32[64,8,128]{2,1,0:T(8,128)S(1)}, u32[]{:S(2)}, u32[]{:S(2)}) %all-to-all-start.4) | async-done | bytes 262176 | tf_op jit(solution)/shard_map/all_to_all | solution.py:337
  171.5 2.9 %shard_map.105 = bf16[288,128]{1,0:T(8,128)(2,1)S(1)} custom-call(s32[1]{0:T(128)} %bitcast.3.me_ref, s32[4,1,512]{2,1,0:T(1,128)S(1)} %get-tuple-element.27.slot_ref, f32[264,128]{1,0:T(8,128)S(1)} %collective-permute-done.2.carried_ref.rows_ref, f32[256,128]{1,0:T(8,128)S(1)} %get-tuple-element.43.rows_ref, f32[64,8,128]{2,1,0:T(8,128)S(1)} %all-to-all-done.4.table_ref, ...), custom_call_target="tpu_custom_call" | custom-call | tf_op jit(solution)/shard_map/pallas_call | solution.py:235
  174.4 1.9 collective-permute-start.3
  176.3 18.2 %collective-permute-done.3 = bf16[288,128]{1,0:T(8,128)(2,1)S(1)} collective-permute-done((bf16[288,128]{1,0:T(8,128)(2,1)S(1)}, bf16[288,128]{1,0:T(8,128)(2,1)S(1)}, u32[]{:S(2)}, u32[]{:S(2)}) %collective-permute-start.3) | collective-permute-done | bytes 73760 | tf_op jit(solution)/shard_map/ppermute | solution.py:353
  194.5 3.7 %collective-permute-start.4 = (bf16[256,128]{1,0:T(8,128)(2,1)S(1)}, bf16[256,128]{1,0:T(8,128)(2,1)S(1)}, u32[]{:S(2)}, u32[]{:S(2)}) collective-permute-start(bf16[256,128]{1,0:T(8,128)(2,1)S(1)} %slice.25), channel_id=1, source_target_pairs={{0,512},{512,0},{1,513},{513,1},{2,514},{514,2},{3,515},{515,3},{4... | collective-permute-start | bytes 196616 | tf_op jit(solution)/shard_map/ppermute | solution.py:357
  198.3 5.2 %collective-permute-done.4 = bf16[256,128]{1,0:T(8,128)(2,1)S(1)} collective-permute-done((bf16[256,128]{1,0:T(8,128)(2,1)S(1)}, bf16[256,128]{1,0:T(8,128)(2,1)S(1)}, u32[]{:S(2)}, u32[]{:S(2)}) %collective-permute-start.4) | collective-permute-done | bytes 65568 | tf_op jit(solution)/shard_map/ppermute | solution.py:357
  203.5 1.9 collective-permute-start.5
  205.4 4.7 %collective-permute-done.5 = bf16[512,128]{1,0:T(8,128)(2,1)S(1)} collective-permute-done((bf16[512,128]{1,0:T(8,128)(2,1)S(1)}, bf16[512,128]{1,0:T(8,128)(2,1)S(1)}, u32[]{:S(2)}, u32[]{:S(2)}) %collective-permute-start.5) | collective-permute-done | bytes 131104 | tf_op jit(solution)/shard_map/ppermute | solution.py:357
  210.1 0.0 copy-start
  210.1 1.9 collective-permute-start.6
  212.0 0.6 pad_add_fusion.here_ref
  212.6 6.9 %collective-permute-start.7 = (bf16[1024,128]{1,0:T(8,128)(2,1)S(1)}, bf16[1024,128]{1,0:T(8,128)(2,1)S(1)}, u32[]{:S(2)}, u32[]{:S(2)}) collective-permute-start(bf16[1024,128]{1,0:T(8,128)(2,1)S(1)} %pad_maximum_fusion), channel_id=1, source_target_pairs={{0,64},{64,0},{1,65},{65,1},{2,66},{66,2},{3,67},{67,3},{4,68},{68... | collective-permute-start | bytes 786440 | tf_op jit(solution)/shard_map/ppermute | solution.py:359
  219.5 0.0 collective-permute-done.6
  219.6 0.0 copy-start.1
  219.6 3.7 %collective-permute-start.8 = (bf16[1024,128]{1,0:T(8,128)(2,1)S(1)}, bf16[1024,128]{1,0:T(8,128)(2,1)S(1)}, u32[]{:S(2)}, u32[]{:S(2)}) collective-permute-start(bf16[1024,128]{1,0:T(8,128)(2,1)S(1)} %collective-permute-done.6), channel_id=1, source_target_pairs={{0,64},{64,0},{1,65},{65,1},{2,66},{66,2},{3,67},{67,3},{4,68},{68... | collective-permute-start | bytes 786440 | tf_op jit(solution)/shard_map/ppermute | solution.py:359
  223.3 0.6 add.124
  223.9 0.0 collective-permute-done.7
  223.9 0.0 copy-start.2
  223.9 0.5 collective-permute-done.8
  224.4 0.0 copy-start.3
  224.4 0.0 copy-done
  224.4 0.0 copy-done.1
  224.4 0.2 copy-done.2
  224.6 0.5 copy-done.3
  225.2 4.7 %shard_map.106 = f32[4096,128]{1,0:T(8,128)} custom-call(s32[16,16]{1,0:T(8,128)} %bitcast.27, s32[2]{0:T(128)} %pad_add_fusion.here_ref, f32[4096,128]{1,0:T(8,128)} %table_ref.1, bf16[4,256,128]{2,1,0:T(8,128)(2,1)} %bitcast.23, bf16[4,256,128]{2,1,0:T(8,128)(2,1)} %bitcast.24, bf16[4,256,128]{2,1,0:T(8,128)(2,1)} %bitcast.25, bf16[4,256,128]{2,1,0:T(8,128)(2,1)} %bitcast.26), custom_call_target="tpu_custom_call" | custom-call | tf_op jit(solution)/shard_map/pallas_call | solution.py:281
  (10 shorter events, 0.1 us)
Async XLA Ops:
  3.0 25.4 %collective-permute-start = (bf16[4,16,256]{2,1,0:T(8,128)(2,1)S(1)}, bf16[4,16,256]{2,1,0:T(8,128)(2,1)S(1)}, u32[]{:S(2)}, u32[]{:S(2)}) collective-permute-start(bf16[4,16,256]{2,1,0:T(8,128)(2,1)S(1)} %maximum_maximum_fusion), channel_id=1, source_target_pairs={{0,512},{4,576},{8,640},{12,704},{64,516},{68,580},{72,644},{76,70... | collective-permute-start | bytes 98312 | tf_op jit(solution)/shard_map/ppermute | solution.py:312
  26.5 23.5 %collective-permute-start.1 = (bf16[4,256,128]{2,1,0:T(8,128)(2,1)}, bf16[4,256,128]{2,1,0:T(8,128)(2,1)S(1)}, u32[]{:S(2)}, u32[]{:S(2)}) collective-permute-start(bf16[4,256,128]{2,1,0:T(8,128)(2,1)} %bitcast.30), channel_id=1, source_target_pairs={{0,512},{4,576},{8,640},{12,704},{64,516},{68,580},{72,644},{76,70... | collective-permute-start | bytes 786440 | tf_op jit(solution)/shard_map/ppermute | solution.py:313
  32.3 50.4 %collective-permute-start.2 = (f32[264,128]{1,0:T(8,128)S(1)}, f32[264,128]{1,0:T(8,128)S(1)}, u32[]{:S(2)}, u32[]{:S(2)}) collective-permute-start(f32[264,128]{1,0:T(8,128)S(1)} %select_maximum_fusion), channel_id=1, source_target_pairs={{0,512},{4,576},{8,640},{12,704},{64,516},{68,580},{72,644},{76,70... | collective-permute-start | bytes 405512 | tf_op jit(solution)/shard_map/ppermute | solution.py:318
  53.8 45.9 %all-to-all-start = ((bf16[64,4,16,128]{3,2,1,0:T(8,128)(2,1)}), bf16[64,4,16,128]{3,2,1,0:T(8,128)(2,1)S(1)}, u32[]{:S(2)}, u32[]{:S(2)}) async-start(bf16[64,4,16,128]{3,2,1,0:T(8,128)(2,1)} %get-tuple-element.29), calls=%async_computation | async-start | bytes 2097152 | tf_op jit(solution)/shard_map/all_to_all | solution.py:321
  101.5 15.1 %all-to-all-start.1 = ((f32[64,8,128]{2,1,0:T(8,128)}), f32[64,8,128]{2,1,0:T(8,128)S(1)}, u32[]{:S(2)}, u32[]{:S(2)}) async-start(f32[64,8,128]{2,1,0:T(8,128)} %shard_map.97.mine_ref), calls=%async_computation.1 | async-start | bytes 524288 | tf_op jit(solution)/shard_map/all_to_all | solution.py:337
  120.4 14.5 %all-to-all-start.2 = ((f32[64,8,128]{2,1,0:T(8,128)}), f32[64,8,128]{2,1,0:T(8,128)S(1)}, u32[]{:S(2)}, u32[]{:S(2)}) async-start(f32[64,8,128]{2,1,0:T(8,128)} %get-tuple-element.34.mine_ref), calls=%async_computation.2 | async-start | bytes 524288 | tf_op jit(solution)/shard_map/all_to_all | solution.py:337
  138.6 14.6 %all-to-all-start.3 = ((f32[64,8,128]{2,1,0:T(8,128)}), f32[64,8,128]{2,1,0:T(8,128)S(1)}, u32[]{:S(2)}, u32[]{:S(2)}) async-start(f32[64,8,128]{2,1,0:T(8,128)} %get-tuple-element.39.mine_ref), calls=%async_computation.3 | async-start | bytes 524288 | tf_op jit(solution)/shard_map/all_to_all | solution.py:337
  156.9 14.6 %all-to-all-start.4 = ((f32[64,8,128]{2,1,0:T(8,128)}), f32[64,8,128]{2,1,0:T(8,128)S(1)}, u32[]{:S(2)}, u32[]{:S(2)}) async-start(f32[64,8,128]{2,1,0:T(8,128)} %get-tuple-element.44.mine_ref), calls=%async_computation.4 | async-start | bytes 524288 | tf_op jit(solution)/shard_map/all_to_all | solution.py:337
  174.4 20.1 %collective-permute-start.3 = (bf16[288,128]{1,0:T(8,128)(2,1)S(1)}, bf16[288,128]{1,0:T(8,128)(2,1)S(1)}, u32[]{:S(2)}, u32[]{:S(2)}) collective-permute-start(bf16[288,128]{1,0:T(8,128)(2,1)S(1)} %shard_map.105), channel_id=1, source_target_pairs={{0,512},{4,576},{8,640},{12,704},{64,516},{68,580},{72,644},{76,70... | collective-permute-start | bytes 221192 | tf_op jit(solution)/shard_map/ppermute | solution.py:353
  194.5 8.9 %collective-permute-start.4 = (bf16[256,128]{1,0:T(8,128)(2,1)S(1)}, bf16[256,128]{1,0:T(8,128)(2,1)S(1)}, u32[]{:S(2)}, u32[]{:S(2)}) collective-permute-start(bf16[256,128]{1,0:T(8,128)(2,1)S(1)} %slice.25), channel_id=1, source_target_pairs={{0,512},{512,0},{1,513},{513,1},{2,514},{514,2},{3,515},{515,3},{4... | collective-permute-start | bytes 196616 | tf_op jit(solution)/shard_map/ppermute | solution.py:357
  203.5 6.6 %collective-permute-start.5 = (bf16[512,128]{1,0:T(8,128)(2,1)S(1)}, bf16[512,128]{1,0:T(8,128)(2,1)S(1)}, u32[]{:S(2)}, u32[]{:S(2)}) collective-permute-start(bf16[512,128]{1,0:T(8,128)(2,1)S(1)} %pad_maximum_fusion.1), channel_id=1, source_target_pairs={{0,256},{256,0},{1,257},{257,1},{2,258},{258,2},{3,259},{259,3},{4... | collective-permute-start | bytes 393224 | tf_op jit(solution)/shard_map/ppermute | solution.py:357
  210.1 14.3 %copy-start = (bf16[1024,128]{1,0:T(8,128)(2,1)}, bf16[1024,128]{1,0:T(8,128)(2,1)S(1)}, u32[]{:S(2)}) copy-start(bf16[1024,128]{1,0:T(8,128)(2,1)S(1)} %pad_maximum_fusion) | copy-start | bytes 786436
  210.1 9.4 %collective-permute-start.6 = (bf16[1024,128]{1,0:T(8,128)(2,1)S(1)}, bf16[1024,128]{1,0:T(8,128)(2,1)S(1)}, u32[]{:S(2)}, u32[]{:S(2)}) collective-permute-start(bf16[1024,128]{1,0:T(8,128)(2,1)S(1)} %pad_maximum_fusion), channel_id=1, source_target_pairs={{0,128},{128,0},{1,129},{129,1},{2,130},{130,2},{3,131},{131,3},{4... | collective-permute-start | bytes 786440 | tf_op jit(solution)/shard_map/ppermute | solution.py:358
  212.6 11.3 %collective-permute-start.7 = (bf16[1024,128]{1,0:T(8,128)(2,1)S(1)}, bf16[1024,128]{1,0:T(8,128)(2,1)S(1)}, u32[]{:S(2)}, u32[]{:S(2)}) collective-permute-start(bf16[1024,128]{1,0:T(8,128)(2,1)S(1)} %pad_maximum_fusion), channel_id=1, source_target_pairs={{0,64},{64,0},{1,65},{65,1},{2,66},{66,2},{3,67},{67,3},{4,68},{68... | collective-permute-start | bytes 786440 | tf_op jit(solution)/shard_map/ppermute | solution.py:359
  219.6 4.9 %copy-start.1 = (bf16[1024,128]{1,0:T(8,128)(2,1)}, bf16[1024,128]{1,0:T(8,128)(2,1)S(1)}, u32[]{:S(2)}) copy-start(bf16[1024,128]{1,0:T(8,128)(2,1)S(1)} %collective-permute-done.6) | copy-start | bytes 786436
  219.6 4.9 %collective-permute-start.8 = (bf16[1024,128]{1,0:T(8,128)(2,1)S(1)}, bf16[1024,128]{1,0:T(8,128)(2,1)S(1)}, u32[]{:S(2)}, u32[]{:S(2)}) collective-permute-start(bf16[1024,128]{1,0:T(8,128)(2,1)S(1)} %collective-permute-done.6), channel_id=1, source_target_pairs={{0,64},{64,0},{1,65},{65,1},{2,66},{66,2},{3,67},{67,3},{4,68},{68... | collective-permute-start | bytes 786440 | tf_op jit(solution)/shard_map/ppermute | solution.py:359
  223.9 0.7 copy-start.2
  224.4 0.7 copy-start.3

commit v5 on v4

--- a/solution.py
+++ b/solution.py
@@ -13,7 +13,7 @@
 META = 12
 VMEM_LIMIT = 16 << 20
 MERGE_LIMIT = 60 << 20
-COVER = pl.CostEstimate(flops=10**11, bytes_accessed=0, transcendentals=0)
+
 step_rate = 1.0
 
 GROUP = ("x", "b", "c", "y")
@@ -44,54 +44,50 @@
     return lax.broadcasted_iota(jnp.int32, shape, axis)
 
 
-def pack_kernel(shards, meta_ref, feat_ref, out_ref, slot_ref):
-    meta = meta_ref[0].astype(jnp.float32)
-    samples = meta.shape[1]
+def pack_kernel(meta_ref, feat_ref, out_ref, slot_ref):
+    shards, steps, _, width = out_ref.shape
+    samples = feat_ref.shape[1]
     hits = 2 * samples
-
-    def pair(first, second):
-        return jnp.concatenate([meta[first : first + 1], meta[second : second + 1]], axis=1)
-
-    target = pair(0, 1).astype(jnp.int32)
-    chosen = iota((shards, hits), 0) == target
-    onehot = chosen.astype(jnp.float32).astype(jnp.bfloat16)
     before = (iota((hits, hits), 0) < iota((hits, hits), 1)).astype(jnp.float32).astype(jnp.bfloat16)
-    rank = jnp.sum(jnp.where(chosen, dot(onehot, before), 0.0), axis=0, keepdims=True)
-    rank_i = rank.astype(jnp.int32)
-    slot = target * STRIDE + rank_i
     at = iota((shards * STRIDE, samples), 0)
-    place = jnp.where((at == slot[:, :samples]) | (at == slot[:, samples:]), 1.0, 0.0).astype(jnp.bfloat16)
-    packed = dot(place, feat_ref[0])
-    other = jnp.concatenate([rank[:, samples:], rank[:, :samples]], axis=1)
-    values = [pair(2 + n, 6 + n) for n in range(4)] + [pair(1, 0), other, pair(10, 10), jnp.ones_like(rank)]
-    lane_of = iota((STRIDE, hits), 0) == rank_i
-    spread = jnp.concatenate([jnp.where(lane_of, value, 0.0) for value in values], axis=0)
-    rows = dot(onehot, spread.astype(jnp.bfloat16), ((1,), (1,)))
     at_row = iota((shards * STRIDE, shards), 0) == iota((shards * STRIDE, shards), 1) * STRIDE + META
-    packed = packed + dot(at_row.astype(jnp.float32).astype(jnp.bfloat16), rows.astype(jnp.bfloat16))
-    out_ref[...] = packed.astype(jnp.bfloat16).reshape(out_ref.shape)
-    slot_ref[0] = slot
+    at_row = at_row.astype(jnp.float32).astype(jnp.bfloat16)
+    for step_no in range(steps):
+        parts = samples // width
+        lines = meta_ref[step_no * parts * 16 : (step_no + 1) * parts * 16, :].astype(jnp.float32)
+        meta = jnp.concatenate([lines[n * 16 : (n + 1) * 16] for n in range(parts)], axis=1)
+
+        def pair(first, second):
+            return jnp.concatenate([meta[first : first + 1], meta[second : second + 1]], axis=1)
+
+        target = pair(0, 1).astype(jnp.int32)
+        chosen = iota((shards, hits), 0) == target
+        onehot = chosen.astype(jnp.float32).astype(jnp.bfloat16)
+        rank = jnp.sum(jnp.where(chosen, dot(onehot, before), 0.0), axis=0, keepdims=True)
+        rank_i = rank.astype(jnp.int32)
+        slot = target * STRIDE + rank_i
+        place = jnp.where((at == slot[:, :samples]) | (at == slot[:, samples:]), 1.0, 0.0).astype(jnp.bfloat16)
+        packed = dot(place, feat_ref[step_no])
+        other = jnp.concatenate([rank[:, samples:], rank[:, :samples]], axis=1)
+        values = [pair(2 + n, 6 + n) for n in range(4)] + [pair(1, 0), other, pair(10, 10), jnp.ones_like(rank)]
+        lane_of = iota((STRIDE, hits), 0) == rank_i
+        spread = jnp.concatenate([jnp.where(lane_of, value, 0.0) for value in values], axis=0)
+        rows = dot(onehot, spread.astype(jnp.bfloat16), ((1,), (1,)))
+        packed = packed + dot(at_row, rows.astype(jnp.bfloat16))
+        out_ref[:, step_no] = packed.astype(jnp.bfloat16).reshape(shards, STRIDE, width)
+        slot_ref[step_no] = slot
 
 
 def pack(meta, feats, shards):
     steps, samples, width = feats.shape
-    return pl.pallas_call(
-        functools.partial(pack_kernel, shards),
-        grid=(steps,),
-        in_specs=[
-            pl.BlockSpec((1, 16, samples), lambda t: (t, 0, 0)),
-            pl.BlockSpec((1, samples, width), lambda t: (t, 0, 0)),
-        ],
-        out_specs=[
-            pl.BlockSpec((shards, 1, STRIDE, width), lambda t: (0, t, 0, 0)),
-            pl.BlockSpec((1, 1, 2 * samples), lambda t: (t, 0, 0)),
-        ],
-        out_shape=[
+    return call(
+        pack_kernel,
+        [meta, feats],
+        [
             jax.ShapeDtypeStruct((shards, steps, STRIDE, width), jnp.bfloat16),
             jax.ShapeDtypeStruct((steps, 1, 2 * samples), jnp.int32),
         ],
-        compiler_params=pltpu.CompilerParams(vmem_limit_bytes=VMEM_LIMIT),
-    )(meta, feats)
+    )
 
 
 def columns(got_ref, step_no):
@@ -162,16 +158,17 @@
     return jnp.sum(jnp.where(here, row, 0.0), axis=1, keepdims=True)
 
 
-def forward(weighted, counts, feats, mine_ref):
+def forward(weighted, counts, feats, mine_ref, sent_ref):
     width = feats.shape[1]
     products = halves(dot(counts, weighted)) * feats.astype(jnp.float32)
     same = iota((128, 128), 0) == iota((128, 128), 1)
     mine = []
-    for k in range(mine_ref.shape[1]):
+    for k in range(mine_ref.shape[0]):
         column = jnp.sum(products[k * 128 : (k + 1) * 128], axis=1, keepdims=True) * width**-0.5
         mine.append(jnp.sum(jnp.where(same, column, 0.0), axis=0, keepdims=True))
     mine = jnp.concatenate(mine, axis=0)
-    mine_ref[...] = jnp.broadcast_to(mine[None], mine_ref.shape)
+    mine_ref[...] = mine
+    sent_ref[...] = jnp.broadcast_to(mine[None], sent_ref.shape)
 
 
 def weigh_kernel(carried_ref, weighted_ref):
@@ -179,9 +176,9 @@
     weighted_ref[...] = wide(weight_column(carried_ref, 0, act_rows) * carried_ref[:act_rows, :])
 
 
-def first_kernel(weighted_ref, got_ref, mine_ref):
+def first_kernel(weighted_ref, got_ref, mine_ref, sent_ref):
     counts = lookups(columns(got_ref, 0), weighted_ref.shape[0]).astype(jnp.bfloat16)
-    forward(weighted_ref[...], counts, got_ref[:, 0].reshape(-1, got_ref.shape[3]), mine_ref)
+    forward(weighted_ref[...], counts, got_ref[:, 0].reshape(-1, got_ref.shape[3]), mine_ref, sent_ref)
 
 
 def gradient(step_no, table_ref, mine_ref, cols_ref, got_ref, turned_ref, grad_ref):
@@ -196,7 +193,7 @@
         wanted = (shard == cols[:, 4:5]).astype(jnp.float32).astype(jnp.bfloat16)
         found = halves(dot(wanted, wide(table_ref[:, k, :])))
         partner = jnp.where(lane == base + cols[:, 5:6].astype(jnp.int32), found, 0.0)
-        own = jnp.where(lane == row, mine_ref[0, k : k + 1, :], 0.0)
+        own = jnp.where(lane == row, mine_ref[k : k + 1, :], 0.0)
         error = jax.nn.sigmoid(jnp.sum(partner + own, axis=1, keepdims=True)) - cols[:, 6:7]
         part = error * feats[k * 128 : (k + 1) * 128].astype(jnp.float32) * width**-0.5
         grad_ref[k * 128 : (k + 1) * 128, :] = part.astype(jnp.bfloat16)
@@ -205,14 +202,14 @@
 
 def step_kernel(
     step_no, carried_ref, rows_ref, table_ref, mine_ref, cols_ref, got_ref, turned_ref, next_counts_ref,
-    new_rows_ref, new_mine_ref, grad_ref,
+    new_rows_ref, new_mine_ref, sent_ref, grad_ref,
 ):
     act_rows, width = new_rows_ref.shape
     row_grad = gradient(step_no, table_ref, mine_ref, cols_ref, got_ref, turned_ref, grad_ref)
     rows = rows_ref[:act_rows, :] - step_rate * (weight_column(carried_ref, step_no, act_rows) * row_grad)
     new_rows_ref[...] = rows
     weighted = weight_column(carried_ref, step_no + 1, act_rows) * rows
-    forward(wide(weighted), next_counts_ref[...], got_ref[:, step_no + 1].reshape(-1, width), new_mine_ref)
+    forward(wide(weighted), next_counts_ref[...], got_ref[:, step_no + 1].reshape(-1, width), new_mine_ref, sent_ref)
 
 
 def last_kernel(
@@ -230,7 +227,7 @@
     back_ref[act_rows:, :] = jnp.concatenate(terms + [jnp.zeros_like(logits)], axis=0).astype(jnp.bfloat16)
 
 
-def call(kernel, args, outs, scratch=(), cost=None):
+def call(kernel, args, outs, scratch=()):
     smem, vmem = (pl.BlockSpec(memory_space=space) for space in (pltpu.SMEM, pltpu.VMEM))
     return pl.pallas_call(
         kernel,
@@ -239,7 +236,6 @@
         out_shape=list(outs),
         scratch_shapes=list(scratch),
         compiler_params=pltpu.CompilerParams(vmem_limit_bytes=VMEM_LIMIT),
-        cost_estimate=cost,
     )(*args)
 
 
@@ -299,47 +295,50 @@
     within = jnp.arange(BLK, dtype=jnp.int32)
 
     there = functools.partial(lax.ppermute, axis_name=HOME, perm=turn)
+    feats = there(dense_feat[0])
     looked = (lookup_slot[0] * BLK + lookup_offset[0] + 1).transpose(0, 2, 3, 1).reshape(steps, 8, samples)
-    meta = jnp.concatenate(
-        [
-            hit_shards[0].transpose(0, 2, 1),
-            looked,
-            labels[0][:, None, :],
-            jnp.zeros((steps, 5, samples), jnp.int32),
-        ],
-        axis=1,
-    ).astype(jnp.bfloat16)
-    meta = there(meta)
-    feats = there(dense_feat[0])
-    meta, blocks = lax.optimization_barrier((meta, active_blocks))
-    my_blocks = blocks[lax.axis_index(("a1", "a0", "b", "c")), 0]
+    meta = [
+        hit_shards[0].transpose(0, 2, 1),
+        looked,
+        labels[0][:, None, :],
+        jnp.zeros((steps, 5, samples), jnp.int32),
+    ]
+    meta = jnp.concatenate(meta, axis=1).reshape(steps, 16, samples // width, width).transpose(0, 2, 1, 3)
+    meta = meta.reshape(-1, width).astype(jnp.bfloat16)
+    my_blocks = active_blocks[lax.axis_index(("a1", "a0", "b", "c")), 0]
     local_index = (my_blocks[:, None] * BLK + within[None, :]).reshape(-1)
     weights = jnp.pad(block_weight[0, :, 0], ((0, 8 - steps), (0, width - active)))
-    carried = there(jnp.concatenate([emb_table[local_index], weights], axis=0))
+    rows = jnp.concatenate([emb_table[local_index], weights], axis=0)
+    high = lax.reduce_precision(rows, 8, 7)
+    rest = there(jnp.concatenate([meta, high.astype(jnp.bfloat16), (rows - high).astype(jnp.bfloat16)], axis=0))
+    feats, rest = lax.optimization_barrier((feats, rest))
+    meta, high, low = jnp.split(rest, [meta.shape[0], meta.shape[0] + rows.shape[0]])
+    carried = high.astype(jnp.float32) + low.astype(jnp.float32)
 
     packed, slot_of = pack(meta, feats, shards)
     got = lax.all_to_all(packed, GROUP, 0, 0, tiled=True)
 
     logit_rows = steps * samples // 128
     rows_like = jax.ShapeDtypeStruct((act_rows, width), jnp.float32)
-    mine_like = jax.ShapeDtypeStruct((shards, slots // 128, 128), jnp.float32)
+    mine_like = jax.ShapeDtypeStruct((slots // 128, 128), jnp.float32)
+    sent_like = jax.ShapeDtypeStruct((shards, slots // 128, 128), jnp.float32)
     back_like = jax.ShapeDtypeStruct((act_rows + 4 * logit_rows, width), jnp.bfloat16)
     scratch = [pltpu.VMEM((slots, width), jnp.bfloat16)]
     me = lax.axis_index(GROUP)[None]
     rows = carried
     weighted_like = jax.ShapeDtypeStruct((act_rows, 2 * width), jnp.bfloat16)
-    (weighted,) = call(weigh_kernel, [carried], [weighted_like], cost=COVER)
-    (mine,) = call(first_kernel, [weighted, got], [mine_like])
+    (weighted,) = call(weigh_kernel, [carried], [weighted_like])
+    mine, sent = call(first_kernel, [weighted, got], [mine_like, sent_like])
     table, known = None, []
     for t in range(steps):
         turned, cols, *more = prep(me, slot_of, got, table, t, act_rows)
         known += more[1:] if t + 1 < steps else more
-        table = lax.all_to_all(mine, GROUP, 0, 0, tiled=True)
+        table = lax.all_to_all(sent, GROUP, 0, 0, tiled=True)
         if t + 1 < steps:
-            rows, mine = call(
+            rows, mine, sent = call(
                 functools.partial(step_kernel, t),
                 [carried, rows, table, mine, cols, got, turned, more[0]],
-                [rows_like, mine_like],
+                [rows_like, mine_like, sent_like],
                 scratch,
             )
         else:

time: 231 us -> 225 us (0.974)
  starting transfers between devices: 113 us -> 88.1 us
  waiting for transfers between devices: 76.8 us -> 99.4 us
  Pallas kernels: 31.3 us -> 27 us
    ppermute x2 -> x1, starting transfers between devices: 41.2 us -> 1.92 us  [body(): there(jnp.concatenate([meta, high.astype(jnp.bfloat16), (rows - high).ast...]
    ppermute x1, starting transfers between devices: 1.92 us -> 23.5 us  [body(): feats = there(dense_feat[0])]
    ppermute x2 -> x1, waiting for transfers between devices: 0.01 us -> 20.2 us  [body(): there(jnp.concatenate([meta, high.astype(jnp.bfloat16), (rows - high).ast...]
    all_to_all x1, starting transfers between devices: 28.8 us -> 24 us  [body(): got = lax.all_to_all(packed, GROUP, 0, 0, tiled=True)]
    pallas_call x1 -> x0, Pallas kernels: 3.81 us -> none  [pack(): pl.pallas_call(functools.partial(pack_kernel, shards), grid=(steps,), in_...]
    pallas_call x10 -> x11, Pallas kernels: 22.8 us -> 22.3 us  [call(): pl.pallas_call(kernel, in_specs=[smem if arg.size == 1 else vmem for arg...]
  transfers between devices with their start and end apart: 14 -> 13, of which waited for: 9 -> 10; matrix products, arithmetic and copies ran while one was open for 2% -> 3% of each run, Pallas kernels for 5% -> 3%
where the time goes in v5:
time: 225 us; the launch traced here: 224 us
  waiting for transfers between devices  99.4 us (44%)
  starting transfers between devices  88.1 us (39%)
  Pallas kernels  27 us (12%)
  other arithmetic  4.41 us (2%)
  local copies, waits for them, and re-layouts  3.83 us (2%)
    all_to_all x4, waiting for transfers between devices, body(): table = lax.all_to_all(sent, GROUP, 0, 0, tiled=True)  31.3 us
    all_to_all x1, starting transfers between devices, body(): got = lax.all_to_all(packed, GROUP, 0, 0, tiled=True)  24 us
    ppermute x1, starting transfers between devices, body(): feats = there(dense_feat[0])  23.5 us
    pallas_call x11, Pallas kernels, call(): pl.pallas_call(kernel, in_specs=[smem if arg.size == 1 else vmem for arg...  22.3 us
    all_to_all x4, starting transfers between devices, body(): table = lax.all_to_all(sent, GROUP, 0, 0, tiled=True)  20.6 us
    ppermute x1, waiting for transfers between devices, body(): there(jnp.concatenate([meta, high.astype(jnp.bfloat16), (rows - high).ast...  20.2 us
    ppermute x1, waiting for transfers between devices, body(): back = there(back)  18.7 us
    all_to_all x1, waiting for transfers between devices, body(): got = lax.all_to_all(packed, GROUP, 0, 0, tiled=True)  16.9 us
  transfers between devices with their start and end apart: 13, of which 10 were waited for; matrix products, arithmetic and copies ran while one was open for 3% of the time, Pallas kernels for 3%

profile of v5, /device:TPU:1, one launch (start us, length us, event | category | flops | bytes accessed | tf_op | source)
XLA Modules:
  0.0 223.8 jit_solution(12983899344729252424)
XLA Ops:
  0.6 23.5 %collective-permute-start = (bf16[4,256,128]{2,1,0:T(8,128)(2,1)}, bf16[4,256,128]{2,1,0:T(8,128)(2,1)S(1)}, u32[]{:S(2)}, u32[]{:S(2)}) collective-permute-start(bf16[4,256,128]{2,1,0:T(8,128)(2,1)} %bitcast.34), channel_id=1, source_target_pairs={{0,512},{4,576},{8,640},{12,704},{64,516},{68,580},{72,644},{76,70... | collective-permute-start | bytes 786440 | tf_op jit(solution)/shard_map/ppermute | solution.py:298
  24.1 0.7 multiply_bitcast_fusion
  24.8 0.1 iota_add_fusion
  24.8 0.1 add.122
  24.9 0.7 convert.20
  25.7 0.8 fusion.1
  26.5 0.7 convert_bitcast_fusion
  27.2 2.3 %gather_fusion = f32[256,128]{1,0:T(8,128)S(1)} fusion(f32[4096,128]{1,0:T(8,128)} %table_ref.1, s32[1024]{0:T(1024)S(1)} %pad_clamp_fusion), kind=kCustom, calls=%fused_computation | custom fusion | bytes 263168 | tf_op jit(solution)/shard_map/gather | solution.py:311
  29.5 0.7 reduce-precision_convert_fusion
  30.2 0.1 pad.18.clone
  30.3 0.1 maximum_maximum_fusion
  30.4 1.9 collective-permute-start.1
  32.3 20.2 %collective-permute-done.1 = bf16[656,128]{1,0:T(8,128)(2,1)S(1)} collective-permute-done((bf16[656,128]{1,0:T(8,128)(2,1)S(1)}, bf16[656,128]{1,0:T(8,128)(2,1)S(1)}, u32[]{:S(2)}, u32[]{:S(2)}) %collective-permute-start.1) | collective-permute-done | bytes 167968 | tf_op jit(solution)/shard_map/ppermute | solution.py:313
  52.5 0.0 collective-permute-done.feat_ref
  52.5 3.3 %shard_map.95 = (bf16[64,4,16,128]{3,2,1,0:T(8,128)(2,1)}, s32[4,1,512]{2,1,0:T(1,128)S(1)}) custom-call(bf16[128,128]{1,0:T(8,128)(2,1)S(1)} %split.9.meta_ref, bf16[4,256,128]{2,1,0:T(8,128)(2,1)S(1)} %collective-permute-done.feat_ref), custom_call_target="tpu_custom_call" | custom-call | tf_op jit(solution)/shard_map/pallas_call | solution.py:232
  55.8 24.0 %all-to-all-start = ((bf16[64,4,16,128]{3,2,1,0:T(8,128)(2,1)}), bf16[64,4,16,128]{3,2,1,0:T(8,128)(2,1)S(1)}, u32[]{:S(2)}, u32[]{:S(2)}) async-start(bf16[64,4,16,128]{3,2,1,0:T(8,128)(2,1)} %get-tuple-element.34), calls=%async_computation | async-start | bytes 2097152 | tf_op jit(solution)/shard_map/all_to_all | solution.py:319
  79.8 0.1 shard_map.96.weighted_ref
  79.9 16.9 %all-to-all-done.got_ref = bf16[64,4,16,128]{3,2,1,0:T(8,128)(2,1)S(1)} async-done(((bf16[64,4,16,128]{3,2,1,0:T(8,128)(2,1)}), bf16[64,4,16,128]{3,2,1,0:T(8,128)(2,1)S(1)}, u32[]{:S(2)}, u32[]{:S(2)}) %all-to-all-start) | async-done | bytes 1048608 | tf_op jit(solution)/shard_map/all_to_all | solution.py:319
  96.8 1.8 shard_map.97
  98.7 5.6 %all-to-all-start.1 = ((f32[64,8,128]{2,1,0:T(8,128)}), f32[64,8,128]{2,1,0:T(8,128)S(1)}, u32[]{:S(2)}, u32[]{:S(2)}) async-start(f32[64,8,128]{2,1,0:T(8,128)} %get-tuple-element.35), calls=%async_computation.1 | async-start | bytes 524288 | tf_op jit(solution)/shard_map/all_to_all | solution.py:336
  104.2 1.6 shard_map.98
  105.8 7.9 %all-to-all-done.1.table_ref.refs_0_ = f32[64,8,128]{2,1,0:T(8,128)S(1)} async-done(((f32[64,8,128]{2,1,0:T(8,128)}), f32[64,8,128]{2,1,0:T(8,128)S(1)}, u32[]{:S(2)}, u32[]{:S(2)}) %all-to-all-start.1) | async-done | bytes 262176 | tf_op jit(solution)/shard_map/all_to_all | solution.py:336
  113.8 2.8 %shard_map.99 = (f32[256,128]{1,0:T(8,128)S(1)}, f32[8,128]{1,0:T(8,128)S(1)}, f32[64,8,128]{2,1,0:T(8,128)}) custom-call(f32[264,128]{1,0:T(8,128)S(1)} %convert_add_fusion.carried_ref.rows_ref, f32[264,128]{1,0:T(8,128)S(1)} %convert_add_fusion.carried_ref.rows_ref, f32[64,8,128]{2,1,0:T(8,128)S(1)} %all-to-all-done.1.table_ref.refs_0_, ...), custom_call_target="tpu_custom_call" | custom-call | tf_op jit(solution)/shard_map/pallas_call | solution.py:232
  116.5 5.0 %all-to-all-start.2 = ((f32[64,8,128]{2,1,0:T(8,128)}), f32[64,8,128]{2,1,0:T(8,128)S(1)}, u32[]{:S(2)}, u32[]{:S(2)}) async-start(f32[64,8,128]{2,1,0:T(8,128)} %get-tuple-element.41), calls=%async_computation.2 | async-start | bytes 524288 | tf_op jit(solution)/shard_map/all_to_all | solution.py:336
  121.6 1.9 shard_map.100
  123.5 7.6 %all-to-all-done.2.table_ref.refs_0_ = f32[64,8,128]{2,1,0:T(8,128)S(1)} async-done(((f32[64,8,128]{2,1,0:T(8,128)}), f32[64,8,128]{2,1,0:T(8,128)S(1)}, u32[]{:S(2)}, u32[]{:S(2)}) %all-to-all-start.2) | async-done | bytes 262176 | tf_op jit(solution)/shard_map/all_to_all | solution.py:336
  131.1 2.8 %shard_map.101 = (f32[256,128]{1,0:T(8,128)S(1)}, f32[8,128]{1,0:T(8,128)S(1)}, f32[64,8,128]{2,1,0:T(8,128)}) custom-call(f32[264,128]{1,0:T(8,128)S(1)} %convert_add_fusion.carried_ref.rows_ref, f32[256,128]{1,0:T(8,128)S(1)} %get-tuple-element.40.rows_ref, f32[64,8,128]{2,1,0:T(8,128)S(1)} %all-to-all-done.2.table_ref.refs_0_, ...), custom_call_target="tpu_custom_call" | custom-call | tf_op jit(solution)/shard_map/pallas_call | solution.py:232
  133.9 5.0 %all-to-all-start.3 = ((f32[64,8,128]{2,1,0:T(8,128)}), f32[64,8,128]{2,1,0:T(8,128)S(1)}, u32[]{:S(2)}, u32[]{:S(2)}) async-start(f32[64,8,128]{2,1,0:T(8,128)} %get-tuple-element.47), calls=%async_computation.3 | async-start | bytes 524288 | tf_op jit(solution)/shard_map/all_to_all | solution.py:336
  138.9 2.0 shard_map.102
  140.9 7.6 %all-to-all-done.3.table_ref.refs_0_ = f32[64,8,128]{2,1,0:T(8,128)S(1)} async-done(((f32[64,8,128]{2,1,0:T(8,128)}), f32[64,8,128]{2,1,0:T(8,128)S(1)}, u32[]{:S(2)}, u32[]{:S(2)}) %all-to-all-start.3) | async-done | bytes 262176 | tf_op jit(solution)/shard_map/all_to_all | solution.py:336
  148.5 2.8 %shard_map.103 = (f32[256,128]{1,0:T(8,128)S(1)}, f32[8,128]{1,0:T(8,128)S(1)}, f32[64,8,128]{2,1,0:T(8,128)}) custom-call(f32[264,128]{1,0:T(8,128)S(1)} %convert_add_fusion.carried_ref.rows_ref, f32[256,128]{1,0:T(8,128)S(1)} %get-tuple-element.46.rows_ref, f32[64,8,128]{2,1,0:T(8,128)S(1)} %all-to-all-done.3.table_ref.refs_0_, ...), custom_call_target="tpu_custom_call" | custom-call | tf_op jit(solution)/shard_map/pallas_call | solution.py:232
  151.2 5.0 %all-to-all-start.4 = ((f32[64,8,128]{2,1,0:T(8,128)}), f32[64,8,128]{2,1,0:T(8,128)S(1)}, u32[]{:S(2)}, u32[]{:S(2)}) async-start(f32[64,8,128]{2,1,0:T(8,128)} %get-tuple-element.53), calls=%async_computation.4 | async-start | bytes 524288 | tf_op jit(solution)/shard_map/all_to_all | solution.py:336
  156.3 1.3 shard_map.104
  157.5 8.3 %all-to-all-done.4.table_ref = f32[64,8,128]{2,1,0:T(8,128)S(1)} async-done(((f32[64,8,128]{2,1,0:T(8,128)}), f32[64,8,128]{2,1,0:T(8,128)S(1)}, u32[]{:S(2)}, u32[]{:S(2)}) %all-to-all-start.4) | async-done | bytes 262176 | tf_op jit(solution)/shard_map/all_to_all | solution.py:336
  165.8 2.0 shard_map.105
  167.8 1.9 collective-permute-start.2
  169.7 18.7 %collective-permute-done.2 = bf16[288,128]{1,0:T(8,128)(2,1)S(1)} collective-permute-done((bf16[288,128]{1,0:T(8,128)(2,1)S(1)}, bf16[288,128]{1,0:T(8,128)(2,1)S(1)}, u32[]{:S(2)}, u32[]{:S(2)}) %collective-permute-start.2) | collective-permute-done | bytes 73760 | tf_op jit(solution)/shard_map/ppermute | solution.py:352
  188.4 1.9 collective-permute-start.3
  190.3 7.1 %collective-permute-done.3 = bf16[256,128]{1,0:T(8,128)(2,1)S(1)} collective-permute-done((bf16[256,128]{1,0:T(8,128)(2,1)S(1)}, bf16[256,128]{1,0:T(8,128)(2,1)S(1)}, u32[]{:S(2)}, u32[]{:S(2)}) %collective-permute-start.3) | collective-permute-done | bytes 65568 | tf_op jit(solution)/shard_map/ppermute | solution.py:356
  197.4 1.9 collective-permute-start.4
  199.4 4.7 %collective-permute-done.4 = bf16[512,128]{1,0:T(8,128)(2,1)S(1)} collective-permute-done((bf16[512,128]{1,0:T(8,128)(2,1)S(1)}, bf16[512,128]{1,0:T(8,128)(2,1)S(1)}, u32[]{:S(2)}, u32[]{:S(2)}) %collective-permute-start.4) | collective-permute-done | bytes 131104 | tf_op jit(solution)/shard_map/ppermute | solution.py:356
  204.1 0.0 copy-start
  204.1 1.9 collective-permute-start.5
  206.0 0.6 pad_add_fusion.here_ref
  206.6 6.7 %collective-permute-start.6 = (bf16[1024,128]{1,0:T(8,128)(2,1)S(1)}, bf16[1024,128]{1,0:T(8,128)(2,1)S(1)}, u32[]{:S(2)}, u32[]{:S(2)}) collective-permute-start(bf16[1024,128]{1,0:T(8,128)(2,1)S(1)} %pad_maximum_fusion), channel_id=1, source_target_pairs={{0,64},{64,0},{1,65},{65,1},{2,66},{66,2},{3,67},{67,3},{4,68},{68... | collective-permute-start | bytes 786440 | tf_op jit(solution)/shard_map/ppermute | solution.py:358
  213.4 0.0 collective-permute-done.5
  213.4 0.0 copy-start.1
  213.4 3.7 %collective-permute-start.7 = (bf16[1024,128]{1,0:T(8,128)(2,1)S(1)}, bf16[1024,128]{1,0:T(8,128)(2,1)S(1)}, u32[]{:S(2)}, u32[]{:S(2)}) collective-permute-start(bf16[1024,128]{1,0:T(8,128)(2,1)S(1)} %collective-permute-done.5), channel_id=1, source_target_pairs={{0,64},{64,0},{1,65},{65,1},{2,66},{66,2},{3,67},{67,3},{4,68},{68... | collective-permute-start | bytes 786440 | tf_op jit(solution)/shard_map/ppermute | solution.py:358
  217.1 0.6 add.128
  217.7 0.0 collective-permute-done.6
  217.7 0.0 copy-start.2
  217.7 0.5 collective-permute-done.7
  218.2 0.0 copy-start.3
  218.2 0.0 copy-done
  218.2 0.0 copy-done.1
  218.2 0.2 copy-done.2
  218.4 0.5 copy-done.3
  218.9 4.7 %shard_map.106 = f32[4096,128]{1,0:T(8,128)} custom-call(s32[16,16]{1,0:T(8,128)} %bitcast.31, s32[2]{0:T(128)} %pad_add_fusion.here_ref, f32[4096,128]{1,0:T(8,128)} %table_ref.1, bf16[4,256,128]{2,1,0:T(8,128)(2,1)} %bitcast.26, bf16[4,256,128]{2,1,0:T(8,128)(2,1)} %bitcast.27, bf16[4,256,128]{2,1,0:T(8,128)(2,1)} %bitcast.28, bf16[4,256,128]{2,1,0:T(8,128)(2,1)} %bitcast.29), custom_call_target="tpu_custom_call" | custom-call | tf_op jit(solution)/shard_map/pallas_call | solution.py:277
  (14 shorter events, 0.1 us)
Async XLA Ops:
  0.6 51.9 %collective-permute-start = (bf16[4,256,128]{2,1,0:T(8,128)(2,1)}, bf16[4,256,128]{2,1,0:T(8,128)(2,1)S(1)}, u32[]{:S(2)}, u32[]{:S(2)}) collective-permute-start(bf16[4,256,128]{2,1,0:T(8,128)(2,1)} %bitcast.34), channel_id=1, source_target_pairs={{0,512},{4,576},{8,640},{12,704},{64,516},{68,580},{72,644},{76,70... | collective-permute-start | bytes 786440 | tf_op jit(solution)/shard_map/ppermute | solution.py:298
  30.4 22.1 %collective-permute-start.1 = (bf16[656,128]{1,0:T(8,128)(2,1)S(1)}, bf16[656,128]{1,0:T(8,128)(2,1)S(1)}, u32[]{:S(2)}, u32[]{:S(2)}) collective-permute-start(bf16[656,128]{1,0:T(8,128)(2,1)S(1)} %pad_maximum_fusion.1), channel_id=1, source_target_pairs={{0,512},{4,576},{8,640},{12,704},{64,516},{68,580},{72,644},{76,70... | collective-permute-start | bytes 503816 | tf_op jit(solution)/shard_map/ppermute | solution.py:313
  55.8 41.0 %all-to-all-start = ((bf16[64,4,16,128]{3,2,1,0:T(8,128)(2,1)}), bf16[64,4,16,128]{3,2,1,0:T(8,128)(2,1)S(1)}, u32[]{:S(2)}, u32[]{:S(2)}) async-start(bf16[64,4,16,128]{3,2,1,0:T(8,128)(2,1)} %get-tuple-element.34), calls=%async_computation | async-start | bytes 2097152 | tf_op jit(solution)/shard_map/all_to_all | solution.py:319
  98.7 15.1 %all-to-all-start.1 = ((f32[64,8,128]{2,1,0:T(8,128)}), f32[64,8,128]{2,1,0:T(8,128)S(1)}, u32[]{:S(2)}, u32[]{:S(2)}) async-start(f32[64,8,128]{2,1,0:T(8,128)} %get-tuple-element.35), calls=%async_computation.1 | async-start | bytes 524288 | tf_op jit(solution)/shard_map/all_to_all | solution.py:336
  116.5 14.6 %all-to-all-start.2 = ((f32[64,8,128]{2,1,0:T(8,128)}), f32[64,8,128]{2,1,0:T(8,128)S(1)}, u32[]{:S(2)}, u32[]{:S(2)}) async-start(f32[64,8,128]{2,1,0:T(8,128)} %get-tuple-element.41), calls=%async_computation.2 | async-start | bytes 524288 | tf_op jit(solution)/shard_map/all_to_all | solution.py:336
  133.9 14.6 %all-to-all-start.3 = ((f32[64,8,128]{2,1,0:T(8,128)}), f32[64,8,128]{2,1,0:T(8,128)S(1)}, u32[]{:S(2)}, u32[]{:S(2)}) async-start(f32[64,8,128]{2,1,0:T(8,128)} %get-tuple-element.47), calls=%async_computation.3 | async-start | bytes 524288 | tf_op jit(solution)/shard_map/all_to_all | solution.py:336
  151.2 14.6 %all-to-all-start.4 = ((f32[64,8,128]{2,1,0:T(8,128)}), f32[64,8,128]{2,1,0:T(8,128)S(1)}, u32[]{:S(2)}, u32[]{:S(2)}) async-start(f32[64,8,128]{2,1,0:T(8,128)} %get-tuple-element.53), calls=%async_computation.4 | async-start | bytes 524288 | tf_op jit(solution)/shard_map/all_to_all | solution.py:336
  167.8 20.6 %collective-permute-start.2 = (bf16[288,128]{1,0:T(8,128)(2,1)S(1)}, bf16[288,128]{1,0:T(8,128)(2,1)S(1)}, u32[]{:S(2)}, u32[]{:S(2)}) collective-permute-start(bf16[288,128]{1,0:T(8,128)(2,1)S(1)} %shard_map.105), channel_id=1, source_target_pairs={{0,512},{4,576},{8,640},{12,704},{64,516},{68,580},{72,644},{76,70... | collective-permute-start | bytes 221192 | tf_op jit(solution)/shard_map/ppermute | solution.py:352
  188.4 9.0 %collective-permute-start.3 = (bf16[256,128]{1,0:T(8,128)(2,1)S(1)}, bf16[256,128]{1,0:T(8,128)(2,1)S(1)}, u32[]{:S(2)}, u32[]{:S(2)}) collective-permute-start(bf16[256,128]{1,0:T(8,128)(2,1)S(1)} %slice.25), channel_id=1, source_target_pairs={{0,512},{512,0},{1,513},{513,1},{2,514},{514,2},{3,515},{515,3},{4... | collective-permute-start | bytes 196616 | tf_op jit(solution)/shard_map/ppermute | solution.py:356
  197.4 6.6 %collective-permute-start.4 = (bf16[512,128]{1,0:T(8,128)(2,1)S(1)}, bf16[512,128]{1,0:T(8,128)(2,1)S(1)}, u32[]{:S(2)}, u32[]{:S(2)}) collective-permute-start(bf16[512,128]{1,0:T(8,128)(2,1)S(1)} %pad_maximum_fusion.2), channel_id=1, source_target_pairs={{0,256},{256,0},{1,257},{257,1},{2,258},{258,2},{3,259},{259,3},{4... | collective-permute-start | bytes 393224 | tf_op jit(solution)/shard_map/ppermute | solution.py:356
  204.1 14.1 %copy-start = (bf16[1024,128]{1,0:T(8,128)(2,1)}, bf16[1024,128]{1,0:T(8,128)(2,1)S(1)}, u32[]{:S(2)}) copy-start(bf16[1024,128]{1,0:T(8,128)(2,1)S(1)} %pad_maximum_fusion) | copy-start | bytes 786436
  204.1 9.3 %collective-permute-start.5 = (bf16[1024,128]{1,0:T(8,128)(2,1)S(1)}, bf16[1024,128]{1,0:T(8,128)(2,1)S(1)}, u32[]{:S(2)}, u32[]{:S(2)}) collective-permute-start(bf16[1024,128]{1,0:T(8,128)(2,1)S(1)} %pad_maximum_fusion), channel_id=1, source_target_pairs={{0,128},{128,0},{1,129},{129,1},{2,130},{130,2},{3,131},{131,3},{4... | collective-permute-start | bytes 786440 | tf_op jit(solution)/shard_map/ppermute | solution.py:357
  206.6 11.1 %collective-permute-start.6 = (bf16[1024,128]{1,0:T(8,128)(2,1)S(1)}, bf16[1024,128]{1,0:T(8,128)(2,1)S(1)}, u32[]{:S(2)}, u32[]{:S(2)}) collective-permute-start(bf16[1024,128]{1,0:T(8,128)(2,1)S(1)} %pad_maximum_fusion), channel_id=1, source_target_pairs={{0,64},{64,0},{1,65},{65,1},{2,66},{66,2},{3,67},{67,3},{4,68},{68... | collective-permute-start | bytes 786440 | tf_op jit(solution)/shard_map/ppermute | solution.py:358
  213.4 4.8 %copy-start.1 = (bf16[1024,128]{1,0:T(8,128)(2,1)}, bf16[1024,128]{1,0:T(8,128)(2,1)S(1)}, u32[]{:S(2)}) copy-start(bf16[1024,128]{1,0:T(8,128)(2,1)S(1)} %collective-permute-done.5) | copy-start | bytes 786436
  213.4 4.8 %collective-permute-start.7 = (bf16[1024,128]{1,0:T(8,128)(2,1)S(1)}, bf16[1024,128]{1,0:T(8,128)(2,1)S(1)}, u32[]{:S(2)}, u32[]{:S(2)}) collective-permute-start(bf16[1024,128]{1,0:T(8,128)(2,1)S(1)} %collective-permute-done.5), channel_id=1, source_target_pairs={{0,64},{64,0},{1,65},{65,1},{2,66},{66,2},{3,67},{67,3},{4,68},{68... | collective-permute-start | bytes 786440 | tf_op jit(solution)/shard_map/ppermute | solution.py:358
  217.7 0.7 copy-start.2
  218.2 0.7 copy-start.3

commit v6 on v5

--- a/solution.py
+++ b/solution.py
@@ -12,7 +12,7 @@
 STRIDE = 16
 META = 12
 VMEM_LIMIT = 16 << 20
-MERGE_LIMIT = 60 << 20
+MERGE_LIMIT = 51 << 20
 
 step_rate = 1.0
 
@@ -52,13 +52,13 @@
     at = iota((shards * STRIDE, samples), 0)
     at_row = iota((shards * STRIDE, shards), 0) == iota((shards * STRIDE, shards), 1) * STRIDE + META
     at_row = at_row.astype(jnp.float32).astype(jnp.bfloat16)
+    meta = meta_ref[...].astype(jnp.float32)
     for step_no in range(steps):
-        parts = samples // width
-        lines = meta_ref[step_no * parts * 16 : (step_no + 1) * parts * 16, :].astype(jnp.float32)
-        meta = jnp.concatenate([lines[n * 16 : (n + 1) * 16] for n in range(parts)], axis=1)
 
         def pair(first, second):
-            return jnp.concatenate([meta[first : first + 1], meta[second : second + 1]], axis=1)
+            parts = samples // width
+            lines = [(value * steps + step_no) * parts + n for value in (first, second) for n in range(parts)]
+            return jnp.concatenate([meta[line : line + 1] for line in lines], axis=1)
 
         target = pair(0, 1).astype(jnp.int32)
         chosen = iota((shards, hits), 0) == target
@@ -273,7 +273,7 @@
 
 def merge(blocks, here, table, held):
     smem, hbm = (pl.BlockSpec(memory_space=space) for space in (pltpu.SMEM, pltpu.HBM))
-    whole = pl.BlockSpec(held[0].shape, lambda i: (0, 0, 0))
+    whole = pl.BlockSpec(memory_space=pltpu.VMEM)
     return pl.pallas_call(
         merge_kernel,
         grid=(1,),
@@ -296,24 +296,23 @@
 
     there = functools.partial(lax.ppermute, axis_name=HOME, perm=turn)
     feats = there(dense_feat[0])
-    looked = (lookup_slot[0] * BLK + lookup_offset[0] + 1).transpose(0, 2, 3, 1).reshape(steps, 8, samples)
-    meta = [
-        hit_shards[0].transpose(0, 2, 1),
-        looked,
-        labels[0][:, None, :],
-        jnp.zeros((steps, 5, samples), jnp.int32),
-    ]
-    meta = jnp.concatenate(meta, axis=1).reshape(steps, 16, samples // width, width).transpose(0, 2, 1, 3)
+    looked = (lookup_slot[0] * BLK + lookup_offset[0] + 1).transpose(2, 3, 0, 1).reshape(-1, steps, samples)
+    meta = jnp.concatenate([hit_shards[0].transpose(2, 0, 1), looked, labels[0][None]], axis=0)
     meta = meta.reshape(-1, width).astype(jnp.bfloat16)
     my_blocks = active_blocks[lax.axis_index(("a1", "a0", "b", "c")), 0]
     local_index = (my_blocks[:, None] * BLK + within[None, :]).reshape(-1)
-    weights = jnp.pad(block_weight[0, :, 0], ((0, 8 - steps), (0, width - active)))
-    rows = jnp.concatenate([emb_table[local_index], weights], axis=0)
-    high = lax.reduce_precision(rows, 8, 7)
-    rest = there(jnp.concatenate([meta, high.astype(jnp.bfloat16), (rows - high).astype(jnp.bfloat16)], axis=0))
+    weights = jnp.pad(block_weight[0, :, 0], ((0, 0), (0, width - active)))
+    parts = [meta]
+    for exact in (weights, emb_table[local_index]):
+        high = lax.reduce_precision(exact, 8, 7)
+        parts += [high.astype(jnp.bfloat16), (exact - high).astype(jnp.bfloat16)]
+    rest = there(jnp.concatenate(parts, axis=0))
     feats, rest = lax.optimization_barrier((feats, rest))
-    meta, high, low = jnp.split(rest, [meta.shape[0], meta.shape[0] + rows.shape[0]])
-    carried = high.astype(jnp.float32) + low.astype(jnp.float32)
+    ends = [sum(part.shape[0] for part in parts[: n + 1]) for n in range(len(parts) - 1)]
+    meta, *terms = [part.astype(jnp.float32) for part in jnp.split(rest, ends)]
+    meta = meta.astype(jnp.bfloat16)
+    weights = jnp.pad(terms[0] + terms[1], ((0, 8 - steps), (0, 0)))
+    carried = jnp.concatenate([terms[2] + terms[3], weights], axis=0)
 
     packed, slot_of = pack(meta, feats, shards)
     got = lax.all_to_all(packed, GROUP, 0, 0, tiled=True)

time: 225 us -> 223 us (level)
  transfers between devices with their start and end apart: 13 -> 13, of which waited for: 10 -> 11; matrix products, arithmetic and copies ran while one was open for 3% -> 3% of each run, Pallas kernels for 3% -> 3%
where the time goes in v6:
time: 223 us; the launch traced here: 222 us
  waiting for transfers between devices  100 us (45%)
  starting transfers between devices  87.4 us (39%)
  Pallas kernels  26.5 us (12%)
  other arithmetic  3.82 us (2%)
  local copies, waits for them, and re-layouts  3.12 us (1%)
    all_to_all x4, waiting for transfers between devices, body(): table = lax.all_to_all(sent, GROUP, 0, 0, tiled=True)  31.3 us
    all_to_all x1, starting transfers between devices, body(): got = lax.all_to_all(packed, GROUP, 0, 0, tiled=True)  23.5 us
    ppermute x1, starting transfers between devices, body(): feats = there(dense_feat[0])  23.5 us
    pallas_call x11, Pallas kernels, call(): pl.pallas_call(kernel, in_specs=[smem if arg.size == 1 else vmem for arg...  22.3 us
    all_to_all x4, starting transfers between devices, body(): table = lax.all_to_all(sent, GROUP, 0, 0, tiled=True)  20.7 us
    ppermute x1, waiting for transfers between devices, body(): back = there(back)  19.9 us
    ppermute x1, waiting for transfers between devices, body(): rest = there(jnp.concatenate(parts, axis=0))  19.4 us
    all_to_all x1, waiting for transfers between devices, body(): got = lax.all_to_all(packed, GROUP, 0, 0, tiled=True)  16.9 us
  transfers between devices with their start and end apart: 13, of which 11 were waited for; matrix products, arithmetic and copies ran while one was open for 3% of the time, Pallas kernels for 3%

profile of v6, /device:TPU:1, one launch (start us, length us, event | category | flops | bytes accessed | tf_op | source)
XLA Modules:
  0.0 222.0 jit_solution(11090415491823809225)
XLA Ops:
  0.6 23.5 %collective-permute-start = (bf16[4,256,128]{2,1,0:T(8,128)(2,1)}, bf16[4,256,128]{2,1,0:T(8,128)(2,1)S(1)}, u32[]{:S(2)}, u32[]{:S(2)}) collective-permute-start(bf16[4,256,128]{2,1,0:T(8,128)(2,1)} %bitcast.30), channel_id=1, source_target_pairs={{0,512},{4,576},{8,640},{12,704},{64,516},{68,580},{72,644},{76,70... | collective-permute-start | bytes 786440 | tf_op jit(solution)/shard_map/ppermute | solution.py:298
  24.1 0.7 convert.16
  24.8 0.8 fusion.1
  25.6 0.7 convert_bitcast_fusion
  26.4 0.7 multiply_bitcast_fusion
  27.0 0.1 iota_add_fusion
  27.1 0.1 add.127
  27.2 2.3 %gather_fusion = f32[256,128]{1,0:T(8,128)S(1)} fusion(f32[4096,128]{1,0:T(8,128)} %table_ref.1, s32[1024]{0:T(1024)S(1)} %pad_clamp_fusion), kind=kCustom, calls=%fused_computation | custom fusion | bytes 263168 | tf_op jit(solution)/shard_map/gather | solution.py:306
  29.6 0.7 fusion.2
  30.3 0.1 concatenate.18
  30.3 1.9 collective-permute-start.1
  32.3 19.4 %collective-permute-done.1 = bf16[608,128]{1,0:T(8,128)(2,1)S(1)} collective-permute-done((bf16[608,128]{1,0:T(8,128)(2,1)S(1)}, bf16[608,128]{1,0:T(8,128)(2,1)S(1)}, u32[]{:S(2)}, u32[]{:S(2)}) %collective-permute-start.1) | collective-permute-done | bytes 155680 | tf_op jit(solution)/shard_map/ppermute | solution.py:309
  51.7 0.0 collective-permute-done.feat_ref
  51.7 3.3 %shard_map.95 = (bf16[64,4,16,128]{3,2,1,0:T(8,128)(2,1)}, s32[4,1,512]{2,1,0:T(1,128)S(1)}) custom-call(bf16[88,128]{1,0:T(8,128)(2,1)S(1)} %split.15.meta_ref, bf16[4,256,128]{2,1,0:T(8,128)(2,1)S(1)} %collective-permute-done.feat_ref), custom_call_target="tpu_custom_call" | custom-call | tf_op jit(solution)/shard_map/pallas_call | solution.py:232
  55.0 23.5 %all-to-all-start = ((bf16[64,4,16,128]{3,2,1,0:T(8,128)(2,1)}), bf16[64,4,16,128]{3,2,1,0:T(8,128)(2,1)S(1)}, u32[]{:S(2)}, u32[]{:S(2)}) async-start(bf16[64,4,16,128]{3,2,1,0:T(8,128)(2,1)} %get-tuple-element.34), calls=%async_computation | async-start | bytes 2097152 | tf_op jit(solution)/shard_map/all_to_all | solution.py:318
  78.5 0.1 shard_map.96.weighted_ref
  78.6 16.9 %all-to-all-done.got_ref = bf16[64,4,16,128]{3,2,1,0:T(8,128)(2,1)S(1)} async-done(((bf16[64,4,16,128]{3,2,1,0:T(8,128)(2,1)}), bf16[64,4,16,128]{3,2,1,0:T(8,128)(2,1)S(1)}, u32[]{:S(2)}, u32[]{:S(2)}) %all-to-all-start) | async-done | bytes 1048608 | tf_op jit(solution)/shard_map/all_to_all | solution.py:318
  95.5 1.8 shard_map.97
  97.3 5.6 %all-to-all-start.1 = ((f32[64,8,128]{2,1,0:T(8,128)}), f32[64,8,128]{2,1,0:T(8,128)S(1)}, u32[]{:S(2)}, u32[]{:S(2)}) async-start(f32[64,8,128]{2,1,0:T(8,128)} %get-tuple-element.35), calls=%async_computation.1 | async-start | bytes 524288 | tf_op jit(solution)/shard_map/all_to_all | solution.py:335
  102.9 1.6 shard_map.98
  104.5 7.9 %all-to-all-done.1.table_ref.refs_0_ = f32[64,8,128]{2,1,0:T(8,128)S(1)} async-done(((f32[64,8,128]{2,1,0:T(8,128)}), f32[64,8,128]{2,1,0:T(8,128)S(1)}, u32[]{:S(2)}, u32[]{:S(2)}) %all-to-all-start.1) | async-done | bytes 262176 | tf_op jit(solution)/shard_map/all_to_all | solution.py:335
  112.4 2.8 %shard_map.99 = (f32[256,128]{1,0:T(8,128)S(1)}, f32[8,128]{1,0:T(8,128)S(1)}, f32[64,8,128]{2,1,0:T(8,128)}) custom-call(f32[264,128]{1,0:T(8,128)S(1)} %select_maximum_fusion.carried_ref.rows_ref, f32[264,128]{1,0:T(8,128)S(1)} %select_maximum_fusion.carried_ref.rows_ref, f32[64,8,128]{2,1,0:T(8,128)S(1)} %all-to-all-done.1.table_ref.refs_0_, ...), custom_call_target="tpu_custom_call" | custom-call | tf_op jit(solution)/shard_map/pallas_call | solution.py:232
  115.2 5.0 %all-to-all-start.2 = ((f32[64,8,128]{2,1,0:T(8,128)}), f32[64,8,128]{2,1,0:T(8,128)S(1)}, u32[]{:S(2)}, u32[]{:S(2)}) async-start(f32[64,8,128]{2,1,0:T(8,128)} %get-tuple-element.41), calls=%async_computation.2 | async-start | bytes 524288 | tf_op jit(solution)/shard_map/all_to_all | solution.py:335
  120.3 2.0 shard_map.100
  122.2 7.6 %all-to-all-done.2.table_ref.refs_0_ = f32[64,8,128]{2,1,0:T(8,128)S(1)} async-done(((f32[64,8,128]{2,1,0:T(8,128)}), f32[64,8,128]{2,1,0:T(8,128)S(1)}, u32[]{:S(2)}, u32[]{:S(2)}) %all-to-all-start.2) | async-done | bytes 262176 | tf_op jit(solution)/shard_map/all_to_all | solution.py:335
  129.8 2.8 %shard_map.101 = (f32[256,128]{1,0:T(8,128)S(1)}, f32[8,128]{1,0:T(8,128)S(1)}, f32[64,8,128]{2,1,0:T(8,128)}) custom-call(f32[264,128]{1,0:T(8,128)S(1)} %select_maximum_fusion.carried_ref.rows_ref, f32[256,128]{1,0:T(8,128)S(1)} %get-tuple-element.40.rows_ref, f32[64,8,128]{2,1,0:T(8,128)S(1)} %all-to-all-done.2.table_ref.refs_0_, ...), custom_call_target="tpu_custom_call" | custom-call | tf_op jit(solution)/shard_map/pallas_call | solution.py:232
  132.6 5.0 %all-to-all-start.3 = ((f32[64,8,128]{2,1,0:T(8,128)}), f32[64,8,128]{2,1,0:T(8,128)S(1)}, u32[]{:S(2)}, u32[]{:S(2)}) async-start(f32[64,8,128]{2,1,0:T(8,128)} %get-tuple-element.47), calls=%async_computation.3 | async-start | bytes 524288 | tf_op jit(solution)/shard_map/all_to_all | solution.py:335
  137.6 2.0 shard_map.102
  139.6 7.6 %all-to-all-done.3.table_ref.refs_0_ = f32[64,8,128]{2,1,0:T(8,128)S(1)} async-done(((f32[64,8,128]{2,1,0:T(8,128)}), f32[64,8,128]{2,1,0:T(8,128)S(1)}, u32[]{:S(2)}, u32[]{:S(2)}) %all-to-all-start.3) | async-done | bytes 262176 | tf_op jit(solution)/shard_map/all_to_all | solution.py:335
  147.1 2.8 %shard_map.103 = (f32[256,128]{1,0:T(8,128)S(1)}, f32[8,128]{1,0:T(8,128)S(1)}, f32[64,8,128]{2,1,0:T(8,128)}) custom-call(f32[264,128]{1,0:T(8,128)S(1)} %select_maximum_fusion.carried_ref.rows_ref, f32[256,128]{1,0:T(8,128)S(1)} %get-tuple-element.46.rows_ref, f32[64,8,128]{2,1,0:T(8,128)S(1)} %all-to-all-done.3.table_ref.refs_0_, ...), custom_call_target="tpu_custom_call" | custom-call | tf_op jit(solution)/shard_map/pallas_call | solution.py:232
  149.9 5.0 %all-to-all-start.4 = ((f32[64,8,128]{2,1,0:T(8,128)}), f32[64,8,128]{2,1,0:T(8,128)S(1)}, u32[]{:S(2)}, u32[]{:S(2)}) async-start(f32[64,8,128]{2,1,0:T(8,128)} %get-tuple-element.53), calls=%async_computation.4 | async-start | bytes 524288 | tf_op jit(solution)/shard_map/all_to_all | solution.py:335
  155.0 0.0 copy-start
  155.0 1.3 shard_map.104
  156.2 8.2 %all-to-all-done.4.table_ref = f32[64,8,128]{2,1,0:T(8,128)S(1)} async-done(((f32[64,8,128]{2,1,0:T(8,128)}), f32[64,8,128]{2,1,0:T(8,128)S(1)}, u32[]{:S(2)}, u32[]{:S(2)}) %all-to-all-start.4) | async-done | bytes 262176 | tf_op jit(solution)/shard_map/all_to_all | solution.py:335
  164.5 2.0 shard_map.105
  166.5 1.9 collective-permute-start.2
  168.4 19.9 %collective-permute-done.2 = bf16[288,128]{1,0:T(8,128)(2,1)S(1)} collective-permute-done((bf16[288,128]{1,0:T(8,128)(2,1)S(1)}, bf16[288,128]{1,0:T(8,128)(2,1)S(1)}, u32[]{:S(2)}, u32[]{:S(2)}) %collective-permute-start.2) | collective-permute-done | bytes 73760 | tf_op jit(solution)/shard_map/ppermute | solution.py:351
  188.3 1.9 collective-permute-start.3
  190.2 7.2 %collective-permute-done.3 = bf16[256,128]{1,0:T(8,128)(2,1)S(1)} collective-permute-done((bf16[256,128]{1,0:T(8,128)(2,1)S(1)}, bf16[256,128]{1,0:T(8,128)(2,1)S(1)}, u32[]{:S(2)}, u32[]{:S(2)}) %collective-permute-start.3) | collective-permute-done | bytes 65568 | tf_op jit(solution)/shard_map/ppermute | solution.py:355
  197.4 1.9 collective-permute-start.4
  199.3 4.7 %collective-permute-done.4 = bf16[512,128]{1,0:T(8,128)(2,1)S(1)} collective-permute-done((bf16[512,128]{1,0:T(8,128)(2,1)S(1)}, bf16[512,128]{1,0:T(8,128)(2,1)S(1)}, u32[]{:S(2)}, u32[]{:S(2)}) %collective-permute-start.4) | collective-permute-done | bytes 131104 | tf_op jit(solution)/shard_map/ppermute | solution.py:355
  204.0 1.9 collective-permute-start.5
  205.9 0.1 pad_add_fusion.here_ref
  206.0 5.6 %collective-permute-start.6 = (bf16[1024,128]{1,0:T(8,128)(2,1)S(1)}, bf16[1024,128]{1,0:T(8,128)(2,1)S(1)}, u32[]{:S(2)}, u32[]{:S(2)}) collective-permute-start(bf16[1024,128]{1,0:T(8,128)(2,1)S(1)} %pad_maximum_fusion), channel_id=1, source_target_pairs={{0,64},{64,0},{1,65},{65,1},{2,66},{66,2},{3,67},{67,3},{4,68},{68... | collective-permute-start | bytes 786440 | tf_op jit(solution)/shard_map/ppermute | solution.py:357
  211.7 0.3 collective-permute-done.5
  211.9 4.6 %collective-permute-start.7 = (bf16[1024,128]{1,0:T(8,128)(2,1)S(1)}, bf16[1024,128]{1,0:T(8,128)(2,1)S(1)}, u32[]{:S(2)}, u32[]{:S(2)}) collective-permute-start(bf16[1024,128]{1,0:T(8,128)(2,1)S(1)} %collective-permute-done.5), channel_id=1, source_target_pairs={{0,64},{64,0},{1,65},{65,1},{2,66},{66,2},{3,67},{67,3},{4,68},{68... | collective-permute-start | bytes 786440 | tf_op jit(solution)/shard_map/ppermute | solution.py:357
  216.5 0.6 add.134
  217.1 0.0 collective-permute-done.6
  217.1 0.5 collective-permute-done.7
  217.6 0.0 copy-done
  217.7 4.2 %shard_map.106 = f32[4096,128]{1,0:T(8,128)} custom-call(s32[16,16]{1,0:T(8,128)S(1)} %bitcast.26, s32[2]{0:T(128)S(1)} %pad_add_fusion.here_ref, f32[4096,128]{1,0:T(8,128)} %table_ref.1, bf16[4,256,128]{2,1,0:T(8,128)(2,1)S(1)} %bitcast.22, bf16[4,256,128]{2,1,0:T(8,128)(2,1)S(1)} %bitcast.23, bf16[4,256,128]{2,1,0:T(8,128)(2,1)S(1)} %bitcast.24, ...), custom_call_target="tpu_custom_call" | custom-call | tf_op jit(solution)/shard_map/pallas_call | solution.py:277
  (16 shorter events, 0.2 us)
Async XLA Ops:
  0.6 51.1 %collective-permute-start = (bf16[4,256,128]{2,1,0:T(8,128)(2,1)}, bf16[4,256,128]{2,1,0:T(8,128)(2,1)S(1)}, u32[]{:S(2)}, u32[]{:S(2)}) collective-permute-start(bf16[4,256,128]{2,1,0:T(8,128)(2,1)} %bitcast.30), channel_id=1, source_target_pairs={{0,512},{4,576},{8,640},{12,704},{64,516},{68,580},{72,644},{76,70... | collective-permute-start | bytes 786440 | tf_op jit(solution)/shard_map/ppermute | solution.py:298
  30.3 21.3 %collective-permute-start.1 = (bf16[608,128]{1,0:T(8,128)(2,1)S(1)}, bf16[608,128]{1,0:T(8,128)(2,1)S(1)}, u32[]{:S(2)}, u32[]{:S(2)}) collective-permute-start(bf16[608,128]{1,0:T(8,128)(2,1)S(1)} %concatenate.18), channel_id=1, source_target_pairs={{0,512},{4,576},{8,640},{12,704},{64,516},{68,580},{72,644},{76,70... | collective-permute-start | bytes 466952 | tf_op jit(solution)/shard_map/ppermute | solution.py:309
  55.0 40.5 %all-to-all-start = ((bf16[64,4,16,128]{3,2,1,0:T(8,128)(2,1)}), bf16[64,4,16,128]{3,2,1,0:T(8,128)(2,1)S(1)}, u32[]{:S(2)}, u32[]{:S(2)}) async-start(bf16[64,4,16,128]{3,2,1,0:T(8,128)(2,1)} %get-tuple-element.34), calls=%async_computation | async-start | bytes 2097152 | tf_op jit(solution)/shard_map/all_to_all | solution.py:318
  97.3 15.1 %all-to-all-start.1 = ((f32[64,8,128]{2,1,0:T(8,128)}), f32[64,8,128]{2,1,0:T(8,128)S(1)}, u32[]{:S(2)}, u32[]{:S(2)}) async-start(f32[64,8,128]{2,1,0:T(8,128)} %get-tuple-element.35), calls=%async_computation.1 | async-start | bytes 524288 | tf_op jit(solution)/shard_map/all_to_all | solution.py:335
  115.2 14.6 %all-to-all-start.2 = ((f32[64,8,128]{2,1,0:T(8,128)}), f32[64,8,128]{2,1,0:T(8,128)S(1)}, u32[]{:S(2)}, u32[]{:S(2)}) async-start(f32[64,8,128]{2,1,0:T(8,128)} %get-tuple-element.41), calls=%async_computation.2 | async-start | bytes 524288 | tf_op jit(solution)/shard_map/all_to_all | solution.py:335
  132.6 14.6 %all-to-all-start.3 = ((f32[64,8,128]{2,1,0:T(8,128)}), f32[64,8,128]{2,1,0:T(8,128)S(1)}, u32[]{:S(2)}, u32[]{:S(2)}) async-start(f32[64,8,128]{2,1,0:T(8,128)} %get-tuple-element.47), calls=%async_computation.3 | async-start | bytes 524288 | tf_op jit(solution)/shard_map/all_to_all | solution.py:335
  149.9 14.6 %all-to-all-start.4 = ((f32[64,8,128]{2,1,0:T(8,128)}), f32[64,8,128]{2,1,0:T(8,128)S(1)}, u32[]{:S(2)}, u32[]{:S(2)}) async-start(f32[64,8,128]{2,1,0:T(8,128)} %get-tuple-element.53), calls=%async_computation.4 | async-start | bytes 524288 | tf_op jit(solution)/shard_map/all_to_all | solution.py:335
  155.0 62.7 %copy-start = (s32[16,1,16]{2,1,0:T(1,128)S(1)}, s32[16,1,16]{2,1,0:T(1,128)}, u32[]{:S(2)}) copy-start(s32[16,1,16]{2,1,0:T(1,128)} %param.9) | copy-start | bytes 3076
  166.5 21.8 %collective-permute-start.2 = (bf16[288,128]{1,0:T(8,128)(2,1)S(1)}, bf16[288,128]{1,0:T(8,128)(2,1)S(1)}, u32[]{:S(2)}, u32[]{:S(2)}) collective-permute-start(bf16[288,128]{1,0:T(8,128)(2,1)S(1)} %shard_map.105), channel_id=1, source_target_pairs={{0,512},{4,576},{8,640},{12,704},{64,516},{68,580},{72,644},{76,70... | collective-permute-start | bytes 221192 | tf_op jit(solution)/shard_map/ppermute | solution.py:351
  188.3 9.1 %collective-permute-start.3 = (bf16[256,128]{1,0:T(8,128)(2,1)S(1)}, bf16[256,128]{1,0:T(8,128)(2,1)S(1)}, u32[]{:S(2)}, u32[]{:S(2)}) collective-permute-start(bf16[256,128]{1,0:T(8,128)(2,1)S(1)} %slice.25), channel_id=1, source_target_pairs={{0,512},{512,0},{1,513},{513,1},{2,514},{514,2},{3,515},{515,3},{4... | collective-permute-start | bytes 196616 | tf_op jit(solution)/shard_map/ppermute | solution.py:355
  197.4 6.6 %collective-permute-start.4 = (bf16[512,128]{1,0:T(8,128)(2,1)S(1)}, bf16[512,128]{1,0:T(8,128)(2,1)S(1)}, u32[]{:S(2)}, u32[]{:S(2)}) collective-permute-start(bf16[512,128]{1,0:T(8,128)(2,1)S(1)} %pad_maximum_fusion.1), channel_id=1, source_target_pairs={{0,256},{256,0},{1,257},{257,1},{2,258},{258,2},{3,259},{259,3},{4... | collective-permute-start | bytes 393224 | tf_op jit(solution)/shard_map/ppermute | solution.py:355
  204.0 7.9 %collective-permute-start.5 = (bf16[1024,128]{1,0:T(8,128)(2,1)S(1)}, bf16[1024,128]{1,0:T(8,128)(2,1)S(1)}, u32[]{:S(2)}, u32[]{:S(2)}) collective-permute-start(bf16[1024,128]{1,0:T(8,128)(2,1)S(1)} %pad_maximum_fusion), channel_id=1, source_target_pairs={{0,128},{128,0},{1,129},{129,1},{2,130},{130,2},{3,131},{131,3},{4... | collective-permute-start | bytes 786440 | tf_op jit(solution)/shard_map/ppermute | solution.py:356
  206.0 11.1 %collective-permute-start.6 = (bf16[1024,128]{1,0:T(8,128)(2,1)S(1)}, bf16[1024,128]{1,0:T(8,128)(2,1)S(1)}, u32[]{:S(2)}, u32[]{:S(2)}) collective-permute-start(bf16[1024,128]{1,0:T(8,128)(2,1)S(1)} %pad_maximum_fusion), channel_id=1, source_target_pairs={{0,64},{64,0},{1,65},{65,1},{2,66},{66,2},{3,67},{67,3},{4,68},{68... | collective-permute-start | bytes 786440 | tf_op jit(solution)/shard_map/ppermute | solution.py:357
  211.9 5.7 %collective-permute-start.7 = (bf16[1024,128]{1,0:T(8,128)(2,1)S(1)}, bf16[1024,128]{1,0:T(8,128)(2,1)S(1)}, u32[]{:S(2)}, u32[]{:S(2)}) collective-permute-start(bf16[1024,128]{1,0:T(8,128)(2,1)S(1)} %collective-permute-done.5), channel_id=1, source_target_pairs={{0,64},{64,0},{1,65},{65,1},{2,66},{66,2},{3,67},{67,3},{4,68},{68... | collective-permute-start | bytes 786440 | tf_op jit(solution)/shard_map/ppermute | solution.py:357

commit v7 on v6

--- a/solution.py
+++ b/solution.py
@@ -239,15 +239,17 @@
     )(*args)
 
 
-def merge_kernel(blocks_ref, here_ref, table_ref, near_ref, far_ref, other_near_ref, other_far_ref, out_ref, sem):
+def merge_kernel(blocks_ref, here_ref, table_ref, near_ref, far_ref, other_near_ref, other_far_ref, out_ref,
+    sum_ref, new_ref, sem, out_sems,
+):
     places, act_rows, _ = near_ref.shape
     places = 2 * places
     active = act_rows // BLK
     groups = 2 * places
     low = here_ref[0] == 0
-    copy = pltpu.make_async_copy(table_ref, out_ref, sem)
+    copy = pltpu.make_async_copy(table_ref, new_ref, sem)
     copy.start()
-    copy.wait()
+    sum_ref[...] = jnp.zeros_like(sum_ref)
 
     def one(place, carry):
         apart = place ^ here_ref[1]
@@ -263,12 +265,23 @@
                 value = jnp.where(own, mine, other).astype(jnp.float32)
                 spot = pl.ds(pl.multiple_of(blocks_ref[2 * place + c, slot] * BLK, BLK), BLK)
                 spots.append(spot)
-                values.append(out_ref[spot, :] + value * (1.0 / groups))
+                values.append(sum_ref[spot, :] + value)
             for spot, value in zip(spots, values):
-                out_ref[spot, :] = value
+                sum_ref[spot, :] = value
         return carry
 
     lax.fori_loop(0, places, one, 0)
+    copy.wait()
+    chunks = out_sems.shape[0]
+    size = out_ref.shape[0] // chunks
+    outs = []
+    for n in range(chunks):
+        part = pl.ds(n * size, size)
+        new_ref[part, :] = new_ref[part, :] + sum_ref[part, :] * (1.0 / groups)
+        outs.append(pltpu.make_async_copy(new_ref.at[part], out_ref.at[part], out_sems.at[n]))
+        outs[-1].start()
+    for out in outs:
+        out.wait()
 
 
 def merge(blocks, here, table, held):
@@ -278,9 +291,14 @@
         merge_kernel,
         grid=(1,),
         in_specs=[smem, smem, hbm] + [whole] * 4,
-        out_specs=pl.BlockSpec(table.shape, lambda i: (0, 0)),
+        out_specs=hbm,
         out_shape=jax.ShapeDtypeStruct(table.shape, jnp.float32),
-        scratch_shapes=[pltpu.SemaphoreType.DMA],
+        scratch_shapes=[
+            pltpu.VMEM(table.shape, jnp.float32),
+            pltpu.VMEM(table.shape, jnp.float32),
+            pltpu.SemaphoreType.DMA,
+            pltpu.SemaphoreType.DMA((8,)),
+        ],
         compiler_params=pltpu.CompilerParams(vmem_limit_bytes=MERGE_LIMIT),
     )(blocks, here, table, *held)
 

time: 223 us -> 222 us (level)
  no operation moved by 1% of the time
where the time goes in v7:
time: 222 us
  waiting for transfers between devices  100 us (45%)
  starting transfers between devices  87.4 us (39%)
  Pallas kernels  26 us (12%)
  other arithmetic  3.82 us (2%)
  local copies, waits for them, and re-layouts  3.12 us (1%)
    all_to_all x4, waiting for transfers between devices, body(): table = lax.all_to_all(sent, GROUP, 0, 0, tiled=True)  31.3 us
    all_to_all x1, starting transfers between devices, body(): got = lax.all_to_all(packed, GROUP, 0, 0, tiled=True)  23.5 us
    ppermute x1, starting transfers between devices, body(): feats = there(dense_feat[0])  23.5 us
    pallas_call x11, Pallas kernels, call(): pl.pallas_call(kernel, in_specs=[smem if arg.size == 1 else vmem for arg...  22.3 us
    all_to_all x4, starting transfers between devices, body(): table = lax.all_to_all(sent, GROUP, 0, 0, tiled=True)  20.7 us
    ppermute x1, waiting for transfers between devices, body(): back = there(back)  19.9 us
    ppermute x1, waiting for transfers between devices, body(): rest = there(jnp.concatenate(parts, axis=0))  19.4 us
    all_to_all x1, waiting for transfers between devices, body(): got = lax.all_to_all(packed, GROUP, 0, 0, tiled=True)  16.9 us
  transfers between devices with their start and end apart: 13, of which 11 were waited for; matrix products, arithmetic and copies ran while one was open for 3% of the time, Pallas kernels for 3%

profile of v7, /device:TPU:1, one launch (start us, length us, event | category | flops | bytes accessed | tf_op | source)
XLA Modules:
  0.0 221.5 jit_solution(13415458172496511080)
XLA Ops:
  0.6 23.5 %collective-permute-start = (bf16[4,256,128]{2,1,0:T(8,128)(2,1)}, bf16[4,256,128]{2,1,0:T(8,128)(2,1)S(1)}, u32[]{:S(2)}, u32[]{:S(2)}) collective-permute-start(bf16[4,256,128]{2,1,0:T(8,128)(2,1)} %bitcast.30), channel_id=1, source_target_pairs={{0,512},{4,576},{8,640},{12,704},{64,516},{68,580},{72,644},{76,70... | collective-permute-start | bytes 786440 | tf_op jit(solution)/shard_map/ppermute | solution.py:316
  24.1 0.7 convert.16
  24.8 0.8 fusion.1
  25.6 0.7 convert_bitcast_fusion
  26.4 0.7 multiply_bitcast_fusion
  27.0 0.1 iota_add_fusion
  27.1 0.1 add.127
  27.2 2.3 %gather_fusion = f32[256,128]{1,0:T(8,128)S(1)} fusion(f32[4096,128]{1,0:T(8,128)} %table_ref.1, s32[1024]{0:T(1024)S(1)} %pad_clamp_fusion), kind=kCustom, calls=%fused_computation | custom fusion | bytes 263168 | tf_op jit(solution)/shard_map/gather | solution.py:324
  29.6 0.7 fusion.2
  30.3 0.1 concatenate.18
  30.3 1.9 collective-permute-start.1
  32.3 19.4 %collective-permute-done.1 = bf16[608,128]{1,0:T(8,128)(2,1)S(1)} collective-permute-done((bf16[608,128]{1,0:T(8,128)(2,1)S(1)}, bf16[608,128]{1,0:T(8,128)(2,1)S(1)}, u32[]{:S(2)}, u32[]{:S(2)}) %collective-permute-start.1) | collective-permute-done | bytes 155680 | tf_op jit(solution)/shard_map/ppermute | solution.py:327
  51.7 0.0 collective-permute-done.feat_ref
  51.7 3.3 %shard_map.95 = (bf16[64,4,16,128]{3,2,1,0:T(8,128)(2,1)}, s32[4,1,512]{2,1,0:T(1,128)S(1)}) custom-call(bf16[88,128]{1,0:T(8,128)(2,1)S(1)} %split.15.meta_ref, bf16[4,256,128]{2,1,0:T(8,128)(2,1)S(1)} %collective-permute-done.feat_ref), custom_call_target="tpu_custom_call" | custom-call | tf_op jit(solution)/shard_map/pallas_call | solution.py:232
  55.0 23.5 %all-to-all-start = ((bf16[64,4,16,128]{3,2,1,0:T(8,128)(2,1)}), bf16[64,4,16,128]{3,2,1,0:T(8,128)(2,1)S(1)}, u32[]{:S(2)}, u32[]{:S(2)}) async-start(bf16[64,4,16,128]{3,2,1,0:T(8,128)(2,1)} %get-tuple-element.34), calls=%async_computation | async-start | bytes 2097152 | tf_op jit(solution)/shard_map/all_to_all | solution.py:336
  78.5 0.1 shard_map.96.weighted_ref
  78.6 16.9 %all-to-all-done.got_ref = bf16[64,4,16,128]{3,2,1,0:T(8,128)(2,1)S(1)} async-done(((bf16[64,4,16,128]{3,2,1,0:T(8,128)(2,1)}), bf16[64,4,16,128]{3,2,1,0:T(8,128)(2,1)S(1)}, u32[]{:S(2)}, u32[]{:S(2)}) %all-to-all-start) | async-done | bytes 1048608 | tf_op jit(solution)/shard_map/all_to_all | solution.py:336
  95.5 1.8 shard_map.97
  97.3 5.6 %all-to-all-start.1 = ((f32[64,8,128]{2,1,0:T(8,128)}), f32[64,8,128]{2,1,0:T(8,128)S(1)}, u32[]{:S(2)}, u32[]{:S(2)}) async-start(f32[64,8,128]{2,1,0:T(8,128)} %get-tuple-element.35), calls=%async_computation.1 | async-start | bytes 524288 | tf_op jit(solution)/shard_map/all_to_all | solution.py:353
  102.9 1.6 shard_map.98
  104.5 7.9 %all-to-all-done.1.table_ref.refs_0_ = f32[64,8,128]{2,1,0:T(8,128)S(1)} async-done(((f32[64,8,128]{2,1,0:T(8,128)}), f32[64,8,128]{2,1,0:T(8,128)S(1)}, u32[]{:S(2)}, u32[]{:S(2)}) %all-to-all-start.1) | async-done | bytes 262176 | tf_op jit(solution)/shard_map/all_to_all | solution.py:353
  112.4 2.8 %shard_map.99 = (f32[256,128]{1,0:T(8,128)S(1)}, f32[8,128]{1,0:T(8,128)S(1)}, f32[64,8,128]{2,1,0:T(8,128)}) custom-call(f32[264,128]{1,0:T(8,128)S(1)} %select_maximum_fusion.carried_ref.rows_ref, f32[264,128]{1,0:T(8,128)S(1)} %select_maximum_fusion.carried_ref.rows_ref, f32[64,8,128]{2,1,0:T(8,128)S(1)} %all-to-all-done.1.table_ref.refs_0_, ...), custom_call_target="tpu_custom_call" | custom-call | tf_op jit(solution)/shard_map/pallas_call | solution.py:232
  115.2 5.0 %all-to-all-start.2 = ((f32[64,8,128]{2,1,0:T(8,128)}), f32[64,8,128]{2,1,0:T(8,128)S(1)}, u32[]{:S(2)}, u32[]{:S(2)}) async-start(f32[64,8,128]{2,1,0:T(8,128)} %get-tuple-element.41), calls=%async_computation.2 | async-start | bytes 524288 | tf_op jit(solution)/shard_map/all_to_all | solution.py:353
  120.3 2.0 shard_map.100
  122.2 7.6 %all-to-all-done.2.table_ref.refs_0_ = f32[64,8,128]{2,1,0:T(8,128)S(1)} async-done(((f32[64,8,128]{2,1,0:T(8,128)}), f32[64,8,128]{2,1,0:T(8,128)S(1)}, u32[]{:S(2)}, u32[]{:S(2)}) %all-to-all-start.2) | async-done | bytes 262176 | tf_op jit(solution)/shard_map/all_to_all | solution.py:353
  129.8 2.8 %shard_map.101 = (f32[256,128]{1,0:T(8,128)S(1)}, f32[8,128]{1,0:T(8,128)S(1)}, f32[64,8,128]{2,1,0:T(8,128)}) custom-call(f32[264,128]{1,0:T(8,128)S(1)} %select_maximum_fusion.carried_ref.rows_ref, f32[256,128]{1,0:T(8,128)S(1)} %get-tuple-element.40.rows_ref, f32[64,8,128]{2,1,0:T(8,128)S(1)} %all-to-all-done.2.table_ref.refs_0_, ...), custom_call_target="tpu_custom_call" | custom-call | tf_op jit(solution)/shard_map/pallas_call | solution.py:232
  132.6 5.0 %all-to-all-start.3 = ((f32[64,8,128]{2,1,0:T(8,128)}), f32[64,8,128]{2,1,0:T(8,128)S(1)}, u32[]{:S(2)}, u32[]{:S(2)}) async-start(f32[64,8,128]{2,1,0:T(8,128)} %get-tuple-element.47), calls=%async_computation.3 | async-start | bytes 524288 | tf_op jit(solution)/shard_map/all_to_all | solution.py:353
  137.6 2.0 shard_map.102
  139.6 7.6 %all-to-all-done.3.table_ref.refs_0_ = f32[64,8,128]{2,1,0:T(8,128)S(1)} async-done(((f32[64,8,128]{2,1,0:T(8,128)}), f32[64,8,128]{2,1,0:T(8,128)S(1)}, u32[]{:S(2)}, u32[]{:S(2)}) %all-to-all-start.3) | async-done | bytes 262176 | tf_op jit(solution)/shard_map/all_to_all | solution.py:353
  147.1 2.8 %shard_map.103 = (f32[256,128]{1,0:T(8,128)S(1)}, f32[8,128]{1,0:T(8,128)S(1)}, f32[64,8,128]{2,1,0:T(8,128)}) custom-call(f32[264,128]{1,0:T(8,128)S(1)} %select_maximum_fusion.carried_ref.rows_ref, f32[256,128]{1,0:T(8,128)S(1)} %get-tuple-element.46.rows_ref, f32[64,8,128]{2,1,0:T(8,128)S(1)} %all-to-all-done.3.table_ref.refs_0_, ...), custom_call_target="tpu_custom_call" | custom-call | tf_op jit(solution)/shard_map/pallas_call | solution.py:232
  149.9 5.0 %all-to-all-start.4 = ((f32[64,8,128]{2,1,0:T(8,128)}), f32[64,8,128]{2,1,0:T(8,128)S(1)}, u32[]{:S(2)}, u32[]{:S(2)}) async-start(f32[64,8,128]{2,1,0:T(8,128)} %get-tuple-element.53), calls=%async_computation.4 | async-start | bytes 524288 | tf_op jit(solution)/shard_map/all_to_all | solution.py:353
  155.0 0.0 copy-start
  155.0 1.3 shard_map.104
  156.2 8.2 %all-to-all-done.4.table_ref = f32[64,8,128]{2,1,0:T(8,128)S(1)} async-done(((f32[64,8,128]{2,1,0:T(8,128)}), f32[64,8,128]{2,1,0:T(8,128)S(1)}, u32[]{:S(2)}, u32[]{:S(2)}) %all-to-all-start.4) | async-done | bytes 262176 | tf_op jit(solution)/shard_map/all_to_all | solution.py:353
  164.5 2.0 shard_map.105
  166.5 1.9 collective-permute-start.2
  168.4 19.9 %collective-permute-done.2 = bf16[288,128]{1,0:T(8,128)(2,1)S(1)} collective-permute-done((bf16[288,128]{1,0:T(8,128)(2,1)S(1)}, bf16[288,128]{1,0:T(8,128)(2,1)S(1)}, u32[]{:S(2)}, u32[]{:S(2)}) %collective-permute-start.2) | collective-permute-done | bytes 73760 | tf_op jit(solution)/shard_map/ppermute | solution.py:369
  188.3 1.9 collective-permute-start.3
  190.2 7.2 %collective-permute-done.3 = bf16[256,128]{1,0:T(8,128)(2,1)S(1)} collective-permute-done((bf16[256,128]{1,0:T(8,128)(2,1)S(1)}, bf16[256,128]{1,0:T(8,128)(2,1)S(1)}, u32[]{:S(2)}, u32[]{:S(2)}) %collective-permute-start.3) | collective-permute-done | bytes 65568 | tf_op jit(solution)/shard_map/ppermute | solution.py:373
  197.4 1.9 collective-permute-start.4
  199.3 4.7 %collective-permute-done.4 = bf16[512,128]{1,0:T(8,128)(2,1)S(1)} collective-permute-done((bf16[512,128]{1,0:T(8,128)(2,1)S(1)}, bf16[512,128]{1,0:T(8,128)(2,1)S(1)}, u32[]{:S(2)}, u32[]{:S(2)}) %collective-permute-start.4) | collective-permute-done | bytes 131104 | tf_op jit(solution)/shard_map/ppermute | solution.py:373
  204.0 1.9 collective-permute-start.5
  205.9 0.1 pad_add_fusion.here_ref
  206.0 5.6 %collective-permute-start.6 = (bf16[1024,128]{1,0:T(8,128)(2,1)S(1)}, bf16[1024,128]{1,0:T(8,128)(2,1)S(1)}, u32[]{:S(2)}, u32[]{:S(2)}) collective-permute-start(bf16[1024,128]{1,0:T(8,128)(2,1)S(1)} %pad_maximum_fusion), channel_id=1, source_target_pairs={{0,64},{64,0},{1,65},{65,1},{2,66},{66,2},{3,67},{67,3},{4,68},{68... | collective-permute-start | bytes 786440 | tf_op jit(solution)/shard_map/ppermute | solution.py:375
  211.7 0.3 collective-permute-done.5
  211.9 4.6 %collective-permute-start.7 = (bf16[1024,128]{1,0:T(8,128)(2,1)S(1)}, bf16[1024,128]{1,0:T(8,128)(2,1)S(1)}, u32[]{:S(2)}, u32[]{:S(2)}) collective-permute-start(bf16[1024,128]{1,0:T(8,128)(2,1)S(1)} %collective-permute-done.5), channel_id=1, source_target_pairs={{0,64},{64,0},{1,65},{65,1},{2,66},{66,2},{3,67},{67,3},{4,68},{68... | collective-permute-start | bytes 786440 | tf_op jit(solution)/shard_map/ppermute | solution.py:375
  216.5 0.6 add.134
  217.1 0.0 collective-permute-done.6
  217.1 0.5 collective-permute-done.7
  217.6 0.0 copy-done
  217.7 3.7 %shard_map.106 = f32[4096,128]{1,0:T(8,128)} custom-call(s32[16,16]{1,0:T(8,128)S(1)} %bitcast.26, s32[2]{0:T(128)S(1)} %pad_add_fusion.here_ref, f32[4096,128]{1,0:T(8,128)} %table_ref.1, bf16[4,256,128]{2,1,0:T(8,128)(2,1)S(1)} %bitcast.22, bf16[4,256,128]{2,1,0:T(8,128)(2,1)S(1)} %bitcast.23, bf16[4,256,128]{2,1,0:T(8,128)(2,1)S(1)} %bitcast.24, ...), custom_call_target="tpu_custom_call" | custom-call | tf_op jit(solution)/shard_map/pallas_call | solution.py:290
  (16 shorter events, 0.2 us)
Async XLA Ops:
  0.6 51.1 %collective-permute-start = (bf16[4,256,128]{2,1,0:T(8,128)(2,1)}, bf16[4,256,128]{2,1,0:T(8,128)(2,1)S(1)}, u32[]{:S(2)}, u32[]{:S(2)}) collective-permute-start(bf16[4,256,128]{2,1,0:T(8,128)(2,1)} %bitcast.30), channel_id=1, source_target_pairs={{0,512},{4,576},{8,640},{12,704},{64,516},{68,580},{72,644},{76,70... | collective-permute-start | bytes 786440 | tf_op jit(solution)/shard_map/ppermute | solution.py:316
  30.3 21.3 %collective-permute-start.1 = (bf16[608,128]{1,0:T(8,128)(2,1)S(1)}, bf16[608,128]{1,0:T(8,128)(2,1)S(1)}, u32[]{:S(2)}, u32[]{:S(2)}) collective-permute-start(bf16[608,128]{1,0:T(8,128)(2,1)S(1)} %concatenate.18), channel_id=1, source_target_pairs={{0,512},{4,576},{8,640},{12,704},{64,516},{68,580},{72,644},{76,70... | collective-permute-start | bytes 466952 | tf_op jit(solution)/shard_map/ppermute | solution.py:327
  55.0 40.5 %all-to-all-start = ((bf16[64,4,16,128]{3,2,1,0:T(8,128)(2,1)}), bf16[64,4,16,128]{3,2,1,0:T(8,128)(2,1)S(1)}, u32[]{:S(2)}, u32[]{:S(2)}) async-start(bf16[64,4,16,128]{3,2,1,0:T(8,128)(2,1)} %get-tuple-element.34), calls=%async_computation | async-start | bytes 2097152 | tf_op jit(solution)/shard_map/all_to_all | solution.py:336
  97.3 15.1 %all-to-all-start.1 = ((f32[64,8,128]{2,1,0:T(8,128)}), f32[64,8,128]{2,1,0:T(8,128)S(1)}, u32[]{:S(2)}, u32[]{:S(2)}) async-start(f32[64,8,128]{2,1,0:T(8,128)} %get-tuple-element.35), calls=%async_computation.1 | async-start | bytes 524288 | tf_op jit(solution)/shard_map/all_to_all | solution.py:353
  115.2 14.6 %all-to-all-start.2 = ((f32[64,8,128]{2,1,0:T(8,128)}), f32[64,8,128]{2,1,0:T(8,128)S(1)}, u32[]{:S(2)}, u32[]{:S(2)}) async-start(f32[64,8,128]{2,1,0:T(8,128)} %get-tuple-element.41), calls=%async_computation.2 | async-start | bytes 524288 | tf_op jit(solution)/shard_map/all_to_all | solution.py:353
  132.6 14.6 %all-to-all-start.3 = ((f32[64,8,128]{2,1,0:T(8,128)}), f32[64,8,128]{2,1,0:T(8,128)S(1)}, u32[]{:S(2)}, u32[]{:S(2)}) async-start(f32[64,8,128]{2,1,0:T(8,128)} %get-tuple-element.47), calls=%async_computation.3 | async-start | bytes 524288 | tf_op jit(solution)/shard_map/all_to_all | solution.py:353
  149.9 14.6 %all-to-all-start.4 = ((f32[64,8,128]{2,1,0:T(8,128)}), f32[64,8,128]{2,1,0:T(8,128)S(1)}, u32[]{:S(2)}, u32[]{:S(2)}) async-start(f32[64,8,128]{2,1,0:T(8,128)} %get-tuple-element.53), calls=%async_computation.4 | async-start | bytes 524288 | tf_op jit(solution)/shard_map/all_to_all | solution.py:353
  155.0 62.7 %copy-start = (s32[16,1,16]{2,1,0:T(1,128)S(1)}, s32[16,1,16]{2,1,0:T(1,128)}, u32[]{:S(2)}) copy-start(s32[16,1,16]{2,1,0:T(1,128)} %param.9) | copy-start | bytes 3076
  166.5 21.8 %collective-permute-start.2 = (bf16[288,128]{1,0:T(8,128)(2,1)S(1)}, bf16[288,128]{1,0:T(8,128)(2,1)S(1)}, u32[]{:S(2)}, u32[]{:S(2)}) collective-permute-start(bf16[288,128]{1,0:T(8,128)(2,1)S(1)} %shard_map.105), channel_id=1, source_target_pairs={{0,512},{4,576},{8,640},{12,704},{64,516},{68,580},{72,644},{76,70... | collective-permute-start | bytes 221192 | tf_op jit(solution)/shard_map/ppermute | solution.py:369
  188.3 9.1 %collective-permute-start.3 = (bf16[256,128]{1,0:T(8,128)(2,1)S(1)}, bf16[256,128]{1,0:T(8,128)(2,1)S(1)}, u32[]{:S(2)}, u32[]{:S(2)}) collective-permute-start(bf16[256,128]{1,0:T(8,128)(2,1)S(1)} %slice.25), channel_id=1, source_target_pairs={{0,512},{512,0},{1,513},{513,1},{2,514},{514,2},{3,515},{515,3},{4... | collective-permute-start | bytes 196616 | tf_op jit(solution)/shard_map/ppermute | solution.py:373
  197.4 6.6 %collective-permute-start.4 = (bf16[512,128]{1,0:T(8,128)(2,1)S(1)}, bf16[512,128]{1,0:T(8,128)(2,1)S(1)}, u32[]{:S(2)}, u32[]{:S(2)}) collective-permute-start(bf16[512,128]{1,0:T(8,128)(2,1)S(1)} %pad_maximum_fusion.1), channel_id=1, source_target_pairs={{0,256},{256,0},{1,257},{257,1},{2,258},{258,2},{3,259},{259,3},{4... | collective-permute-start | bytes 393224 | tf_op jit(solution)/shard_map/ppermute | solution.py:373
  204.0 7.9 %collective-permute-start.5 = (bf16[1024,128]{1,0:T(8,128)(2,1)S(1)}, bf16[1024,128]{1,0:T(8,128)(2,1)S(1)}, u32[]{:S(2)}, u32[]{:S(2)}) collective-permute-start(bf16[1024,128]{1,0:T(8,128)(2,1)S(1)} %pad_maximum_fusion), channel_id=1, source_target_pairs={{0,128},{128,0},{1,129},{129,1},{2,130},{130,2},{3,131},{131,3},{4... | collective-permute-start | bytes 786440 | tf_op jit(solution)/shard_map/ppermute | solution.py:374
  206.0 11.1 %collective-permute-start.6 = (bf16[1024,128]{1,0:T(8,128)(2,1)S(1)}, bf16[1024,128]{1,0:T(8,128)(2,1)S(1)}, u32[]{:S(2)}, u32[]{:S(2)}) collective-permute-start(bf16[1024,128]{1,0:T(8,128)(2,1)S(1)} %pad_maximum_fusion), channel_id=1, source_target_pairs={{0,64},{64,0},{1,65},{65,1},{2,66},{66,2},{3,67},{67,3},{4,68},{68... | collective-permute-start | bytes 786440 | tf_op jit(solution)/shard_map/ppermute | solution.py:375
  211.9 5.7 %collective-permute-start.7 = (bf16[1024,128]{1,0:T(8,128)(2,1)S(1)}, bf16[1024,128]{1,0:T(8,128)(2,1)S(1)}, u32[]{:S(2)}, u32[]{:S(2)}) collective-permute-start(bf16[1024,128]{1,0:T(8,128)(2,1)S(1)} %collective-permute-done.5), channel_id=1, source_target_pairs={{0,64},{64,0},{1,65},{65,1},{2,66},{66,2},{3,67},{67,3},{4,68},{68... | collective-permute-start | bytes 786440 | tf_op jit(solution)/shard_map/ppermute | solution.py:375
